TPU v7x, 256 devices: a whole 4x4x8 slice. The times are simulated.
256 devices in a mesh: grp: 2 (over core), seq: 128 (over z, x, y).
Axes of the slice: x: 4, y: 4, z: 8, core: 2. Of those that a mesh axis runs over, the one named last changes fastest.
Arguments:
- latent_large: bfloat16 [4096, 5120], P('seq'), may hold values from -6 to 6
- latent_small: bfloat16 [4096, 1536], P('seq'), may hold values from -6 to 6
- gain_large: float32 [5120], replicated, may hold values from 0.1 to 1.9
- gain_small: float32 [1536], replicated, may hold values from 0.1 to 1.9
- qkv_large: bfloat16 [5120, 12288], P(None, ('grp', 'seq')), may hold values from -0.08385255 to 0.08385255
- qkv_small: bfloat16 [1536, 3072], P(None, ('grp', 'seq')), may hold values from -0.15309311 to 0.15309311
- mix_large: bfloat16 [4096, 64], P('grp'), may hold values from -0.09375 to 0.09375
- mix_small: bfloat16 [1024, 64], P('grp'), may hold values from -0.1875 to 0.1875
- head_large: bfloat16 [5120, 64], replicated, may hold values from -0.078125 to 0.078125
- head_small: bfloat16 [1536, 64], replicated, may hold values from -0.15625 to 0.15625
Outputs:
- guided: float32 [4096, 64], P('seq')
All inputs are finite; a program needn't handle non-finite values.
Results may differ from a plain program's by a relative error of at most 0.00095.
The roundings to bfloat16 on the way count: a program that leaves them out, or rounds other values in their place, can miss the bound.
Values may be sent and summed in bfloat16 or wider, within the bound.
No kernel may reach another device: no remote copies, remote signals or barrier semaphores. Data moves between devices by JAX's collectives and lax.ppermute only.
A program may use at most 64 MiB of HBM per device.

v0:
```python
import jax
import jax.numpy as jnp
from jax import lax
from jax.experimental import pallas as pl
from jax.experimental.pallas import tpu as pltpu
from jax.sharding import Mesh, PartitionSpec as P

HD = 128
GUIDANCE = 3.0
EPSILON = 1e-06
BF = jnp.bfloat16
F32 = jnp.float32
DL, DS = 5120, 1536
KS = DS // 2
PART = 512
LOG2E = 1.4426950408889634
VMEM = pl.BlockSpec(memory_space=pltpu.VMEM)
SMEM = pl.BlockSpec(memory_space=pltpu.SMEM)
ANY = pl.BlockSpec(memory_space=pl.ANY)
OPPOSITE = [(0, 3), (3, 0), (1, 2), (2, 1)]


def flip(block, axis, mask):
    count = lax.axis_size(axis)
    return lax.ppermute(block, axis, [(i, i ^ mask) for i in range(count)])


def swap(block):
    return flip(block, "grp", 1)


def cross(block):
    return lax.ppermute(block, "x", OPPOSITE)


def spread(block, axis):
    n = lax.axis_size(axis)
    pairs = [(i, (i + 1) % n) for i in range(n)]
    pairs += [(n + i, n + (i - 1) % n) for i in range(n)]
    return lax.ppermute(block, ("grp", axis), pairs)


def tie(*values):
    return lax.optimization_barrier(values)


def dot_t(rows, columns):
    return lax.dot_general(
        rows, columns, (((1,), (1,)), ((), ())), preferred_element_type=F32
    )


def call(body, outs, args, scratch=(), limit=16, placed=None, flops=0):
    return pl.pallas_call(
        body,
        out_shape=[jax.ShapeDtypeStruct(shape, dtype) for shape, dtype in outs],
        in_specs=placed or [SMEM] + [VMEM] * (len(args) - 1),
        out_specs=[VMEM] * len(outs),
        scratch_shapes=list(scratch),
        compiler_params=pltpu.CompilerParams(vmem_limit_bytes=limit * 2**20),
        cost_estimate=pl.CostEstimate(flops=flops, bytes_accessed=2**20, transcendentals=0),
    )(*args)


def norm_body(where, large, small, gain_l, gain_s, mine, other, out_s, hold_l, hold_s, g_l, g_s, sems):
    core = where[0]
    tasks = [
        pltpu.make_async_copy(source, target, sems.at[i])
        for i, (source, target) in enumerate(
            ((large, hold_l), (small, hold_s), (gain_l, g_l), (gain_s, g_s))
        )
    ]
    for task in tasks:
        task.start()
    for task in tasks:
        task.wait()

    def normed(latent, gain, half, width):
        values = latent[pl.ds(pl.multiple_of(half * 16, 16), 16), :].astype(F32)
        mean = jnp.mean(values * values, axis=-1, keepdims=True)
        return (values * lax.rsqrt(mean + EPSILON) * gain[...].reshape(1, width)).astype(BF)

    mine[...] = normed(hold_l, g_l, core, DL)
    other[...] = normed(hold_l, g_l, 1 - core, DL)
    for at, half in ((0, core), (32, 1 - core)):
        value = normed(hold_s, g_s, half, DS)
        out_s[at : at + 16, :] = value[:, :KS]
        out_s[at + 16 : at + 32, :] = value[:, KS:]


def block_body(where, mine, other, across, got, small, out):
    out[0:16, :DL] = mine[...]
    out[16:32, :DL] = across[...]
    out[32:48, :DL] = other[...]
    out[48:64, :DL] = got[...]
    out[:, DL:] = small[...]


def project_body(
    where, near, z1, z2, z3, zf, s_got, w0, y1, y1_g, fo, fo_g, pr, y2, y2_g, fp, fp_g,
    order_l, order_s, kept_q, kept_kv, sent, kept_s, sent_s, rows_s,
):
    core, z, x = where[0], where[1], where[2]
    way = 2 * core - 1

    def at_z(step):
        return pl.ds(pl.multiple_of((z + 8 + step) % 8 * 16, 16), 16)

    def put(step, ref, row, col):
        rows_s[at_z(step), :KS] = ref[row : row + 16, col:]
        rows_s[at_z(step), KS:] = ref[row + 16 : row + 32, col:]

    put(0, near, 0, DL)
    put(4, zf, 0, DL)
    for i, ref in ((1, z1), (2, z2), (3, z3)):
        put(way * i, ref, 0, DL)
        put(-way * i, s_got, 32 * i - 32, 0)

    plain = ((w0, 0), (y1, 0), (fo, 0), (y1_g, 48), (w0, 48), (y1, 48), (fo_g, 0), (y1_g, 0))
    paired = ((pr, 0), (y2, 0), (fp, 0), (y2_g, 48), (pr, 48), (y2, 48), (fp_g, 0), (y2_g, 0))
    blocks = plain[:4] + paired[:4] + plain[4:] + paired[4:]
    total = None
    for k in range(0, DL, 512):
        at = slice(k, k + 512)
        cols = jnp.concatenate([ref[row : row + 48, at] for ref, row in blocks], 0)
        rows = jnp.concatenate([near[:32, at], z1[:, at], z2[:, at], z3[:, at], zf[:, at]], 0)
        term = dot_t(cols, rows)
        total = term if total is None else total + term
    total = total.astype(BF)

    def ordered(value, order):
        return lax.dot_general(
            value, order[...], (((0,), (0,)), ((), ())), preferred_element_type=F32
        ).astype(BF)

    own, other = total[:384, :], total[384:, :]
    mine = core == x % 2
    sent[...] = ordered(jnp.where(mine, other, own), order_l)
    value = ordered(jnp.where(mine, own, other), order_l)
    kept_q[...] = value[:, :HD]
    kept_kv[...] = value[:, HD:]

    small = None
    for q in range(3):
        cols = jnp.concatenate(
            [
                ref[row + 16 * q : row + 16 * q + 16, DL + PART * side : DL + PART * side + PART]
                for ref, row in paired
                for side in range(4)
            ],
            0,
        )
        term = dot_t(cols, rows_s[:, PART * q : PART * q + PART])
        small = term if small is None else small + term
    small = ordered(small.astype(BF), order_s)
    kept_s[...] = small[:, :256]
    sent_s[...] = small[:, 256:]


def attend(query, pairs, scores):
    top = None
    start = 0
    for ref, first, last in pairs:
        for lo in range(first, last, 512):
            count = 512
            block = dot_t(query, ref[lo : lo + count, :HD])
            scores[:, start : start + count] = block
            for at in range(0, count, 128):
                part = block[:, at : at + 128]
                top = part if top is None else jnp.maximum(top, part)
            start += count
    biggest = jnp.max(top, axis=1, keepdims=True)
    total, mixed = None, None
    start = 0
    for ref, first, last in pairs:
        for lo in range(first, last, 512):
            count = 512
            block = scores[:, start : start + count]
            weights = jnp.exp2((block - biggest) * (HD**-0.5 * LOG2E))
            for at in range(0, count, 128):
                part = weights[:, at : at + 128]
                total = part if total is None else total + part
            values = ref[lo : lo + count, HD:]
            term = jnp.dot(weights.astype(BF), values, preferred_element_type=F32)
            mixed = term if mixed is None else mixed + term
            start += count
    return (mixed / jnp.sum(total, axis=1, keepdims=True)).astype(BF)


def large_body(
    where, kept, taken, map_left, map_right, own, side, side_g, far, far_g,
    keep, send, scores, query,
):
    pairs = ((own, 0, 1024), (side, 0, 1024), (side_g, 0, 1024), (far, 0, 512), (far_g, 0, 512))
    core, z, x = where[0], where[1], where[2]
    way = 2 * core - 1
    keep[...] = jnp.zeros_like(keep)
    send[...] = jnp.zeros_like(send)
    query[:256, :] = kept[...]
    query[256:, :] = taken[:, :HD]

    @pl.loop(0, 2)
    def _(s):
        done = attend(query[pl.ds(pl.multiple_of(s * 256, 256), 256), :], pairs, scores)
        left = GUIDANCE * jnp.dot(done, map_left[...], preferred_element_type=F32)
        right = GUIDANCE * jnp.dot(done, map_right[...], preferred_element_type=F32)
        x_own = x ^ s

        def chip(step, x_at):
            return (z + 8 + step) % 8 * 4 + x_at

        def folded(row):
            return left[row : row + 8] + right[row + 8 : row + 16]

        for step, row in ((0, 0), (4, 224)) + tuple((way * i, 64 * i - 32) for i in (1, 2, 3)):
            keep[chip(step, x_own)] = folded(row)
            keep[chip(step, x_own ^ 3)] = folded(row + 16)
        for i in (1, 2, 3):
            send[chip(way * i, x_own)] = folded(64 * i)
            send[chip(way * i, x_own ^ 3)] = folded(64 * i + 16)


def pack_body(where, own, x1, x1_g, x2, got, x2_g, out):
    out[0:128, :] = own[...]
    out[128:256, :] = x1[0:128, :]
    out[256:384, :] = x1_g[128:256, :]
    out[384:512, :] = x2[...]
    out[512:640, :] = got[...]
    out[640:768, :] = x1[128:256, :]
    out[768:896, :] = x1_g[0:128, :]
    out[896:1024, :] = x2_g[...]


def small_body(
    where, query, map_left, map_right, keep, got, own, side, side_g, far, far_g, out, scores
):
    pairs = ((own, 0, 1024), (side, 0, 1024), (side_g, 0, 1024), (far, 0, 512), (far_g, 0, 512))
    x = where[2]
    done = attend(query[...], pairs, scores)
    left = (1.0 - GUIDANCE) * jnp.dot(done, map_left[...], preferred_element_type=F32)
    right = (1.0 - GUIDANCE) * jnp.dot(done, map_right[...], preferred_element_type=F32)
    out[...] = keep[...] + got[...]
    for z in range(8):
        out[z * 4 + x] += left[16 * z : 16 * z + 8] + right[16 * z + 8 : 16 * z + 16]


def shards(
    latent_large,
    latent_small,
    gain_large,
    gain_small,
    qkv_large,
    qkv_small,
    mix_large,
    mix_small,
    head_large,
    head_small,
):
    core, z, x, y = (lax.axis_index(name) for name in ("grp", "z", "x", "y"))
    x_low, z_low = x & 1, z & 1
    where = jnp.stack([core, z, x, y])

    mine, other, small = call(
        norm_body,
        [((16, DL), BF), ((16, DL), BF), ((64, KS), BF)],
        (where, latent_large, latent_small, gain_large, gain_small),
        [
            pltpu.VMEM((32, DL), BF),
            pltpu.VMEM((32, DS), BF),
            pltpu.VMEM((DL,), F32),
            pltpu.VMEM((DS,), F32),
            pltpu.SemaphoreType.DMA((4,)),
        ],
        limit=60,
        placed=[SMEM] + [ANY] * 4,
    )
    w, ws = qkv_large.T, qkv_small.T
    w_g = swap(w)
    xw = flip(w, "x", 1)
    across = cross(mine)
    w_g, ws, _ = tie(w_g, ws, mine)
    w0 = jnp.concatenate([w, w_g], 0)
    y1 = spread(w0, "y")
    ws = jnp.concatenate([ws, jnp.zeros((4, DS), BF)], 0)
    ws = jnp.concatenate([ws[:, :PART], ws[:, PART : 2 * PART], ws[:, 2 * PART :]], 0)
    ws_cross = cross(ws)
    (near,) = call(
        block_body, [((64, DL + KS), BF)], (where, mine, other, across, swap(across), small)
    )

    z1 = spread(near, "z")
    ws_cross, xw, _ = tie(ws_cross, xw, near)
    ws2 = jnp.concatenate([ws, ws_cross], 1)
    xw_g = swap(xw)
    ws4 = jnp.concatenate([ws2, flip(ws2, "x", 1)], 1)
    pr = jnp.concatenate(
        [jnp.concatenate([xw, ws4], 1), jnp.concatenate([xw_g, swap(ws4)], 1)], 0
    )
    y2 = spread(pr, "y")

    map_l = lax.dynamic_slice_in_dim(mix_large, (z * 2 + (x >> 1)) * HD, HD, 0)
    map_s = lax.dynamic_slice_in_dim(mix_small, (z >> 1) * HD, HD, 0)
    swapped = swap(jnp.concatenate([map_l, map_s], 0))
    map_l = jnp.where(core == x_low, map_l, swapped[:HD])
    map_s = jnp.where(core == z_low, map_s, swapped[HD:])
    blank = jnp.zeros((HD, 64), BF)
    maps = [
        jnp.concatenate(pair, 1)
        for pair in ((map_l, blank), (blank, map_l), (map_s, blank), (blank, map_s))
    ]

    def position(y_at):
        away = (y - y_at) & 3
        return jnp.where((away & 1 == 1) & (core == 1), 4 - away, away)

    source = lax.broadcasted_iota(jnp.int32, (384, 384), 0)
    target = lax.broadcasted_iota(jnp.int32, (384, 384), 1)
    block = target // 48
    from_l = jnp.where(block // 4 == x_low, 0, 4) + position(block & 3)
    order_l = (source == from_l * 48 + target % 48).astype(BF)
    source = lax.broadcasted_iota(jnp.int32, (512, 512), 0)
    target = lax.broadcasted_iota(jnp.int32, (512, 512), 1)
    group = jnp.where((target // 256 == 0) == (core == z_low), 0, 1)
    within = target % 256
    piece = within // 12
    mask = ((piece // 4) & 3) ^ x
    side = jnp.where(mask == 3, 1, jnp.where(mask == 1, 2, jnp.where(mask == 2, 3, 0)))
    from_s = (group * 16 + position(piece & 3) * 4 + side) * 16 + within % 12
    order_s = ((source == from_s) & (within < 192)).astype(BF)

    z1, order_l, order_s, *maps = tie(z1, order_l, order_s, *maps)
    z2 = spread(z1, "z")
    y1, _ = tie(y1, z1)
    fo = spread(y1[:48], "y")
    y1_g = swap(y1)

    z3 = spread(z2, "z")
    y2, fo, _ = tie(y2, fo, z2)
    fp = spread(y2[:48], "y")
    y2_g, fo_g = swap(y2), swap(fo)

    zf = spread(z3[:32], "z")
    s_got = swap(jnp.concatenate([v[32:, DL:] for v in (z1, z2, z3)], 0))
    fp, _ = tie(fp, z3)
    fp_g = swap(fp)

    kept_q, kept_kv, sent, kept_s, sent_s = call(
        project_body,
        [((256, HD), BF), ((256, 2 * HD), BF), ((256, 384), BF)] + [((128, 256), BF)] * 2,
        (
            where, near, z1, z2, z3, zf, s_got, w0, y1, y1_g, fo, fo_g, pr, y2, y2_g, fp, fp_g,
            order_l, order_s,
        ),
        [pltpu.VMEM((128, DS), BF)],
        limit=12,
    )

    taken, taken_s = tie(flip(sent, "x", 1), flip(sent_s, "z", 1))
    kept_g = swap(kept_kv)
    taken_g = swap(taken)
    all_l = jnp.concatenate([kept_kv, taken[:, HD:], kept_g, taken_g[:, HD:]], 0)
    k_side = spread(all_l, "y")

    kept_s, taken_s = kept_s[:, :192], taken_s[:, :192]
    head_s = jnp.where(
        z_low == 0,
        jnp.concatenate([kept_s, taken_s], 1),
        jnp.concatenate([taken_s, kept_s], 1),
    )
    own_s = head_s[:, HD:]
    got_s = swap(own_s)
    x1 = spread(jnp.concatenate([own_s, got_s], 0), "x")
    x2 = flip(own_s, "x", 2)
    x1_g, x2_g = swap(x1), swap(x2)
    (all_s,) = call(
        pack_body, [((1024, 2 * HD), BF)], (where, own_s, x1, x1_g, x2, got_s, x2_g)
    )
    s_side = spread(all_s, "y")
    k_side, _ = tie(k_side, all_s)
    k_far = spread(k_side[:512], "y")
    k_side_g = swap(k_side)
    k_far, s_side = tie(k_far, s_side)
    k_far_g = swap(k_far)
    s_far = spread(s_side[:512], "y")
    s_side_g = swap(s_side)

    keep, send = call(
        large_body,
        [((32, 8, 128), F32)] * 2,
        (where, kept_q, taken, *maps[:2], all_l, k_side, k_side_g, k_far, k_far_g),
        [pltpu.VMEM((256, 4096), F32), pltpu.VMEM((512, HD), BF)],
        flops=2**32,
    )
    keep, send, s_far = tie(keep, send, s_far)
    got = swap(send)
    s_far_g = swap(s_far)
    (total,) = call(
        small_body,
        [((32, 8, 128), F32)],
        (where, head_s[:, :HD], *maps[2:], keep, got, all_s, s_side, s_side_g, s_far, s_far_g),
        [pltpu.VMEM((128, 4096), F32)],
        flops=2**30,
    )

    returned = lax.all_to_all(total, ("z", "x"), split_axis=0, concat_axis=0, tiled=True)
    returned = jnp.sum(returned, axis=0)
    latent_l = lax.dynamic_slice_in_dim(latent_large, core * 16, 16, 0)
    latent_s = lax.dynamic_slice_in_dim(latent_small, core * 16, 16, 0)
    direct = GUIDANCE * jnp.dot(latent_l, head_large, preferred_element_type=F32) + (
        1.0 - GUIDANCE
    ) * jnp.dot(latent_s, head_small, preferred_element_type=F32)
    part = direct + jnp.concatenate([returned[:, :64], returned[:, 64:]], 0)
    other_part = swap(part)
    return jnp.where(
        core == 0,
        jnp.concatenate([part, other_part], 0),
        jnp.concatenate([other_part, part], 0),
    )


def solution(mesh):
    grid = Mesh(mesh.devices.reshape(2, 8, 4, 4), ("grp", "z", "x", "y"))
    tokens = ("z", "x", "y")
    return jax.shard_map(
        shards,
        mesh=grid,
        in_specs=(
            P(tokens, None),
            P(tokens, None),
            P(),
            P(),
            P(None, ("grp",) + tokens),
            P(None, ("grp",) + tokens),
            P("grp", None),
            P("grp", None),
            P(),
            P(),
        ),
        out_specs=P(tokens, None),
        check_vma=False,
    )
```

profile of v0, /device:TPU:1, one launch (start us, length us, event | category | flops | bytes accessed | tf_op | source)
XLA Modules:
  0.0 163.0 jit_solution(6281234139480170073)
XLA Ops:
  0.0 3.2 %collective-permute-start.8 = (bf16[48,5120]{1,0:T(8,128)(2,1)}, bf16[48,5120]{1,0:T(8,128)(2,1)S(1)}, u32[]{:S(2)}, u32[]{:S(2)}) collective-permute-start(bf16[48,5120]{1,0:T(8,128)(2,1)} %bitcast.11), channel_id=1, source_target_pairs={{0,128},{128,0},{1,129},{129,1},{2,130},{130,2},{3,131},{131,3},{4... | collective-permute-start | bytes 1474568 | tf_op jit(solution)/shard_map/ppermute | solution.py:25
  3.9 2.8 %shard_map.100 = (bf16[16,5120]{1,0:T(8,128)(2,1)}, bf16[16,5120]{1,0:T(8,128)(2,1)}, bf16[64,768]{1,0:T(8,128)(2,1)}) custom-call(s32[4]{0:T(128)} %pad_add_fusion.where, bf16[32,5120]{1,0:T(8,128)(2,1)} %large.1, bf16[32,1536]{1,0:T(8,128)(2,1)} %small.1, f32[5120]{0:T(1024)} %gain_l.1, f32[1536]{0:T(1024)} %gain_s.1), custom_call_target="tpu_custom_call" | custom-call | bytes 1048576 | tf_op jit(solution)/shard_map/pallas_call | solution.py:54
  11.4 2.6 %collective-permute-done.across = bf16[16,5120]{1,0:T(8,128)(2,1)S(1)} collective-permute-done((bf16[16,5120]{1,0:T(8,128)(2,1)}, bf16[16,5120]{1,0:T(8,128)(2,1)S(1)}, u32[]{:S(2)}, u32[]{:S(2)}) %collective-permute-start) | collective-permute-done | bytes 163872 | tf_op jit(solution)/shard_map/ppermute | solution.py:33
  19.6 1.5 shard_map.101.near
  21.2 5.7 %collective-permute-start.2 = (bf16[64,5888]{1,0:T(8,128)(2,1)}, bf16[64,5888]{1,0:T(8,128)(2,1)}, u32[]{:S(2)}, u32[]{:S(2)}) collective-permute-start(bf16[64,5888]{1,0:T(8,128)(2,1)} %shard_map.101.near), channel_id=1, source_target_pairs={{0,16},{16,32},{32,48},{48,64},{64,80},{80,96},{96,112},{112,0},{1... | collective-permute-start | bytes 2261000 | tf_op jit(solution)/shard_map/ppermute | solution.py:40
  28.8 2.8 %collective-permute-start.9 = (bf16[96,5120]{1,0:T(8,128)(2,1)S(1)}, bf16[96,5120]{1,0:T(8,128)(2,1)}, u32[]{:S(2)}, u32[]{:S(2)}) collective-permute-start(bf16[96,5120]{1,0:T(8,128)(2,1)S(1)} %pad_maximum_fusion.w0), channel_id=1, source_target_pairs={{0,1},{1,2},{2,3},{3,0},{128,131},{129,128},{130,129},{131,130},{4... | collective-permute-start | bytes 2949128 | tf_op jit(solution)/shard_map/ppermute | solution.py:40
  31.6 5.7 %maximum_maximum_fusion.pr = bf16[96,7168]{1,0:T(8,128)(2,1)S(1)} fusion(bf16[48,2048]{1,0:T(8,128)(2,1)S(1)} %collective-permute-done.15, bf16[48,5120]{1,0:T(8,128)(2,1)S(1)} %collective-permute-done.14, bf16[48,1024]{1,0:T(8,128)(2,1)S(1)} %collective-permute-done.13, bf16[48,512]{1,0:T(8,128)(2,1)S(1)} %copy-done.19, bf16[16,512]{1,0:T(8,128)(2,1)S(1)} %copy-done.25, ...), kind=kLoop, calls=%fused_computation.19 | loop fusion | flops 11010048 | bytes 2752512 | tf_op jit(solution)/shard_map/concatenate | solution.py:296
  40.2 4.6 %collective-permute-start.4 = (bf16[64,5888]{1,0:T(8,128)(2,1)}, bf16[64,5888]{1,0:T(8,128)(2,1)S(1)}, u32[]{:S(2)}, u32[]{:S(2)}) collective-permute-start(bf16[64,5888]{1,0:T(8,128)(2,1)} %collective-permute-done.2.z1), channel_id=1, source_target_pairs={{0,16},{16,32},{32,48},{48,64},{64,80},{80,96},{96,112},{112,0},{1... | collective-permute-start | bytes 2261000 | tf_op jit(solution)/shard_map/ppermute | solution.py:40
  47.2 6.5 %collective-permute-done.4.z2 = bf16[64,5888]{1,0:T(8,128)(2,1)S(1)} collective-permute-done((bf16[64,5888]{1,0:T(8,128)(2,1)}, bf16[64,5888]{1,0:T(8,128)(2,1)S(1)}, u32[]{:S(2)}, u32[]{:S(2)}) %collective-permute-start.4) | collective-permute-done | bytes 753696 | tf_op jit(solution)/shard_map/ppermute | solution.py:40
  53.7 3.4 %collective-permute-start.5 = (bf16[64,5888]{1,0:T(8,128)(2,1)S(1)}, bf16[64,5888]{1,0:T(8,128)(2,1)S(1)}, u32[]{:S(2)}, u32[]{:S(2)}) collective-permute-start(bf16[64,5888]{1,0:T(8,128)(2,1)S(1)} %collective-permute-done.4.z2), channel_id=1, source_target_pairs={{0,16},{16,32},{32,48},{48,64},{64,80},{80,96},{96,112},{112,0},{1... | collective-permute-start | bytes 2261000 | tf_op jit(solution)/shard_map/ppermute | solution.py:40
  57.1 5.5 %collective-permute-done.17.fo = bf16[48,5120]{1,0:T(8,128)(2,1)S(1)} collective-permute-done((bf16[48,5120]{1,0:T(8,128)(2,1)S(1)}, bf16[48,5120]{1,0:T(8,128)(2,1)S(1)}, u32[]{:S(2)}, u32[]{:S(2)}) %collective-permute-start.17) | collective-permute-done | bytes 491552 | tf_op jit(solution)/shard_map/ppermute | solution.py:40
  63.8 3.5 %collective-permute-start.20 = (bf16[48,7168]{1,0:T(8,128)(2,1)S(1)}, bf16[48,7168]{1,0:T(8,128)(2,1)S(1)}, u32[]{:S(2)}, u32[]{:S(2)}) collective-permute-start(bf16[48,7168]{1,0:T(8,128)(2,1)S(1)} %slice.73), channel_id=1, source_target_pairs={{0,1},{1,2},{2,3},{3,0},{128,131},{129,128},{130,129},{131,130},{4... | collective-permute-start | bytes 2064392 | tf_op jit(solution)/shard_map/ppermute | solution.py:40
  67.8 7.4 %collective-permute-done.20.fp = bf16[48,7168]{1,0:T(8,128)(2,1)S(1)} collective-permute-done((bf16[48,7168]{1,0:T(8,128)(2,1)S(1)}, bf16[48,7168]{1,0:T(8,128)(2,1)S(1)}, u32[]{:S(2)}, u32[]{:S(2)}) %collective-permute-start.20) | collective-permute-done | bytes 688160 | tf_op jit(solution)/shard_map/ppermute | solution.py:40
  75.2 2.4 %collective-permute-start.21 = (bf16[48,7168]{1,0:T(8,128)(2,1)S(1)}, bf16[48,7168]{1,0:T(8,128)(2,1)S(1)}, u32[]{:S(2)}, u32[]{:S(2)}) collective-permute-start(bf16[48,7168]{1,0:T(8,128)(2,1)S(1)} %collective-permute-done.20.fp), channel_id=1, source_target_pairs={{0,128},{128,0},{1,129},{129,1},{2,130},{130,2},{3,131},{131,3},{4... | collective-permute-start | bytes 2064392 | tf_op jit(solution)/shard_map/ppermute | solution.py:25
  77.6 4.7 %collective-permute-start.6 = (bf16[32,5888]{1,0:T(8,128)(2,1)S(1)}, bf16[32,5888]{1,0:T(8,128)(2,1)S(1)}, u32[]{:S(2)}, u32[]{:S(2)}) collective-permute-start(bf16[32,5888]{1,0:T(8,128)(2,1)S(1)} %slice.86), channel_id=1, source_target_pairs={{0,16},{16,32},{32,48},{48,64},{64,80},{80,96},{96,112},{112,0},{1... | collective-permute-start | bytes 1130504 | tf_op jit(solution)/shard_map/ppermute | solution.py:40
  84.6 2.2 %collective-permute-done.6.zf = bf16[32,5888]{1,0:T(8,128)(2,1)S(1)} collective-permute-done((bf16[32,5888]{1,0:T(8,128)(2,1)S(1)}, bf16[32,5888]{1,0:T(8,128)(2,1)S(1)}, u32[]{:S(2)}, u32[]{:S(2)}) %collective-permute-start.6) | collective-permute-done | bytes 376864 | tf_op jit(solution)/shard_map/ppermute | solution.py:40
  86.8 7.4 %shard_map.102 = (bf16[256,128]{1,0:T(8,128)(2,1)S(1)}, bf16[256,256]{1,0:T(8,128)(2,1)S(1)}, bf16[256,384]{1,0:T(8,128)(2,1)}, bf16[128,256]{1,0:T(8,128)(2,1)S(1)}, bf16[128,256]{1,0:T(8,128)(2,1)}) custom-call(s32[4]{0:T(128)S(1)} %copy-done.11, bf16[64,5888]{1,0:T(8,128)(2,1)} %shard_map.101.near, bf16[64,5888]{1,0:T(8,128)(2,1)} %collective-permute-done.2.z1, ...), custom_call_target="tpu_custom_call" | custom-call | bytes 1048576 | tf_op jit(solution)/shard_map/pallas_call | solution.py:54
  96.1 3.3 %collective-permute-done.23 = bf16[128,256]{1,0:T(8,128)(2,1)S(1)} collective-permute-done((bf16[128,256]{1,0:T(8,128)(2,1)}, bf16[128,256]{1,0:T(8,128)(2,1)S(1)}, u32[]{:S(2)}, u32[]{:S(2)}) %collective-permute-start.23) | collective-permute-done | bytes 65568 | tf_op jit(solution)/shard_map/ppermute | solution.py:25
  99.4 1.4 collective-permute-done.22.taken
  100.8 3.0 %collective-permute-start.25 = (bf16[256,384]{1,0:T(8,128)(2,1)S(1)}, bf16[256,384]{1,0:T(8,128)(2,1)S(1)}, u32[]{:S(2)}, u32[]{:S(2)}) collective-permute-start(bf16[256,384]{1,0:T(8,128)(2,1)S(1)} %collective-permute-done.22.taken), channel_id=1, source_target_pairs={{0,128},{128,0},{1,129},{129,1},{2,130},{130,2},{3,131},{131,3},{4... | collective-permute-start | bytes 589832 | tf_op jit(solution)/shard_map/ppermute | solution.py:25
  110.2 2.3 %collective-permute-done.28.x1 = bf16[256,256]{1,0:T(8,128)(2,1)S(1)} collective-permute-done((bf16[256,256]{1,0:T(8,128)(2,1)S(1)}, bf16[256,256]{1,0:T(8,128)(2,1)S(1)}, u32[]{:S(2)}, u32[]{:S(2)}) %collective-permute-start.28) | collective-permute-done | bytes 131104 | tf_op jit(solution)/shard_map/ppermute | solution.py:40
  112.5 3.4 %collective-permute-start.29 = (bf16[256,256]{1,0:T(8,128)(2,1)S(1)}, bf16[256,256]{1,0:T(8,128)(2,1)S(1)}, u32[]{:S(2)}, u32[]{:S(2)}) collective-permute-start(bf16[256,256]{1,0:T(8,128)(2,1)S(1)} %collective-permute-done.28.x1), channel_id=1, source_target_pairs={{0,128},{128,0},{1,129},{129,1},{2,130},{130,2},{3,131},{131,3},{4... | collective-permute-start | bytes 393224 | tf_op jit(solution)/shard_map/ppermute | solution.py:25
  117.7 2.0 %collective-permute-start.34 = (bf16[1024,256]{1,0:T(8,128)(2,1)S(1)}, bf16[1024,256]{1,0:T(8,128)(2,1)S(1)}, u32[]{:S(2)}, u32[]{:S(2)}) collective-permute-start(bf16[1024,256]{1,0:T(8,128)(2,1)S(1)} %shard_map.103.own), channel_id=1, source_target_pairs={{0,1},{1,2},{2,3},{3,0},{128,131},{129,128},{130,129},{131,130},{4... | collective-permute-start | bytes 1572872 | tf_op jit(solution)/shard_map/ppermute | solution.py:40
  120.0 6.2 %collective-permute-done.34.side = bf16[1024,256]{1,0:T(8,128)(2,1)S(1)} collective-permute-done((bf16[1024,256]{1,0:T(8,128)(2,1)S(1)}, bf16[1024,256]{1,0:T(8,128)(2,1)S(1)}, u32[]{:S(2)}, u32[]{:S(2)}) %collective-permute-start.34) | collective-permute-done | bytes 524320 | tf_op jit(solution)/shard_map/ppermute | solution.py:40
  126.1 2.8 %collective-permute-done.33.far = bf16[512,256]{1,0:T(8,128)(2,1)S(1)} collective-permute-done((bf16[512,256]{1,0:T(8,128)(2,1)S(1)}, bf16[512,256]{1,0:T(8,128)(2,1)S(1)}, u32[]{:S(2)}, u32[]{:S(2)}) %collective-permute-start.33) | collective-permute-done | bytes 262176 | tf_op jit(solution)/shard_map/ppermute | solution.py:40
  128.9 2.2 %collective-permute-start.35 = (bf16[512,256]{1,0:T(8,128)(2,1)S(1)}, bf16[512,256]{1,0:T(8,128)(2,1)S(1)}, u32[]{:S(2)}, u32[]{:S(2)}) collective-permute-start(bf16[512,256]{1,0:T(8,128)(2,1)S(1)} %collective-permute-done.33.far), channel_id=1, source_target_pairs={{0,128},{128,0},{1,129},{129,1},{2,130},{130,2},{3,131},{131,3},{4... | collective-permute-start | bytes 786440 | tf_op jit(solution)/shard_map/ppermute | solution.py:25
  132.5 4.6 %shard_map.104 = (f32[32,8,128]{2,1,0:T(8,128)S(1)}, f32[32,8,128]{2,1,0:T(8,128)S(1)}) custom-call(s32[4]{0:T(128)S(1)} %copy-done.11, bf16[256,128]{1,0:T(8,128)(2,1)S(1)} %copy-done.13, bf16[256,384]{1,0:T(8,128)(2,1)S(1)} %collective-permute-done.22.taken, bf16[128,128]{1,0:T(8,128)(2,1)S(1)} %copy-done.9, bf16[128,128]{1,0:T(8,128)(2,1)S(1)} %copy-done.10, ...), custom_call_target="tpu_custom_call" | custom-call | flops 4294967296 | bytes 1048576 | tf_op jit(solution)/shard_map/pallas_call | solution.py:54
  137.1 2.3 %collective-permute-start.39 = (bf16[512,256]{1,0:T(8,128)(2,1)S(1)}, bf16[512,256]{1,0:T(8,128)(2,1)S(1)}, u32[]{:S(2)}, u32[]{:S(2)}) collective-permute-start(bf16[512,256]{1,0:T(8,128)(2,1)S(1)} %collective-permute-done.36.far), channel_id=1, source_target_pairs={{0,128},{128,0},{1,129},{129,1},{2,130},{130,2},{3,131},{131,3},{4... | collective-permute-start | bytes 786440 | tf_op jit(solution)/shard_map/ppermute | solution.py:25
  140.8 2.5 %shard_map.105 = f32[32,8,128]{2,1,0:T(8,128)} custom-call(s32[4]{0:T(128)S(1)} %copy-done.11, bf16[128,128]{1,0:T(8,128)(2,1)S(1)} %slice.89.query, bf16[128,128]{1,0:T(8,128)(2,1)S(1)} %copy-done.8, bf16[128,128]{1,0:T(8,128)(2,1)S(1)} %copy-done.7, f32[32,8,128]{2,1,0:T(8,128)S(1)} %get-tuple-element.68.keep, ...), custom_call_target="tpu_custom_call" | custom-call | flops 1073741824 | bytes 1048576 | tf_op jit(solution)/shard_map/pallas_call | solution.py:54
  143.2 6.6 %all-to-all-start = ((f32[32,8,128]{2,1,0:T(8,128)}), f32[32,8,128]{2,1,0:T(8,128)S(1)}, u32[]{:S(2)}, u32[]{:S(2)}) async-start(f32[32,8,128]{2,1,0:T(8,128)} %shard_map.105), calls=%async_computation | async-start | bytes 262144 | tf_op jit(solution)/shard_map/all_to_all | solution.py:405
  150.2 9.0 %all-to-all-done = f32[32,8,128]{2,1,0:T(8,128)S(1)} async-done(((f32[32,8,128]{2,1,0:T(8,128)}), f32[32,8,128]{2,1,0:T(8,128)S(1)}, u32[]{:S(2)}, u32[]{:S(2)}) %all-to-all-start) | async-done | bytes 131104 | tf_op jit(solution)/shard_map/all_to_all | solution.py:405
  159.5 2.1 %collective-permute-start.40 = (f32[16,64]{1,0:T(8,128)S(1)}, f32[16,64]{1,0:T(8,128)S(1)}, u32[]{:S(2)}, u32[]{:S(2)}) collective-permute-start(f32[16,64]{1,0:T(8,128)S(1)} %fusion.5), channel_id=1, source_target_pairs={{0,128},{128,0},{1,129},{129,1},{2,130},{130,2},{3,131},{131,3},{4... | collective-permute-start | bytes 12296 | tf_op jit(solution)/shard_map/ppermute | solution.py:25
  (165 shorter events, 36.9 us)
Async XLA Ops:
  0.0 14.8 %collective-permute-start.8 = (bf16[48,5120]{1,0:T(8,128)(2,1)}, bf16[48,5120]{1,0:T(8,128)(2,1)S(1)}, u32[]{:S(2)}, u32[]{:S(2)}) collective-permute-start(bf16[48,5120]{1,0:T(8,128)(2,1)} %bitcast.11), channel_id=1, source_target_pairs={{0,128},{128,0},{1,129},{129,1},{2,130},{130,2},{3,131},{131,3},{4... | collective-permute-start | bytes 1474568 | tf_op jit(solution)/shard_map/ppermute | solution.py:25
  3.2 17.8 %collective-permute-start.12 = (bf16[48,5120]{1,0:T(8,128)(2,1)}, bf16[48,5120]{1,0:T(8,128)(2,1)S(1)}, u32[]{:S(2)}, u32[]{:S(2)}) collective-permute-start(bf16[48,5120]{1,0:T(8,128)(2,1)} %bitcast.12), channel_id=1, source_target_pairs={{0,4},{4,0},{8,12},{12,8},{1,5},{5,1},{9,13},{13,9},{2,6},{6,2},{1... | collective-permute-start | bytes 1474568 | tf_op jit(solution)/shard_map/ppermute | solution.py:25
  6.7 7.3 %collective-permute-start = (bf16[16,5120]{1,0:T(8,128)(2,1)}, bf16[16,5120]{1,0:T(8,128)(2,1)S(1)}, u32[]{:S(2)}, u32[]{:S(2)}) collective-permute-start(bf16[16,5120]{1,0:T(8,128)(2,1)} %get-tuple-element.38.mine), channel_id=1, source_target_pairs={{0,12},{12,0},{4,8},{8,4},{1,13},{13,1},{5,9},{9,5},{2,14},{14,2},... | collective-permute-start | bytes 491528 | tf_op jit(solution)/shard_map/ppermute | solution.py:33
  10.4 28.2 %collective-permute-start.3 = (bf16[256,64]{1,0:T(8,128)(2,1)}, bf16[256,64]{1,0:T(8,128)(2,1)}, u32[]{:S(2)}, u32[]{:S(2)}) collective-permute-start(bf16[256,64]{1,0:T(8,128)(2,1)} %pad_maximum_fusion.6), channel_id=1, source_target_pairs={{0,128},{128,0},{1,129},{129,1},{2,130},{130,2},{3,131},{131,3},{4... | collective-permute-start | bytes 98312 | tf_op jit(solution)/shard_map/ppermute | solution.py:25
  14.9 6.2 %collective-permute-start.11 = (bf16[48,512]{1,0:T(8,128)(2,1)S(1)}, bf16[48,512]{1,0:T(8,128)(2,1)S(1)}, u32[]{:S(2)}, u32[]{:S(2)}) collective-permute-start(bf16[48,512]{1,0:T(8,128)(2,1)S(1)} %pad_maximum_fusion.7), channel_id=1, source_target_pairs={{0,12},{12,0},{4,8},{8,4},{1,13},{13,1},{5,9},{9,5},{2,14},{14,2},... | collective-permute-start | bytes 147464 | tf_op jit(solution)/shard_map/ppermute | solution.py:33
  21.1 5.8 %collective-permute-start.13 = (bf16[48,1024]{1,0:T(8,128)(2,1)S(1)}, bf16[48,1024]{1,0:T(8,128)(2,1)S(1)}, u32[]{:S(2)}, u32[]{:S(2)}) collective-permute-start(bf16[48,1024]{1,0:T(8,128)(2,1)S(1)} %pad_maximum_fusion.5), channel_id=1, source_target_pairs={{0,4},{4,0},{8,12},{12,8},{1,5},{5,1},{9,13},{13,9},{2,6},{6,2},{1... | collective-permute-start | bytes 294920 | tf_op jit(solution)/shard_map/ppermute | solution.py:25
  21.2 19.0 %collective-permute-start.2 = (bf16[64,5888]{1,0:T(8,128)(2,1)}, bf16[64,5888]{1,0:T(8,128)(2,1)}, u32[]{:S(2)}, u32[]{:S(2)}) collective-permute-start(bf16[64,5888]{1,0:T(8,128)(2,1)} %shard_map.101.near), channel_id=1, source_target_pairs={{0,16},{16,32},{32,48},{48,64},{64,80},{80,96},{96,112},{112,0},{1... | collective-permute-start | bytes 2261000 | tf_op jit(solution)/shard_map/ppermute | solution.py:40
  26.9 4.7 %collective-permute-start.14 = (bf16[48,5120]{1,0:T(8,128)(2,1)S(1)}, bf16[48,5120]{1,0:T(8,128)(2,1)S(1)}, u32[]{:S(2)}, u32[]{:S(2)}) collective-permute-start(bf16[48,5120]{1,0:T(8,128)(2,1)S(1)} %collective-permute-done.12), channel_id=1, source_target_pairs={{0,128},{128,0},{1,129},{129,1},{2,130},{130,2},{3,131},{131,3},{4... | collective-permute-start | bytes 1474568 | tf_op jit(solution)/shard_map/ppermute | solution.py:25
  26.9 4.6 %collective-permute-start.15 = (bf16[48,2048]{1,0:T(8,128)(2,1)S(1)}, bf16[48,2048]{1,0:T(8,128)(2,1)S(1)}, u32[]{:S(2)}, u32[]{:S(2)}) collective-permute-start(bf16[48,2048]{1,0:T(8,128)(2,1)S(1)} %pad_maximum_fusion.2), channel_id=1, source_target_pairs={{0,128},{128,0},{1,129},{129,1},{2,130},{130,2},{3,131},{131,3},{4... | collective-permute-start | bytes 589832 | tf_op jit(solution)/shard_map/ppermute | solution.py:25
  28.8 16.0 %collective-permute-start.9 = (bf16[96,5120]{1,0:T(8,128)(2,1)S(1)}, bf16[96,5120]{1,0:T(8,128)(2,1)}, u32[]{:S(2)}, u32[]{:S(2)}) collective-permute-start(bf16[96,5120]{1,0:T(8,128)(2,1)S(1)} %pad_maximum_fusion.w0), channel_id=1, source_target_pairs={{0,1},{1,2},{2,3},{3,0},{128,131},{129,128},{130,129},{131,130},{4... | collective-permute-start | bytes 2949128 | tf_op jit(solution)/shard_map/ppermute | solution.py:40
  37.3 25.3 %collective-permute-start.16 = (bf16[96,7168]{1,0:T(8,128)(2,1)S(1)}, bf16[96,7168]{1,0:T(8,128)(2,1)}, u32[]{:S(2)}, u32[]{:S(2)}) collective-permute-start(bf16[96,7168]{1,0:T(8,128)(2,1)S(1)} %maximum_maximum_fusion.pr), channel_id=1, source_target_pairs={{0,1},{1,2},{2,3},{3,0},{128,131},{129,128},{130,129},{131,130},{4... | collective-permute-start | bytes 4128776 | tf_op jit(solution)/shard_map/ppermute | solution.py:40
  40.2 13.5 %collective-permute-start.4 = (bf16[64,5888]{1,0:T(8,128)(2,1)}, bf16[64,5888]{1,0:T(8,128)(2,1)S(1)}, u32[]{:S(2)}, u32[]{:S(2)}) collective-permute-start(bf16[64,5888]{1,0:T(8,128)(2,1)} %collective-permute-done.2.z1), channel_id=1, source_target_pairs={{0,16},{16,32},{32,48},{48,64},{64,80},{80,96},{96,112},{112,0},{1... | collective-permute-start | bytes 2261000 | tf_op jit(solution)/shard_map/ppermute | solution.py:40
  45.9 16.8 %collective-permute-start.17 = (bf16[48,5120]{1,0:T(8,128)(2,1)S(1)}, bf16[48,5120]{1,0:T(8,128)(2,1)S(1)}, u32[]{:S(2)}, u32[]{:S(2)}) collective-permute-start(bf16[48,5120]{1,0:T(8,128)(2,1)S(1)} %slice.72), channel_id=1, source_target_pairs={{0,1},{1,2},{2,3},{3,0},{128,131},{129,128},{130,129},{131,130},{4... | collective-permute-start | bytes 1474568 | tf_op jit(solution)/shard_map/ppermute | solution.py:40
  53.7 14.1 %collective-permute-start.5 = (bf16[64,5888]{1,0:T(8,128)(2,1)S(1)}, bf16[64,5888]{1,0:T(8,128)(2,1)S(1)}, u32[]{:S(2)}, u32[]{:S(2)}) collective-permute-start(bf16[64,5888]{1,0:T(8,128)(2,1)S(1)} %collective-permute-done.4.z2), channel_id=1, source_target_pairs={{0,16},{16,32},{32,48},{48,64},{64,80},{80,96},{96,112},{112,0},{1... | collective-permute-start | bytes 2261000 | tf_op jit(solution)/shard_map/ppermute | solution.py:40
  63.8 11.4 %collective-permute-start.20 = (bf16[48,7168]{1,0:T(8,128)(2,1)S(1)}, bf16[48,7168]{1,0:T(8,128)(2,1)S(1)}, u32[]{:S(2)}, u32[]{:S(2)}) collective-permute-start(bf16[48,7168]{1,0:T(8,128)(2,1)S(1)} %slice.73), channel_id=1, source_target_pairs={{0,1},{1,2},{2,3},{3,0},{128,131},{129,128},{130,129},{131,130},{4... | collective-permute-start | bytes 2064392 | tf_op jit(solution)/shard_map/ppermute | solution.py:40
  67.3 19.5 %collective-permute-start.19 = (bf16[96,7168]{1,0:T(8,128)(2,1)}, bf16[96,7168]{1,0:T(8,128)(2,1)S(1)}, u32[]{:S(2)}, u32[]{:S(2)}) collective-permute-start(bf16[96,7168]{1,0:T(8,128)(2,1)} %collective-permute-done.16.y2), channel_id=1, source_target_pairs={{0,128},{128,0},{1,129},{129,1},{2,130},{130,2},{3,131},{131,3},{4... | collective-permute-start | bytes 4128776 | tf_op jit(solution)/shard_map/ppermute | solution.py:25
  67.3 15.8 %collective-permute-start.10 = (bf16[96,5120]{1,0:T(8,128)(2,1)}, bf16[96,5120]{1,0:T(8,128)(2,1)S(1)}, u32[]{:S(2)}, u32[]{:S(2)}) collective-permute-start(bf16[96,5120]{1,0:T(8,128)(2,1)} %collective-permute-done.9.y1), channel_id=1, source_target_pairs={{0,128},{128,0},{1,129},{129,1},{2,130},{130,2},{3,131},{131,3},{4... | collective-permute-start | bytes 2949128 | tf_op jit(solution)/shard_map/ppermute | solution.py:25
  75.2 11.7 %collective-permute-start.21 = (bf16[48,7168]{1,0:T(8,128)(2,1)S(1)}, bf16[48,7168]{1,0:T(8,128)(2,1)S(1)}, u32[]{:S(2)}, u32[]{:S(2)}) collective-permute-start(bf16[48,7168]{1,0:T(8,128)(2,1)S(1)} %collective-permute-done.20.fp), channel_id=1, source_target_pairs={{0,128},{128,0},{1,129},{129,1},{2,130},{130,2},{3,131},{131,3},{4... | collective-permute-start | bytes 2064392 | tf_op jit(solution)/shard_map/ppermute | solution.py:25
  77.6 7.0 %collective-permute-start.18 = (bf16[48,5120]{1,0:T(8,128)(2,1)S(1)}, bf16[48,5120]{1,0:T(8,128)(2,1)S(1)}, u32[]{:S(2)}, u32[]{:S(2)}) collective-permute-start(bf16[48,5120]{1,0:T(8,128)(2,1)S(1)} %collective-permute-done.17.fo), channel_id=1, source_target_pairs={{0,128},{128,0},{1,129},{129,1},{2,130},{130,2},{3,131},{131,3},{4... | collective-permute-start | bytes 1474568 | tf_op jit(solution)/shard_map/ppermute | solution.py:25
  77.6 9.2 %collective-permute-start.6 = (bf16[32,5888]{1,0:T(8,128)(2,1)S(1)}, bf16[32,5888]{1,0:T(8,128)(2,1)S(1)}, u32[]{:S(2)}, u32[]{:S(2)}) collective-permute-start(bf16[32,5888]{1,0:T(8,128)(2,1)S(1)} %slice.86), channel_id=1, source_target_pairs={{0,16},{16,32},{32,48},{48,64},{64,80},{80,96},{96,112},{112,0},{1... | collective-permute-start | bytes 1130504 | tf_op jit(solution)/shard_map/ppermute | solution.py:40
  96.1 4.7 %collective-permute-start.22 = (bf16[256,384]{1,0:T(8,128)(2,1)}, bf16[256,384]{1,0:T(8,128)(2,1)S(1)}, u32[]{:S(2)}, u32[]{:S(2)}) collective-permute-start(bf16[256,384]{1,0:T(8,128)(2,1)} %get-tuple-element.53), channel_id=1, source_target_pairs={{0,4},{4,0},{8,12},{12,8},{1,5},{5,1},{9,13},{13,9},{2,6},{6,2},{1... | collective-permute-start | bytes 589832 | tf_op jit(solution)/shard_map/ppermute | solution.py:25
  100.8 5.4 %collective-permute-start.25 = (bf16[256,384]{1,0:T(8,128)(2,1)S(1)}, bf16[256,384]{1,0:T(8,128)(2,1)S(1)}, u32[]{:S(2)}, u32[]{:S(2)}) collective-permute-start(bf16[256,384]{1,0:T(8,128)(2,1)S(1)} %collective-permute-done.22.taken), channel_id=1, source_target_pairs={{0,128},{128,0},{1,129},{129,1},{2,130},{130,2},{3,131},{131,3},{4... | collective-permute-start | bytes 589832 | tf_op jit(solution)/shard_map/ppermute | solution.py:25
  107.5 12.2 %collective-permute-start.26 = (bf16[1024,256]{1,0:T(8,128)(2,1)S(1)}, bf16[1024,256]{1,0:T(8,128)(2,1)S(1)}, u32[]{:S(2)}, u32[]{:S(2)}) collective-permute-start(bf16[1024,256]{1,0:T(8,128)(2,1)S(1)} %pad_maximum_fusion.1.own), channel_id=1, source_target_pairs={{0,1},{1,2},{2,3},{3,0},{128,131},{129,128},{130,129},{131,130},{4... | collective-permute-start | bytes 1572872 | tf_op jit(solution)/shard_map/ppermute | solution.py:40
  108.4 4.1 %collective-permute-start.28 = (bf16[256,256]{1,0:T(8,128)(2,1)S(1)}, bf16[256,256]{1,0:T(8,128)(2,1)S(1)}, u32[]{:S(2)}, u32[]{:S(2)}) collective-permute-start(bf16[256,256]{1,0:T(8,128)(2,1)S(1)} %pad_maximum_fusion.4), channel_id=1, source_target_pairs={{0,4},{4,8},{8,12},{12,0},{128,140},{132,128},{136,132},{140,136},... | collective-permute-start | bytes 393224 | tf_op jit(solution)/shard_map/ppermute | solution.py:40
  109.2 6.7 %collective-permute-start.30 = (bf16[128,256]{1,0:T(8,128)(2,1)S(1)}, bf16[128,256]{1,0:T(8,128)(2,1)S(1)}, u32[]{:S(2)}, u32[]{:S(2)}) collective-permute-start(bf16[128,256]{1,0:T(8,128)(2,1)S(1)} %slice.91.own), channel_id=1, source_target_pairs={{0,8},{4,12},{8,0},{12,4},{1,9},{5,13},{9,1},{13,5},{2,10},{6,14},... | collective-permute-start | bytes 196616 | tf_op jit(solution)/shard_map/ppermute | solution.py:25
  112.5 4.7 %collective-permute-start.29 = (bf16[256,256]{1,0:T(8,128)(2,1)S(1)}, bf16[256,256]{1,0:T(8,128)(2,1)S(1)}, u32[]{:S(2)}, u32[]{:S(2)}) collective-permute-start(bf16[256,256]{1,0:T(8,128)(2,1)S(1)} %collective-permute-done.28.x1), channel_id=1, source_target_pairs={{0,128},{128,0},{1,129},{129,1},{2,130},{130,2},{3,131},{131,3},{4... | collective-permute-start | bytes 393224 | tf_op jit(solution)/shard_map/ppermute | solution.py:25
  117.7 8.4 %collective-permute-start.34 = (bf16[1024,256]{1,0:T(8,128)(2,1)S(1)}, bf16[1024,256]{1,0:T(8,128)(2,1)S(1)}, u32[]{:S(2)}, u32[]{:S(2)}) collective-permute-start(bf16[1024,256]{1,0:T(8,128)(2,1)S(1)} %shard_map.103.own), channel_id=1, source_target_pairs={{0,1},{1,2},{2,3},{3,0},{128,131},{129,128},{130,129},{131,130},{4... | collective-permute-start | bytes 1572872 | tf_op jit(solution)/shard_map/ppermute | solution.py:40
  119.8 9.2 %collective-permute-start.33 = (bf16[512,256]{1,0:T(8,128)(2,1)S(1)}, bf16[512,256]{1,0:T(8,128)(2,1)S(1)}, u32[]{:S(2)}, u32[]{:S(2)}) collective-permute-start(bf16[512,256]{1,0:T(8,128)(2,1)S(1)} %slice.80), channel_id=1, source_target_pairs={{0,1},{1,2},{2,3},{3,0},{128,131},{129,128},{130,129},{131,130},{4... | collective-permute-start | bytes 786440 | tf_op jit(solution)/shard_map/ppermute | solution.py:40
  119.9 12.5 %collective-permute-start.32 = (bf16[1024,256]{1,0:T(8,128)(2,1)S(1)}, bf16[1024,256]{1,0:T(8,128)(2,1)S(1)}, u32[]{:S(2)}, u32[]{:S(2)}) collective-permute-start(bf16[1024,256]{1,0:T(8,128)(2,1)S(1)} %collective-permute-done.26.side), channel_id=1, source_target_pairs={{0,128},{128,0},{1,129},{129,1},{2,130},{130,2},{3,131},{131,3},{4... | collective-permute-start | bytes 1572872 | tf_op jit(solution)/shard_map/ppermute | solution.py:25
  131.2 9.5 %collective-permute-start.38 = (bf16[1024,256]{1,0:T(8,128)(2,1)S(1)}, bf16[1024,256]{1,0:T(8,128)(2,1)S(1)}, u32[]{:S(2)}, u32[]{:S(2)}) collective-permute-start(bf16[1024,256]{1,0:T(8,128)(2,1)S(1)} %collective-permute-done.34.side), channel_id=1, source_target_pairs={{0,128},{128,0},{1,129},{129,1},{2,130},{130,2},{3,131},{131,3},{4... | collective-permute-start | bytes 1572872 | tf_op jit(solution)/shard_map/ppermute | solution.py:25
  131.3 5.7 %collective-permute-start.36 = (bf16[512,256]{1,0:T(8,128)(2,1)S(1)}, bf16[512,256]{1,0:T(8,128)(2,1)S(1)}, u32[]{:S(2)}, u32[]{:S(2)}) collective-permute-start(bf16[512,256]{1,0:T(8,128)(2,1)S(1)} %slice.81), channel_id=1, source_target_pairs={{0,1},{1,2},{2,3},{3,0},{128,131},{129,128},{130,129},{131,130},{4... | collective-permute-start | bytes 786440 | tf_op jit(solution)/shard_map/ppermute | solution.py:40
  143.2 16.0 %all-to-all-start = ((f32[32,8,128]{2,1,0:T(8,128)}), f32[32,8,128]{2,1,0:T(8,128)S(1)}, u32[]{:S(2)}, u32[]{:S(2)}) async-start(f32[32,8,128]{2,1,0:T(8,128)} %shard_map.105), calls=%async_computation | async-start | bytes 262144 | tf_op jit(solution)/shard_map/all_to_all | solution.py:405
  (42 other events, 502.7 us)
where the time goes:
time: 164 us; the launch traced here: 163 us
  starting transfers between devices  64 us (39%)
  waiting for transfers between devices  55.2 us (34%)
  Pallas kernels  19.2 us (12%)
  other arithmetic  13.3 us (8%)
  local copies, waits for them, and re-layouts  10.3 us (6%)
    ppermute x13, waiting for transfers between devices, spread(): return lax.ppermute(block, ('grp', axis), pairs)  32.9 us
    ppermute x13, starting transfers between devices, spread(): return lax.ppermute(block, ('grp', axis), pairs)  31.4 us
    ppermute x26, starting transfers between devices, flip(): return lax.ppermute(block, axis, [(i, i ^ mask) for i in range(count)])  23.2 us
    pallas_call x6, Pallas kernels, call(): pl.pallas_call(body, out_shape=[jax.ShapeDtypeStruct(shape, dtype) for sh...  19.2 us
    ppermute x26, waiting for transfers between devices, flip(): return lax.ppermute(block, axis, [(i, i ^ mask) for i in range(count)])  10.6 us
    all_to_all x1, waiting for transfers between devices, shards(): lax.all_to_all(total, ('z', 'x'), split_axis=0, concat_axis=0, tiled=True)  9.05 us
    all_to_all x1, starting transfers between devices, shards(): lax.all_to_all(total, ('z', 'x'), split_axis=0, concat_axis=0, tiled=True)  6.63 us
    concatenate x1, other arithmetic, shards(): jnp.concatenate([jnp.concatenate([xw, ws4], 1), jnp.concatenate([xw_g, sw...  5.68 us
  transfers between devices with their start and end apart: 42, of which 17 were waited for; matrix products, arithmetic and copies ran while one was open for 11% of the time, Pallas kernels for 6%

commit v1 on v0

v1 whole, which is shorter than its diff:
```python
import jax
import jax.numpy as jnp
from jax import lax
from jax.experimental import pallas as pl
from jax.experimental.pallas import tpu as pltpu
from jax.sharding import Mesh, PartitionSpec as P

HD = 128
GUIDANCE = 3.0
EPSILON = 1e-06
BF = jnp.bfloat16
F32 = jnp.float32
DL, DS = 5120, 1536
KS = DS // 2
PART = 512
LOG2E = 1.4426950408889634
VMEM = pl.BlockSpec(memory_space=pltpu.VMEM)
SMEM = pl.BlockSpec(memory_space=pltpu.SMEM)
ANY = pl.BlockSpec(memory_space=pl.ANY)
OPPOSITE = [(0, 3), (3, 0), (1, 2), (2, 1)]


def flip(block, axis, mask):
    count = lax.axis_size(axis)
    return lax.ppermute(block, axis, [(i, i ^ mask) for i in range(count)])


def swap(block):
    return flip(block, "grp", 1)


def cross(block):
    return lax.ppermute(block, "x", OPPOSITE)


def spread(block, axis):
    n = lax.axis_size(axis)
    pairs = [(i, (i + 1) % n) for i in range(n)]
    pairs += [(n + i, n + (i - 1) % n) for i in range(n)]
    return lax.ppermute(block, ("grp", axis), pairs)


def tie(*values):
    return lax.optimization_barrier(values)


def dot_t(rows, columns):
    return lax.dot_general(
        rows, columns, (((1,), (1,)), ((), ())), preferred_element_type=F32
    )


def call(body, outs, args, scratch=(), limit=16, placed=None, flops=0):
    return pl.pallas_call(
        body,
        out_shape=[jax.ShapeDtypeStruct(shape, dtype) for shape, dtype in outs],
        in_specs=placed or [SMEM] + [VMEM] * (len(args) - 1),
        out_specs=[VMEM] * len(outs),
        scratch_shapes=list(scratch),
        compiler_params=pltpu.CompilerParams(vmem_limit_bytes=limit * 2**20),
        cost_estimate=pl.CostEstimate(flops=flops, bytes_accessed=2**20, transcendentals=0),
    )(*args)


def pack(shape, pieces):
    def body(*refs):
        sources, out, sems = refs[: len(pieces)], refs[-2], refs[-1]
        tasks = []
        for i, (source, (_, part, to)) in enumerate(zip(sources, pieces)):
            source = source if part is None else source.at[part]
            tasks.append(pltpu.make_async_copy(source, out.at[to], sems.at[i]))
        for task in tasks:
            task.start()
        for task in tasks:
            task.wait()

    return pl.pallas_call(
        body,
        out_shape=jax.ShapeDtypeStruct(shape, BF),
        in_specs=[ANY] * len(pieces),
        out_specs=ANY,
        scratch_shapes=[pltpu.SemaphoreType.DMA((len(pieces),))],
        compiler_params=pltpu.CompilerParams(vmem_limit_bytes=2**20),
    )(*[piece[0] for piece in pieces])


def norm_body(
    where, large, small, gain_l, gain_s, mine, other, out_s, hold_l, hold_s, g_l, g_s, sems
):
    core = where[0]
    tasks = [
        pltpu.make_async_copy(source, target, sems.at[i])
        for i, (source, target) in enumerate(
            ((large, hold_l), (small, hold_s), (gain_l, g_l), (gain_s, g_s))
        )
    ]
    for task in tasks:
        task.start()
    for task in tasks:
        task.wait()

    def normed(latent, gain, half, width):
        values = latent[pl.ds(pl.multiple_of(half * 16, 16), 16), :].astype(F32)
        mean = jnp.mean(values * values, axis=-1, keepdims=True)
        return (values * lax.rsqrt(mean + EPSILON) * gain[...].reshape(1, width)).astype(BF)

    mine[...] = normed(hold_l, g_l, core, DL)
    other[...] = normed(hold_l, g_l, 1 - core, DL)
    for at, half in ((0, core), (32, 1 - core)):
        value = normed(hold_s, g_s, half, DS)
        out_s[at : at + 16, :] = value[:, :KS]
        out_s[at + 16 : at + 32, :] = value[:, KS:]


def ordered(value, order):
    return lax.dot_general(
        value, order[...], (((0,), (0,)), ((), ())), preferred_element_type=F32
    ).astype(BF)


def setup_body(where, mix_l, mix_s, order_l, order_s, maps):
    core, z, x, y = (where[i] for i in range(4))
    x_low, z_low = x % 2, z % 2

    def position(y_at):
        away = (y - y_at) & 3
        return jnp.where((away & 1 == 1) & (core == 1), 4 - away, away)

    def lines(size, axis):
        return lax.broadcasted_iota(jnp.int32, (1, size) if axis else (size, 1), axis)

    target = lines(384, 1)
    block = target // 48
    base = jnp.where(block // 4 == x_low, 0, 4) + position(block & 3)
    order_l[...] = (lines(384, 0) == base * 48 + target % 48).astype(F32).astype(BF)

    half = target // 192
    group = jnp.where((half == z_low) == (core == z_low), 0, 1)
    within = target % 192
    piece = within // 12
    mask = (piece // 4) ^ x
    side = jnp.where(mask == 3, 1, jnp.where(mask == 1, 2, jnp.where(mask == 2, 3, 0)))
    base = (group * 16 + position(piece & 3) * 4 + side) * 16 + within % 12
    order_s[...] = (lines(512, 0) == base).astype(F32).astype(BF)

    maps[:64, :] = mix_l[:, pl.ds(pl.multiple_of((z * 2 + x // 2) * HD, HD), HD)]
    maps[64:, :] = mix_s[:, pl.ds(pl.multiple_of(z // 2 * HD, HD), HD)]


def sides(mine, own, other):
    rows = jnp.where(mine, own, other)
    blank = jnp.zeros_like(rows)
    return jnp.concatenate([rows, blank], 0), jnp.concatenate([blank, rows], 0)


def project_small_body(
    where, own, s1, a1, a2, a3, got, ws, ws_g, yz, yz_g, far, far_g, order, query, pairs, rows
):
    core, z = where[0], where[1]
    way = 2 * core - 1

    def put(step, ref, row, col):
        at = pl.ds(pl.multiple_of((z + 8 + step) % 8 * 16, 16), 16)
        rows[at, :KS] = ref[row : row + 16, col:]
        rows[at, KS:] = ref[row + 16 : row + 32, col:]

    put(0, own, 0, 0)
    put(4, a3, 0, DL)
    for i, ref, col in ((1, s1, 0), (2, a1, DL), (3, a2, DL)):
        put(way * i, ref, 0, col)
        put(-way * i, got, 32 * i - 32, 0)

    blocks = (
        (ws, 0), (yz, 2 * DL), (far, 0), (yz_g, 2 * DL + 4 * PART),
        (ws_g, 0), (yz, 2 * DL + 4 * PART), (far_g, 0), (yz_g, 2 * DL),
    )
    small = None
    for q in range(3):
        cols = jnp.concatenate(
            [
                ref[16 * q : 16 * q + 16, col + PART * side : col + PART * side + PART]
                for ref, col in blocks
                for side in range(4)
            ],
            0,
        )
        term = dot_t(cols, rows[:, PART * q : PART * q + PART])
        small = term if small is None else small + term
    small = ordered(small.astype(BF), order)
    query[...] = small[:, :HD]
    pairs[...] = small[:, HD:]


def project_body(
    where, near, a1, a2, a3, a4, b1, b2, b3, w0, y1, y1_g, pr, y2, y2_g, far, far_g,
    order, kept, sent,
):
    core, x = where[0], where[2]
    blocks = (
        (w0, 0, 0), (y1, 0, 0), (far, 0, 0), (y1_g, 48, 0),
        (pr, 0, 0), (y2, 0, 0), (far, 0, DL), (y2_g, 48, 0),
        (w0, 48, 0), (y1, 48, 0), (far_g, 0, 0), (y1_g, 0, 0),
        (pr, 48, 0), (y2, 48, 0), (far_g, 0, DL), (y2_g, 0, 0),
    )
    total = None
    for k in range(0, DL, 1024):
        at = slice(k, k + 1024)
        cols = jnp.concatenate(
            [ref[row : row + 48, col + k : col + k + 1024] for ref, row, col in blocks], 0
        )
        rows = jnp.concatenate([ref[:, at] for ref in (near, a1, b1, a2, b2, a3, b3, a4)], 0)
        term = dot_t(cols, rows)
        total = term if total is None else total + term
    total = total.astype(BF)
    own, other = total[:384, :], total[384:, :]
    mine = core == x % 2
    sent[...] = ordered(jnp.where(mine, other, own), order)
    kept[...] = ordered(jnp.where(mine, own, other), order)


def attend(query, pairs, scores):
    top = None
    start = 0
    for ref, first, last in pairs:
        for lo in range(first, last, 512):
            count = 512
            block = dot_t(query, ref[lo : lo + count, :HD])
            scores[:, start : start + count] = block
            for at in range(0, count, 128):
                part = block[:, at : at + 128]
                top = part if top is None else jnp.maximum(top, part)
            start += count
    biggest = jnp.max(top, axis=1, keepdims=True)
    total, mixed = None, None
    start = 0
    for ref, first, last in pairs:
        for lo in range(first, last, 512):
            count = 512
            block = scores[:, start : start + count]
            weights = jnp.exp2((block - biggest) * (HD**-0.5 * LOG2E))
            for at in range(0, count, 128):
                part = weights[:, at : at + 128]
                total = part if total is None else total + part
            values = ref[lo : lo + count, HD:]
            term = jnp.dot(weights.astype(BF), values, preferred_element_type=F32)
            mixed = term if mixed is None else mixed + term
            start += count
    return (mixed / jnp.sum(total, axis=1, keepdims=True)).astype(BF)


def large_body(
    where, kept, taken, maps, maps_g, own, side, side_g, far, far_g,
    keep, send, scores, query,
):
    pairs = ((own, 0, 1024), (side, 0, 1024), (side_g, 0, 1024), (far, 0, 512), (far_g, 0, 512))
    core, z, x = where[0], where[1], where[2]
    way = 2 * core - 1
    keep[...] = jnp.zeros_like(keep)
    send[...] = jnp.zeros_like(send)
    query[:256, :] = kept[:, :HD]
    query[256:, :] = taken[:, :HD]
    map_left, map_right = sides(core == x % 2, maps[:64, :], maps_g[:64, :])

    @pl.loop(0, 2)
    def _(s):
        done = attend(query[pl.ds(pl.multiple_of(s * 256, 256), 256), :], pairs, scores)
        left = GUIDANCE * dot_t(done, map_left)
        right = GUIDANCE * dot_t(done, map_right)
        x_own = x ^ s

        def chip(step, x_at):
            return (z + 8 + step) % 8 * 4 + x_at

        def folded(row):
            return left[row : row + 8] + right[row + 8 : row + 16]

        for step, row in ((0, 0), (4, 224)) + tuple((way * i, 64 * i - 32) for i in (1, 2, 3)):
            keep[chip(step, x_own)] = folded(row)
            keep[chip(step, x_own ^ 3)] = folded(row + 16)
        for i in (1, 2, 3):
            send[chip(way * i, x_own)] = folded(64 * i)
            send[chip(way * i, x_own ^ 3)] = folded(64 * i + 16)


def small_body(
    where, query, maps, maps_g, keep, got, own, side, side_g, far, far_g, out, scores
):
    pairs = ((own, 0, 1024), (side, 0, 1024), (side_g, 0, 1024), (far, 0, 512), (far_g, 0, 512))
    core, z_at, x = where[0], where[1], where[2]
    map_left, map_right = sides(core == z_at % 2, maps[64:, :], maps_g[64:, :])
    done = attend(query[...], pairs, scores)
    left = (1.0 - GUIDANCE) * dot_t(done, map_left)
    right = (1.0 - GUIDANCE) * dot_t(done, map_right)
    out[...] = keep[...] + got[...]
    for z in range(8):
        out[z * 4 + x] += left[16 * z : 16 * z + 8] + right[16 * z + 8 : 16 * z + 16]


def shards(
    latent_large,
    latent_small,
    gain_large,
    gain_small,
    qkv_large,
    qkv_small,
    mix_large,
    mix_small,
    head_large,
    head_small,
):
    core, z, x, y = (lax.axis_index(name) for name in ("grp", "z", "x", "y"))
    x_low, z_low = x & 1, z & 1
    where = jnp.stack([core, z, x, y])

    mine, other, s0 = call(
        norm_body,
        [((16, DL), BF), ((16, DL), BF), ((64, KS), BF)],
        (where, latent_large, latent_small, gain_large, gain_small),
        [
            pltpu.VMEM((32, DL), BF),
            pltpu.VMEM((32, DS), BF),
            pltpu.VMEM((DL,), F32),
            pltpu.VMEM((DS,), F32),
            pltpu.SemaphoreType.DMA((4,)),
        ],
        limit=60,
        placed=[SMEM] + [ANY] * 4,
    )
    w, ws = qkv_large.T, qkv_small.T
    w_g = swap(w)
    xw = flip(w, "x", 1)
    across = cross(mine)
    s1 = spread(s0, "z")
    ws, mix_l, mix_s, _ = tie(ws, mix_large.T, mix_small.T, mine)
    top, low, left, right = slice(0, 48), slice(48, 96), slice(0, DL), slice(DL, None)
    near, pair, every = slice(0, 16), slice(16, 32), slice(None)
    order_l, order_s, maps = call(
        setup_body,
        [((384, 384), BF), ((512, 384), BF), ((HD, HD), BF)],
        (where, mix_l, mix_s),
    )
    w_g, _ = tie(w_g, mine)
    w0 = pack((96, DL), [(w, None, top), (w_g, None, low)])
    y1 = spread(w0, "y")
    ws = jnp.concatenate([ws, jnp.zeros((4, DS), BF)], 0)
    ws = jnp.concatenate([ws[:, :PART], ws[:, PART : 2 * PART], ws[:, 2 * PART :]], 0)
    trade = [(g * 8 + i, (1 - g) * 8 + (i ^ 1)) for g in range(2) for i in range(8) if i % 2 != g]
    ws_other = lax.ppermute(ws, ("grp", "z"), trade)

    across, s1, w0, ws_other = tie(across, s1, w0, ws_other)
    ws = jnp.where(core == z_low, ws, ws_other)
    ws_cross = cross(ws)

    def block(own, facing, small):
        return pack(
            (32, DL + KS),
            [
                (own, None, (near, left)),
                (facing, None, (pair, left)),
                (s1, small, (every, right)),
            ],
        )

    a0 = block(mine, across, slice(0, 32))
    a1 = spread(a0, "z")
    across, xw, _ = tie(across, xw, a0)
    b0 = block(other, swap(across), slice(32, 64))
    pr = pack((96, DL), [(xw, None, top), (swap(xw), None, low)])

    a1, b0, y1, pr, ws_cross, maps = tie(a1, b0, y1, pr, ws_cross, maps)
    a2 = spread(a1, "z")
    b1 = spread(b0, "z")
    y2 = spread(pr, "y")
    ws2 = jnp.concatenate([ws, ws_cross], 1)
    ws4 = jnp.concatenate([ws2, flip(ws2, "x", 1)], 1)
    ws4_g = swap(ws4)
    y1_g = swap(y1)
    maps_g = swap(maps)

    a2, b1, y1, y1_g, y2, ws4, ws4_g, maps_g = tie(a2, b1, y1, y1_g, y2, ws4, ws4_g, maps_g)
    a3 = spread(a2, "z")
    b2 = spread(b1, "z")
    ends = [slice(DL, 2 * DL), slice(2 * DL, 2 * DL + 4 * PART), slice(2 * DL + 4 * PART, None)]
    yz = spread(
        pack(
            (48, 2 * DL + 8 * PART),
            [(y1, top, (every, left)), (y2, top, (every, ends[0]))]
            + [(ws4, None, (every, ends[1])), (ws4_g, None, (every, ends[2]))],
        ),
        "y",
    )
    y2_g = swap(y2)

    a3, b2, y2_g = tie(a3, b2, y2_g)
    a4 = spread(a3, "z")
    b3 = spread(b2, "z")
    s_got = swap(
        pack(
            (96, KS),
            [
                (s1, slice(32, 64), slice(0, 32)),
                (b1, (every, right), slice(32, 64)),
                (b2, (every, right), slice(64, 96)),
            ],
        )
    )

    a4, b3, yz, s_got = tie(a4, b3, yz, s_got)
    far_s = spread(pack((48, 4 * PART), [(yz, (every, ends[1]), every)]), "y")
    yz_g = swap(yz)
    kept, sent = call(
        project_body,
        [((256, 384), BF)] * 2,
        (where, a0, a1, a2, a3, a4, b1, b2, b3)
        + (w0, y1, y1_g, pr, y2, y2_g, yz, yz_g, order_l),
        limit=12,
        flops=2**32,
    )

    taken = flip(sent, "x", 1)
    kept_g = swap(kept)
    far_s, _ = tie(far_s, sent)
    far_s_g = swap(far_s)
    query_s, own_s = call(
        project_small_body,
        [((128, HD), BF), ((128, 2 * HD), BF)],
        (where, s0, s1, a1, a2, a3, s_got, ws4, ws4_g, yz, yz_g, far_s, far_s_g, order_s),
        [pltpu.VMEM((128, DS), BF)],
        limit=6,
        flops=2**29,
    )
    got_s = swap(own_s)
    taken, got_s = tie(taken, got_s)
    x1 = spread(jnp.concatenate([own_s, got_s], 0), "x")
    x2 = flip(own_s, "x", 2)

    pairs = slice(HD, None)
    taken_g = swap(taken)
    all_l = pack(
        (1024, 2 * HD),
        [
            (value, (every, pairs), slice(256 * i, 256 * i + 256))
            for i, value in enumerate((kept, taken, kept_g, taken_g))
        ],
    )
    k_side = spread(all_l, "y")

    x1_g, x2_g = swap(x1), swap(x2)
    first, second = slice(0, 128), slice(128, 256)
    parts = ((own_s, None), (x1, first), (x1_g, second), (x2, None))
    parts += ((got_s, None), (x1, second), (x1_g, first), (x2_g, None))
    all_s = pack(
        (1024, 2 * HD),
        [(value, part, slice(128 * i, 128 * i + 128)) for i, (value, part) in enumerate(parts)],
    )
    s_side = spread(all_s, "y")
    k_side, _ = tie(k_side, all_s)
    k_far = spread(k_side[:512], "y")
    k_side_g = swap(k_side)
    k_far, _ = tie(k_far, s_side)
    k_far_g = swap(k_far)
    s_far = spread(s_side[:512], "y")
    s_side_g = swap(s_side)

    keep, send = call(
        large_body,
        [((32, 8, 128), F32)] * 2,
        (where, kept, taken, maps, maps_g, all_l, k_side, k_side_g, k_far, k_far_g),
        [pltpu.VMEM((256, 4096), F32), pltpu.VMEM((512, HD), BF)],
        flops=2**32,
    )
    keep, send, s_far = tie(keep, send, s_far)
    got = swap(send)
    s_far_g = swap(s_far)
    (total,) = call(
        small_body,
        [((32, 8, 128), F32)],
        (where, query_s, maps, maps_g, keep, got, all_s, s_side, s_side_g, s_far, s_far_g),
        [pltpu.VMEM((128, 4096), F32)],
        flops=2**30,
    )

    returned = lax.all_to_all(total, ("z", "x"), split_axis=0, concat_axis=0, tiled=True)
    returned = jnp.sum(returned, axis=0)
    latent_l = lax.dynamic_slice_in_dim(latent_large, core * 16, 16, 0)
    latent_s = lax.dynamic_slice_in_dim(latent_small, core * 16, 16, 0)
    direct = GUIDANCE * jnp.dot(latent_l, head_large, preferred_element_type=F32) + (
        1.0 - GUIDANCE
    ) * jnp.dot(latent_s, head_small, preferred_element_type=F32)
    part = direct + jnp.concatenate([returned[:, :64], returned[:, 64:]], 0)
    other_part = swap(part)
    return jnp.where(
        core == 0,
        jnp.concatenate([part, other_part], 0),
        jnp.concatenate([other_part, part], 0),
    )


def solution(mesh):
    grid = Mesh(mesh.devices.reshape(2, 8, 4, 4), ("grp", "z", "x", "y"))
    tokens = ("z", "x", "y")
    return jax.shard_map(
        shards,
        mesh=grid,
        in_specs=(
            P(tokens, None),
            P(tokens, None),
            P(),
            P(),
            P(None, ("grp",) + tokens),
            P(None, ("grp",) + tokens),
            P("grp", None),
            P("grp", None),
            P(),
            P(),
        ),
        out_specs=P(tokens, None),
        check_vma=False,
    )
```

time: 164 us -> 146 us (0.89)
  other arithmetic: 13.3 us -> 2.14 us
  local copies, waits for them, and re-layouts: 10.3 us -> 2.12 us
  waiting for transfers between devices: 55.2 us -> 63.2 us
  starting transfers between devices: 64 us -> 56.8 us
  Pallas kernels: 19.2 us -> 20.9 us
    concatenate x5 -> x0, other arithmetic: 8.47 us -> none  [the longest x1 5.68 us: shards(): jnp.concatenate([jnp.concatenate([xw, ws4], 1), jnp.concatenate([xw_g, sw...]
    ppermute x13 -> x17, starting transfers between devices: 31.4 us -> 24.3 us  [spread(): return lax.ppermute(block, ('grp', axis), pairs)]
    ppermute x26 -> x25, waiting for transfers between devices: 10.6 us -> 16.3 us  [flip(): return lax.ppermute(block, axis, [(i, i ^ mask) for i in range(count)])]
    pallas_call x0 -> x9, Pallas kernels: none -> 4.29 us  [pack(): pl.pallas_call(body, out_shape=jax.ShapeDtypeStruct(shape, BF), in_specs=...]
    ppermute x0 -> x1, waiting for transfers between devices: none -> 3.48 us  [shards(): ws_other = lax.ppermute(ws, ('grp', 'z'), trade)]
    slice x10 -> x0, local copies, waits for them, and re-layouts: 3.07 us -> none  [the longest x1 1.14 us: shards(): fp = spread(y2[:48], 'y')]
    unnamed x66 -> x36, local copies, waits for them, and re-layouts: 4.95 us -> 2 us
    pallas_call x6, Pallas kernels: 19.2 us -> 16.6 us  [call(): pl.pallas_call(body, out_shape=[jax.ShapeDtypeStruct(shape, dtype) for sh...]
  transfers between devices with their start and end apart: 42 -> 46, of which waited for: 17 -> 26; matrix products, arithmetic and copies ran while one was open for 11% -> 1% of each run, Pallas kernels for 6% -> 12%
where the time goes in v1:
time: 146 us
  waiting for transfers between devices  63.2 us (43%)
  starting transfers between devices  56.8 us (39%)
  Pallas kernels  20.9 us (14%)
  other arithmetic  2.14 us (1%)
  local copies, waits for them, and re-layouts  2.12 us (1%)
    ppermute x17, waiting for transfers between devices, spread(): return lax.ppermute(block, ('grp', axis), pairs)  34.2 us
    ppermute x17, starting transfers between devices, spread(): return lax.ppermute(block, ('grp', axis), pairs)  24.3 us
    ppermute x25, starting transfers between devices, flip(): return lax.ppermute(block, axis, [(i, i ^ mask) for i in range(count)])  22 us
    pallas_call x6, Pallas kernels, call(): pl.pallas_call(body, out_shape=[jax.ShapeDtypeStruct(shape, dtype) for sh...  16.6 us
    ppermute x25, waiting for transfers between devices, flip(): return lax.ppermute(block, axis, [(i, i ^ mask) for i in range(count)])  16.3 us
    all_to_all x1, waiting for transfers between devices, shards(): lax.all_to_all(total, ('z', 'x'), split_axis=0, concat_axis=0, tiled=True)  9.05 us
    all_to_all x1, starting transfers between devices, shards(): lax.all_to_all(total, ('z', 'x'), split_axis=0, concat_axis=0, tiled=True)  5.59 us
    pallas_call x9, Pallas kernels, pack(): pl.pallas_call(body, out_shape=jax.ShapeDtypeStruct(shape, BF), in_specs=...  4.29 us
  transfers between devices with their start and end apart: 46, of which 26 were waited for; matrix products, arithmetic and copies ran while one was open for 1% of the time, Pallas kernels for 12%

profile of v1, /device:TPU:1, one launch (start us, length us, event | category | flops | bytes accessed | tf_op | source)
XLA Modules:
  0.0 146.0 jit_solution(9395046738073910363)
XLA Ops:
  0.0 3.2 %collective-permute-start.2 = (bf16[48,5120]{1,0:T(8,128)(2,1)}, bf16[48,5120]{1,0:T(8,128)(2,1)S(1)}, u32[]{:S(2)}, u32[]{:S(2)}) collective-permute-start(bf16[48,5120]{1,0:T(8,128)(2,1)} %bitcast.10), channel_id=1, source_target_pairs={{0,128},{128,0},{1,129},{129,1},{2,130},{130,2},{3,131},{131,3},{4... | collective-permute-start | bytes 1474568 | tf_op jit(solution)/shard_map/ppermute | solution.py:25
  3.9 2.7 %shard_map.100 = (bf16[16,5120]{1,0:T(8,128)(2,1)}, bf16[16,5120]{1,0:T(8,128)(2,1)}, bf16[64,768]{1,0:T(8,128)(2,1)}) custom-call(s32[4]{0:T(128)} %pad_add_fusion.where, bf16[32,5120]{1,0:T(8,128)(2,1)} %large.1, bf16[32,1536]{1,0:T(8,128)(2,1)} %small.1, f32[5120]{0:T(1024)} %gain_l.1, f32[1536]{0:T(1024)} %gain_s.1), custom_call_target="tpu_custom_call" | custom-call | bytes 1048576 | tf_op jit(solution)/shard_map/pallas_call | solution.py:54
  8.3 2.3 %collective-permute-start.7 = (bf16[96,5120]{1,0:T(8,128)(2,1)S(1)}, bf16[96,5120]{1,0:T(8,128)(2,1)S(1)}, u32[]{:S(2)}, u32[]{:S(2)}) collective-permute-start(bf16[96,5120]{1,0:T(8,128)(2,1)S(1)} %shard_map.101.w0), channel_id=1, source_target_pairs={{0,1},{1,2},{2,3},{3,0},{128,131},{129,128},{130,129},{131,130},{4... | collective-permute-start | bytes 2949128 | tf_op jit(solution)/shard_map/ppermute | solution.py:40
  10.6 1.8 %collective-permute-start = (bf16[16,5120]{1,0:T(8,128)(2,1)S(1)}, bf16[16,5120]{1,0:T(8,128)(2,1)S(1)}, u32[]{:S(2)}, u32[]{:S(2)}) collective-permute-start(bf16[16,5120]{1,0:T(8,128)(2,1)S(1)} %copy-done.5), channel_id=1, source_target_pairs={{0,12},{12,0},{4,8},{8,4},{1,13},{13,1},{5,9},{9,5},{2,14},{14,2},... | collective-permute-start | bytes 491528 | tf_op jit(solution)/shard_map/ppermute | solution.py:33
  12.4 5.6 %collective-permute-start.1 = (bf16[64,768]{1,0:T(8,128)(2,1)S(1)}, bf16[64,768]{1,0:T(8,128)(2,1)S(1)}, u32[]{:S(2)}, u32[]{:S(2)}) collective-permute-start(bf16[64,768]{1,0:T(8,128)(2,1)S(1)} %copy-done.6), channel_id=1, source_target_pairs={{0,16},{16,32},{32,48},{48,64},{64,80},{80,96},{96,112},{112,0},{1... | collective-permute-start | bytes 294920 | tf_op jit(solution)/shard_map/ppermute | solution.py:40
  18.0 1.9 %collective-permute-start.3 = (bf16[48,512]{1,0:T(8,128)(2,1)S(1)}, bf16[48,512]{1,0:T(8,128)(2,1)S(1)}, u32[]{:S(2)}, u32[]{:S(2)}) collective-permute-start(bf16[48,512]{1,0:T(8,128)(2,1)S(1)} %pad_maximum_fusion.3), channel_id=1, source_target_pairs={{16,128},{48,160},{80,192},{112,224},{128,16},{160,48},{192,80},{2... | collective-permute-start | bytes 147464 | tf_op jit(solution)/shard_map/ppermute | solution.py:348
  20.0 3.5 %collective-permute-done.3 = bf16[48,512]{1,0:T(8,128)(2,1)S(1)} collective-permute-done((bf16[48,512]{1,0:T(8,128)(2,1)S(1)}, bf16[48,512]{1,0:T(8,128)(2,1)S(1)}, u32[]{:S(2)}, u32[]{:S(2)}) %collective-permute-start.3) | collective-permute-done | bytes 49184 | tf_op jit(solution)/shard_map/ppermute | solution.py:348
  31.6 2.5 %collective-permute-start.12 = (bf16[96,5120]{1,0:T(8,128)(2,1)S(1)}, bf16[96,5120]{1,0:T(8,128)(2,1)S(1)}, u32[]{:S(2)}, u32[]{:S(2)}) collective-permute-start(bf16[96,5120]{1,0:T(8,128)(2,1)S(1)} %collective-permute-done.7.refs_0_.y1), channel_id=1, source_target_pairs={{0,128},{128,0},{1,129},{129,1},{2,130},{130,2},{3,131},{131,3},{4... | collective-permute-start | bytes 2949128 | tf_op jit(solution)/shard_map/ppermute | solution.py:25
  35.5 4.0 %collective-permute-done.14 = bf16[48,1024]{1,0:T(8,128)(2,1)S(1)} collective-permute-done((bf16[48,1024]{1,0:T(8,128)(2,1)S(1)}, bf16[48,1024]{1,0:T(8,128)(2,1)S(1)}, u32[]{:S(2)}, u32[]{:S(2)}) %collective-permute-start.14) | collective-permute-done | bytes 98336 | tf_op jit(solution)/shard_map/ppermute | solution.py:25
  42.3 4.0 %collective-permute-done.11.refs_1_.b1 = bf16[32,5888]{1,0:T(8,128)(2,1)S(1)} collective-permute-done((bf16[32,5888]{1,0:T(8,128)(2,1)S(1)}, bf16[32,5888]{1,0:T(8,128)(2,1)S(1)}, u32[]{:S(2)}, u32[]{:S(2)}) %collective-permute-start.11) | collective-permute-done | bytes 376864 | tf_op jit(solution)/shard_map/ppermute | solution.py:40
  47.6 2.0 %collective-permute-start.22 = (bf16[48,14336]{1,0:T(8,128)(2,1)S(1)}, bf16[48,14336]{1,0:T(8,128)(2,1)S(1)}, u32[]{:S(2)}, u32[]{:S(2)}) collective-permute-start(bf16[48,14336]{1,0:T(8,128)(2,1)S(1)} %shard_map.106), channel_id=1, source_target_pairs={{0,1},{1,2},{2,3},{3,0},{128,131},{129,128},{130,129},{131,130},{4... | collective-permute-start | bytes 4128776 | tf_op jit(solution)/shard_map/ppermute | solution.py:40
  50.6 6.2 %collective-permute-done.17.a3 = bf16[32,5888]{1,0:T(8,128)(2,1)S(1)} collective-permute-done((bf16[32,5888]{1,0:T(8,128)(2,1)S(1)}, bf16[32,5888]{1,0:T(8,128)(2,1)S(1)}, u32[]{:S(2)}, u32[]{:S(2)}) %collective-permute-start.17) | collective-permute-done | bytes 376864 | tf_op jit(solution)/shard_map/ppermute | solution.py:40
  56.8 4.0 %collective-permute-done.18.refs_2_.b2 = bf16[32,5888]{1,0:T(8,128)(2,1)S(1)} collective-permute-done((bf16[32,5888]{1,0:T(8,128)(2,1)S(1)}, bf16[32,5888]{1,0:T(8,128)(2,1)S(1)}, u32[]{:S(2)}, u32[]{:S(2)}) %collective-permute-start.18) | collective-permute-done | bytes 376864 | tf_op jit(solution)/shard_map/ppermute | solution.py:40
  64.3 3.3 %collective-permute-done.20.a4 = bf16[32,5888]{1,0:T(8,128)(2,1)S(1)} collective-permute-done((bf16[32,5888]{1,0:T(8,128)(2,1)S(1)}, bf16[32,5888]{1,0:T(8,128)(2,1)S(1)}, u32[]{:S(2)}, u32[]{:S(2)}) %collective-permute-start.20) | collective-permute-done | bytes 376864 | tf_op jit(solution)/shard_map/ppermute | solution.py:40
  67.6 4.0 %collective-permute-done.21.b3 = bf16[32,5888]{1,0:T(8,128)(2,1)S(1)} collective-permute-done((bf16[32,5888]{1,0:T(8,128)(2,1)S(1)}, bf16[32,5888]{1,0:T(8,128)(2,1)S(1)}, u32[]{:S(2)}, u32[]{:S(2)}) %collective-permute-start.21) | collective-permute-done | bytes 376864 | tf_op jit(solution)/shard_map/ppermute | solution.py:40
  71.6 4.3 %collective-permute-start.24 = (bf16[48,14336]{1,0:T(8,128)(2,1)S(1)}, bf16[48,14336]{1,0:T(8,128)(2,1)S(1)}, u32[]{:S(2)}, u32[]{:S(2)}) collective-permute-start(bf16[48,14336]{1,0:T(8,128)(2,1)S(1)} %collective-permute-done.22.refs_0_.far.yz), channel_id=1, source_target_pairs={{0,128},{128,0},{1,129},{129,1},{2,130},{130,2},{3,131},{131,3},{4... | collective-permute-start | bytes 4128776 | tf_op jit(solution)/shard_map/ppermute | solution.py:25
  76.0 2.6 %collective-permute-start.25 = (bf16[48,2048]{1,0:T(8,128)(2,1)S(1)}, bf16[48,2048]{1,0:T(8,128)(2,1)S(1)}, u32[]{:S(2)}, u32[]{:S(2)}) collective-permute-start(bf16[48,2048]{1,0:T(8,128)(2,1)S(1)} %shard_map.108), channel_id=1, source_target_pairs={{0,1},{1,2},{2,3},{3,0},{128,131},{129,128},{130,129},{131,130},{4... | collective-permute-start | bytes 589832 | tf_op jit(solution)/shard_map/ppermute | solution.py:40
  78.7 4.2 %shard_map.109 = (bf16[256,384]{1,0:T(8,128)(2,1)S(1)}, bf16[256,384]{1,0:T(8,128)(2,1)S(1)}) custom-call(s32[4]{0:T(128)S(1)} %copy-done.9, bf16[32,5888]{1,0:T(8,128)(2,1)} %shard_map.102.near, bf16[32,5888]{1,0:T(8,128)(2,1)} %collective-permute-done.4.a1, bf16[32,5888]{1,0:T(8,128)(2,1)S(1)} %collective-permute-done.10.a2, ...), custom_call_target="tpu_custom_call" | custom-call | flops 4294967296 | bytes 1048576 | tf_op jit(solution)/shard_map/pallas_call | solution.py:54
  84.5 1.9 %shard_map.110 = (bf16[128,128]{1,0:T(8,128)(2,1)S(1)}, bf16[128,256]{1,0:T(8,128)(2,1)S(1)}) custom-call(s32[4]{0:T(128)S(1)} %copy-done.9, bf16[64,768]{1,0:T(8,128)(2,1)S(1)} %copy-done.7, bf16[64,768]{1,0:T(8,128)(2,1)S(1)} %collective-permute-done.1.refs_2_.refs_0_.s1, bf16[32,5888]{1,0:T(8,128)(2,1)} %collective-permute-done.4.a1, ...), custom_call_target="tpu_custom_call" | custom-call | flops 536870912 | bytes 1048576 | tf_op jit(solution)/shard_map/pallas_call | solution.py:54
  87.0 2.8 %collective-permute-done.27.refs_1_.taken = bf16[256,384]{1,0:T(8,128)(2,1)S(1)} collective-permute-done((bf16[256,384]{1,0:T(8,128)(2,1)S(1)}, bf16[256,384]{1,0:T(8,128)(2,1)S(1)}, u32[]{:S(2)}, u32[]{:S(2)}) %collective-permute-start.27) | collective-permute-done | bytes 196640 | tf_op jit(solution)/shard_map/ppermute | solution.py:25
  91.9 2.6 %collective-permute-start.31 = (bf16[1024,256]{1,0:T(8,128)(2,1)S(1)}, bf16[1024,256]{1,0:T(8,128)(2,1)S(1)}, u32[]{:S(2)}, u32[]{:S(2)}) collective-permute-start(bf16[1024,256]{1,0:T(8,128)(2,1)S(1)} %shard_map.111.own), channel_id=1, source_target_pairs={{0,1},{1,2},{2,3},{3,0},{128,131},{129,128},{130,129},{131,130},{4... | collective-permute-start | bytes 1572872 | tf_op jit(solution)/shard_map/ppermute | solution.py:40
  96.9 2.3 %collective-permute-done.32.refs_1_.refs_5_ = bf16[256,256]{1,0:T(8,128)(2,1)S(1)} collective-permute-done((bf16[256,256]{1,0:T(8,128)(2,1)S(1)}, bf16[256,256]{1,0:T(8,128)(2,1)S(1)}, u32[]{:S(2)}, u32[]{:S(2)}) %collective-permute-start.32) | collective-permute-done | bytes 131104 | tf_op jit(solution)/shard_map/ppermute | solution.py:40
  102.3 2.7 %collective-permute-start.38 = (bf16[1024,256]{1,0:T(8,128)(2,1)S(1)}, bf16[1024,256]{1,0:T(8,128)(2,1)S(1)}, u32[]{:S(2)}, u32[]{:S(2)}) collective-permute-start(bf16[1024,256]{1,0:T(8,128)(2,1)S(1)} %shard_map.112.own), channel_id=1, source_target_pairs={{0,1},{1,2},{2,3},{3,0},{128,131},{129,128},{130,129},{131,130},{4... | collective-permute-start | bytes 1572872 | tf_op jit(solution)/shard_map/ppermute | solution.py:40
  105.8 5.4 %collective-permute-done.38.side = bf16[1024,256]{1,0:T(8,128)(2,1)S(1)} collective-permute-done((bf16[1024,256]{1,0:T(8,128)(2,1)S(1)}, bf16[1024,256]{1,0:T(8,128)(2,1)S(1)}, u32[]{:S(2)}, u32[]{:S(2)}) %collective-permute-start.38) | collective-permute-done | bytes 524320 | tf_op jit(solution)/shard_map/ppermute | solution.py:40
  111.2 2.8 %collective-permute-done.37.far = bf16[512,256]{1,0:T(8,128)(2,1)S(1)} collective-permute-done((bf16[512,256]{1,0:T(8,128)(2,1)S(1)}, bf16[512,256]{1,0:T(8,128)(2,1)S(1)}, u32[]{:S(2)}, u32[]{:S(2)}) %collective-permute-start.37) | collective-permute-done | bytes 262176 | tf_op jit(solution)/shard_map/ppermute | solution.py:40
  114.0 1.7 %collective-permute-start.39 = (bf16[512,256]{1,0:T(8,128)(2,1)S(1)}, bf16[512,256]{1,0:T(8,128)(2,1)S(1)}, u32[]{:S(2)}, u32[]{:S(2)}) collective-permute-start(bf16[512,256]{1,0:T(8,128)(2,1)S(1)} %collective-permute-done.37.far), channel_id=1, source_target_pairs={{0,128},{128,0},{1,129},{129,1},{2,130},{130,2},{3,131},{131,3},{4... | collective-permute-start | bytes 786440 | tf_op jit(solution)/shard_map/ppermute | solution.py:25
  117.2 4.6 %shard_map.113 = (f32[32,8,128]{2,1,0:T(8,128)S(1)}, f32[32,8,128]{2,1,0:T(8,128)S(1)}) custom-call(s32[4]{0:T(128)S(1)} %copy-done.9, bf16[256,384]{1,0:T(8,128)(2,1)S(1)} %get-tuple-element.96.refs_0_.kept, bf16[256,384]{1,0:T(8,128)(2,1)S(1)} %collective-permute-done.27.refs_1_.taken, bf16[128,128]{1,0:T(8,128)(2,1)S(1)} %get-tuple-element.74.maps, ...), custom_call_target="tpu_custom_call" | custom-call | flops 4294967296 | bytes 1048576 | tf_op jit(solution)/shard_map/pallas_call | solution.py:54
  121.8 1.6 %collective-permute-start.43 = (bf16[512,256]{1,0:T(8,128)(2,1)S(1)}, bf16[512,256]{1,0:T(8,128)(2,1)S(1)}, u32[]{:S(2)}, u32[]{:S(2)}) collective-permute-start(bf16[512,256]{1,0:T(8,128)(2,1)S(1)} %collective-permute-done.40.far), channel_id=1, source_target_pairs={{0,128},{128,0},{1,129},{129,1},{2,130},{130,2},{3,131},{131,3},{4... | collective-permute-start | bytes 786440 | tf_op jit(solution)/shard_map/ppermute | solution.py:25
  124.8 2.4 %shard_map.114 = f32[32,8,128]{2,1,0:T(8,128)} custom-call(s32[4]{0:T(128)S(1)} %copy-done.9, bf16[128,128]{1,0:T(8,128)(2,1)S(1)} %get-tuple-element.94.query, bf16[128,128]{1,0:T(8,128)(2,1)S(1)} %get-tuple-element.74.maps, bf16[128,128]{1,0:T(8,128)(2,1)S(1)} %collective-permute-done.16.maps_g, f32[32,8,128]{2,1,0:T(8,128)S(1)} %get-tuple-element.104.keep, ...), custom_call_target="tpu_custom_call" | custom-call | flops 1073741824 | bytes 1048576 | tf_op jit(solution)/shard_map/pallas_call | solution.py:54
  127.2 5.6 %all-to-all-start = ((f32[32,8,128]{2,1,0:T(8,128)}), f32[32,8,128]{2,1,0:T(8,128)S(1)}, u32[]{:S(2)}, u32[]{:S(2)}) async-start(f32[32,8,128]{2,1,0:T(8,128)} %shard_map.114), calls=%async_computation | async-start | bytes 262144 | tf_op jit(solution)/shard_map/all_to_all | solution.py:483
  133.1 9.1 %all-to-all-done = f32[32,8,128]{2,1,0:T(8,128)S(1)} async-done(((f32[32,8,128]{2,1,0:T(8,128)}), f32[32,8,128]{2,1,0:T(8,128)S(1)}, u32[]{:S(2)}, u32[]{:S(2)}) %all-to-all-start) | async-done | bytes 131104 | tf_op jit(solution)/shard_map/all_to_all | solution.py:483
  142.4 2.1 %collective-permute-start.44 = (f32[16,64]{1,0:T(8,128)S(1)}, f32[16,64]{1,0:T(8,128)S(1)}, u32[]{:S(2)}, u32[]{:S(2)}) collective-permute-start(f32[16,64]{1,0:T(8,128)S(1)} %fusion.1), channel_id=1, source_target_pairs={{0,128},{128,0},{1,129},{129,1},{2,130},{130,2},{3,131},{131,3},{4... | collective-permute-start | bytes 12296 | tf_op jit(solution)/shard_map/ppermute | solution.py:25
  (125 shorter events, 35.8 us)
Async XLA Ops:
  0.0 6.6 %collective-permute-start.2 = (bf16[48,5120]{1,0:T(8,128)(2,1)}, bf16[48,5120]{1,0:T(8,128)(2,1)S(1)}, u32[]{:S(2)}, u32[]{:S(2)}) collective-permute-start(bf16[48,5120]{1,0:T(8,128)(2,1)} %bitcast.10), channel_id=1, source_target_pairs={{0,128},{128,0},{1,129},{129,1},{2,130},{130,2},{3,131},{131,3},{4... | collective-permute-start | bytes 1474568 | tf_op jit(solution)/shard_map/ppermute | solution.py:25
  3.2 21.1 %collective-permute-start.5 = (bf16[48,5120]{1,0:T(8,128)(2,1)}, bf16[48,5120]{1,0:T(8,128)(2,1)S(1)}, u32[]{:S(2)}, u32[]{:S(2)}) collective-permute-start(bf16[48,5120]{1,0:T(8,128)(2,1)} %bitcast.11), channel_id=1, source_target_pairs={{0,4},{4,0},{8,12},{12,8},{1,5},{5,1},{9,13},{13,9},{2,6},{6,2},{1... | collective-permute-start | bytes 1474568 | tf_op jit(solution)/shard_map/ppermute | solution.py:25
  8.3 23.3 %collective-permute-start.7 = (bf16[96,5120]{1,0:T(8,128)(2,1)S(1)}, bf16[96,5120]{1,0:T(8,128)(2,1)S(1)}, u32[]{:S(2)}, u32[]{:S(2)}) collective-permute-start(bf16[96,5120]{1,0:T(8,128)(2,1)S(1)} %shard_map.101.w0), channel_id=1, source_target_pairs={{0,1},{1,2},{2,3},{3,0},{128,131},{129,128},{130,129},{131,130},{4... | collective-permute-start | bytes 2949128 | tf_op jit(solution)/shard_map/ppermute | solution.py:40
  10.6 12.9 %collective-permute-start = (bf16[16,5120]{1,0:T(8,128)(2,1)S(1)}, bf16[16,5120]{1,0:T(8,128)(2,1)S(1)}, u32[]{:S(2)}, u32[]{:S(2)}) collective-permute-start(bf16[16,5120]{1,0:T(8,128)(2,1)S(1)} %copy-done.5), channel_id=1, source_target_pairs={{0,12},{12,0},{4,8},{8,4},{1,13},{13,1},{5,9},{9,5},{2,14},{14,2},... | collective-permute-start | bytes 491528 | tf_op jit(solution)/shard_map/ppermute | solution.py:33
  12.4 11.1 %collective-permute-start.1 = (bf16[64,768]{1,0:T(8,128)(2,1)S(1)}, bf16[64,768]{1,0:T(8,128)(2,1)S(1)}, u32[]{:S(2)}, u32[]{:S(2)}) collective-permute-start(bf16[64,768]{1,0:T(8,128)(2,1)S(1)} %copy-done.6), channel_id=1, source_target_pairs={{0,16},{16,32},{32,48},{48,64},{64,80},{80,96},{96,112},{112,0},{1... | collective-permute-start | bytes 294920 | tf_op jit(solution)/shard_map/ppermute | solution.py:40
  18.0 5.4 %collective-permute-start.3 = (bf16[48,512]{1,0:T(8,128)(2,1)S(1)}, bf16[48,512]{1,0:T(8,128)(2,1)S(1)}, u32[]{:S(2)}, u32[]{:S(2)}) collective-permute-start(bf16[48,512]{1,0:T(8,128)(2,1)S(1)} %pad_maximum_fusion.3), channel_id=1, source_target_pairs={{16,128},{48,160},{80,192},{112,224},{128,16},{160,48},{192,80},{2... | collective-permute-start | bytes 147464 | tf_op jit(solution)/shard_map/ppermute | solution.py:348
  24.3 4.8 %collective-permute-start.8 = (bf16[48,5120]{1,0:T(8,128)(2,1)S(1)}, bf16[48,5120]{1,0:T(8,128)(2,1)}, u32[]{:S(2)}, u32[]{:S(2)}) collective-permute-start(bf16[48,5120]{1,0:T(8,128)(2,1)S(1)} %collective-permute-done.5.refs_0_), channel_id=1, source_target_pairs={{0,128},{128,0},{1,129},{129,1},{2,130},{130,2},{3,131},{131,3},{4... | collective-permute-start | bytes 1474568 | tf_op jit(solution)/shard_map/ppermute | solution.py:25
  24.5 7.1 %collective-permute-start.4 = (bf16[32,5888]{1,0:T(8,128)(2,1)}, bf16[32,5888]{1,0:T(8,128)(2,1)}, u32[]{:S(2)}, u32[]{:S(2)}) collective-permute-start(bf16[32,5888]{1,0:T(8,128)(2,1)} %shard_map.102.near), channel_id=1, source_target_pairs={{0,16},{16,32},{32,48},{48,64},{64,80},{80,96},{96,112},{112,0},{1... | collective-permute-start | bytes 1130504 | tf_op jit(solution)/shard_map/ppermute | solution.py:40
  25.9 4.8 %collective-permute-start.9 = (bf16[48,512]{1,0:T(8,128)(2,1)S(1)}, bf16[48,512]{1,0:T(8,128)(2,1)S(1)}, u32[]{:S(2)}, u32[]{:S(2)}) collective-permute-start(bf16[48,512]{1,0:T(8,128)(2,1)S(1)} %broadcast_select_fusion), channel_id=1, source_target_pairs={{0,12},{12,0},{4,8},{8,4},{1,13},{13,1},{5,9},{9,5},{2,14},{14,2},... | collective-permute-start | bytes 147464 | tf_op jit(solution)/shard_map/ppermute | solution.py:33
  31.6 14.7 %collective-permute-start.12 = (bf16[96,5120]{1,0:T(8,128)(2,1)S(1)}, bf16[96,5120]{1,0:T(8,128)(2,1)S(1)}, u32[]{:S(2)}, u32[]{:S(2)}) collective-permute-start(bf16[96,5120]{1,0:T(8,128)(2,1)S(1)} %collective-permute-done.7.refs_0_.y1), channel_id=1, source_target_pairs={{0,128},{128,0},{1,129},{129,1},{2,130},{130,2},{3,131},{131,3},{4... | collective-permute-start | bytes 2949128 | tf_op jit(solution)/shard_map/ppermute | solution.py:25
  34.1 13.2 %collective-permute-start.13 = (bf16[96,5120]{1,0:T(8,128)(2,1)S(1)}, bf16[96,5120]{1,0:T(8,128)(2,1)S(1)}, u32[]{:S(2)}, u32[]{:S(2)}) collective-permute-start(bf16[96,5120]{1,0:T(8,128)(2,1)S(1)} %shard_map.104.pr), channel_id=1, source_target_pairs={{0,1},{1,2},{2,3},{3,0},{128,131},{129,128},{130,129},{131,130},{4... | collective-permute-start | bytes 2949128 | tf_op jit(solution)/shard_map/ppermute | solution.py:40
  34.9 4.6 %collective-permute-start.14 = (bf16[48,1024]{1,0:T(8,128)(2,1)S(1)}, bf16[48,1024]{1,0:T(8,128)(2,1)S(1)}, u32[]{:S(2)}, u32[]{:S(2)}) collective-permute-start(bf16[48,1024]{1,0:T(8,128)(2,1)S(1)} %pad_maximum_fusion.2), channel_id=1, source_target_pairs={{0,4},{4,0},{8,12},{12,8},{1,5},{5,1},{9,13},{13,9},{2,6},{6,2},{1... | collective-permute-start | bytes 294920 | tf_op jit(solution)/shard_map/ppermute | solution.py:25
  35.3 7.0 %collective-permute-start.10 = (bf16[32,5888]{1,0:T(8,128)(2,1)}, bf16[32,5888]{1,0:T(8,128)(2,1)S(1)}, u32[]{:S(2)}, u32[]{:S(2)}) collective-permute-start(bf16[32,5888]{1,0:T(8,128)(2,1)} %collective-permute-done.4.a1), channel_id=1, source_target_pairs={{0,16},{16,32},{32,48},{48,64},{64,80},{80,96},{96,112},{112,0},{1... | collective-permute-start | bytes 1130504 | tf_op jit(solution)/shard_map/ppermute | solution.py:40
  35.3 11.0 %collective-permute-start.11 = (bf16[32,5888]{1,0:T(8,128)(2,1)S(1)}, bf16[32,5888]{1,0:T(8,128)(2,1)S(1)}, u32[]{:S(2)}, u32[]{:S(2)}) collective-permute-start(bf16[32,5888]{1,0:T(8,128)(2,1)S(1)} %shard_map.103), channel_id=1, source_target_pairs={{0,16},{16,32},{32,48},{48,64},{64,80},{80,96},{96,112},{112,0},{1... | collective-permute-start | bytes 1130504 | tf_op jit(solution)/shard_map/ppermute | solution.py:40
  47.6 24.0 %collective-permute-start.22 = (bf16[48,14336]{1,0:T(8,128)(2,1)S(1)}, bf16[48,14336]{1,0:T(8,128)(2,1)S(1)}, u32[]{:S(2)}, u32[]{:S(2)}) collective-permute-start(bf16[48,14336]{1,0:T(8,128)(2,1)S(1)} %shard_map.106), channel_id=1, source_target_pairs={{0,1},{1,2},{2,3},{3,0},{128,131},{129,128},{130,129},{131,130},{4... | collective-permute-start | bytes 4128776 | tf_op jit(solution)/shard_map/ppermute | solution.py:40
  49.7 11.2 %collective-permute-start.19 = (bf16[96,5120]{1,0:T(8,128)(2,1)S(1)}, bf16[96,5120]{1,0:T(8,128)(2,1)S(1)}, u32[]{:S(2)}, u32[]{:S(2)}) collective-permute-start(bf16[96,5120]{1,0:T(8,128)(2,1)S(1)} %collective-permute-done.13.refs_1_.y2), channel_id=1, source_target_pairs={{0,128},{128,0},{1,129},{129,1},{2,130},{130,2},{3,131},{131,3},{4... | collective-permute-start | bytes 2949128 | tf_op jit(solution)/shard_map/ppermute | solution.py:25
  50.1 6.7 %collective-permute-start.17 = (bf16[32,5888]{1,0:T(8,128)(2,1)S(1)}, bf16[32,5888]{1,0:T(8,128)(2,1)S(1)}, u32[]{:S(2)}, u32[]{:S(2)}) collective-permute-start(bf16[32,5888]{1,0:T(8,128)(2,1)S(1)} %collective-permute-done.10.a2), channel_id=1, source_target_pairs={{0,16},{16,32},{32,48},{48,64},{64,80},{80,96},{96,112},{112,0},{1... | collective-permute-start | bytes 1130504 | tf_op jit(solution)/shard_map/ppermute | solution.py:40
  50.2 10.6 %collective-permute-start.18 = (bf16[32,5888]{1,0:T(8,128)(2,1)S(1)}, bf16[32,5888]{1,0:T(8,128)(2,1)S(1)}, u32[]{:S(2)}, u32[]{:S(2)}) collective-permute-start(bf16[32,5888]{1,0:T(8,128)(2,1)S(1)} %collective-permute-done.11.refs_1_.b1), channel_id=1, source_target_pairs={{0,16},{16,32},{32,48},{48,64},{64,80},{80,96},{96,112},{112,0},{1... | collective-permute-start | bytes 1130504 | tf_op jit(solution)/shard_map/ppermute | solution.py:40
  60.9 6.7 %collective-permute-start.20 = (bf16[32,5888]{1,0:T(8,128)(2,1)S(1)}, bf16[32,5888]{1,0:T(8,128)(2,1)S(1)}, u32[]{:S(2)}, u32[]{:S(2)}) collective-permute-start(bf16[32,5888]{1,0:T(8,128)(2,1)S(1)} %collective-permute-done.17.a3), channel_id=1, source_target_pairs={{0,16},{16,32},{32,48},{48,64},{64,80},{80,96},{96,112},{112,0},{1... | collective-permute-start | bytes 1130504 | tf_op jit(solution)/shard_map/ppermute | solution.py:40
  62.2 9.4 %collective-permute-start.21 = (bf16[32,5888]{1,0:T(8,128)(2,1)S(1)}, bf16[32,5888]{1,0:T(8,128)(2,1)S(1)}, u32[]{:S(2)}, u32[]{:S(2)}) collective-permute-start(bf16[32,5888]{1,0:T(8,128)(2,1)S(1)} %collective-permute-done.18.refs_2_.b2), channel_id=1, source_target_pairs={{0,16},{16,32},{32,48},{48,64},{64,80},{80,96},{96,112},{112,0},{1... | collective-permute-start | bytes 1130504 | tf_op jit(solution)/shard_map/ppermute | solution.py:40
  71.6 7.0 %collective-permute-start.24 = (bf16[48,14336]{1,0:T(8,128)(2,1)S(1)}, bf16[48,14336]{1,0:T(8,128)(2,1)S(1)}, u32[]{:S(2)}, u32[]{:S(2)}) collective-permute-start(bf16[48,14336]{1,0:T(8,128)(2,1)S(1)} %collective-permute-done.22.refs_0_.far.yz), channel_id=1, source_target_pairs={{0,128},{128,0},{1,129},{129,1},{2,130},{130,2},{3,131},{131,3},{4... | collective-permute-start | bytes 4128776 | tf_op jit(solution)/shard_map/ppermute | solution.py:25
  76.0 7.0 %collective-permute-start.25 = (bf16[48,2048]{1,0:T(8,128)(2,1)S(1)}, bf16[48,2048]{1,0:T(8,128)(2,1)S(1)}, u32[]{:S(2)}, u32[]{:S(2)}) collective-permute-start(bf16[48,2048]{1,0:T(8,128)(2,1)S(1)} %shard_map.108), channel_id=1, source_target_pairs={{0,1},{1,2},{2,3},{3,0},{128,131},{129,128},{130,129},{131,130},{4... | collective-permute-start | bytes 589832 | tf_op jit(solution)/shard_map/ppermute | solution.py:40
  83.4 6.4 %collective-permute-start.27 = (bf16[256,384]{1,0:T(8,128)(2,1)S(1)}, bf16[256,384]{1,0:T(8,128)(2,1)S(1)}, u32[]{:S(2)}, u32[]{:S(2)}) collective-permute-start(bf16[256,384]{1,0:T(8,128)(2,1)S(1)} %get-tuple-element.91), channel_id=1, source_target_pairs={{0,4},{4,0},{8,12},{12,8},{1,5},{5,1},{9,13},{13,9},{2,6},{6,2},{1... | collective-permute-start | bytes 589832 | tf_op jit(solution)/shard_map/ppermute | solution.py:25
  91.9 13.1 %collective-permute-start.31 = (bf16[1024,256]{1,0:T(8,128)(2,1)S(1)}, bf16[1024,256]{1,0:T(8,128)(2,1)S(1)}, u32[]{:S(2)}, u32[]{:S(2)}) collective-permute-start(bf16[1024,256]{1,0:T(8,128)(2,1)S(1)} %shard_map.111.own), channel_id=1, source_target_pairs={{0,1},{1,2},{2,3},{3,0},{128,131},{129,128},{130,129},{131,130},{4... | collective-permute-start | bytes 1572872 | tf_op jit(solution)/shard_map/ppermute | solution.py:40
  94.5 4.7 %collective-permute-start.32 = (bf16[256,256]{1,0:T(8,128)(2,1)S(1)}, bf16[256,256]{1,0:T(8,128)(2,1)S(1)}, u32[]{:S(2)}, u32[]{:S(2)}) collective-permute-start(bf16[256,256]{1,0:T(8,128)(2,1)S(1)} %pad_maximum_fusion.1), channel_id=1, source_target_pairs={{0,4},{4,8},{8,12},{12,0},{128,140},{132,128},{136,132},{140,136},... | collective-permute-start | bytes 393224 | tf_op jit(solution)/shard_map/ppermute | solution.py:40
  95.7 4.6 %collective-permute-start.34 = (bf16[128,256]{1,0:T(8,128)(2,1)S(1)}, bf16[128,256]{1,0:T(8,128)(2,1)S(1)}, u32[]{:S(2)}, u32[]{:S(2)}) collective-permute-start(bf16[128,256]{1,0:T(8,128)(2,1)S(1)} %get-tuple-element.97.refs_0_), channel_id=1, source_target_pairs={{0,8},{4,12},{8,0},{12,4},{1,9},{5,13},{9,1},{13,5},{2,10},{6,14},... | collective-permute-start | bytes 196616 | tf_op jit(solution)/shard_map/ppermute | solution.py:25
  102.3 9.0 %collective-permute-start.38 = (bf16[1024,256]{1,0:T(8,128)(2,1)S(1)}, bf16[1024,256]{1,0:T(8,128)(2,1)S(1)}, u32[]{:S(2)}, u32[]{:S(2)}) collective-permute-start(bf16[1024,256]{1,0:T(8,128)(2,1)S(1)} %shard_map.112.own), channel_id=1, source_target_pairs={{0,1},{1,2},{2,3},{3,0},{128,131},{129,128},{130,129},{131,130},{4... | collective-permute-start | bytes 1572872 | tf_op jit(solution)/shard_map/ppermute | solution.py:40
  105.0 9.1 %collective-permute-start.37 = (bf16[512,256]{1,0:T(8,128)(2,1)S(1)}, bf16[512,256]{1,0:T(8,128)(2,1)S(1)}, u32[]{:S(2)}, u32[]{:S(2)}) collective-permute-start(bf16[512,256]{1,0:T(8,128)(2,1)S(1)} %slice.24), channel_id=1, source_target_pairs={{0,1},{1,2},{2,3},{3,0},{128,131},{129,128},{130,129},{131,130},{4... | collective-permute-start | bytes 786440 | tf_op jit(solution)/shard_map/ppermute | solution.py:40
  105.7 11.5 %collective-permute-start.36 = (bf16[1024,256]{1,0:T(8,128)(2,1)S(1)}, bf16[1024,256]{1,0:T(8,128)(2,1)S(1)}, u32[]{:S(2)}, u32[]{:S(2)}) collective-permute-start(bf16[1024,256]{1,0:T(8,128)(2,1)S(1)} %collective-permute-done.31.side), channel_id=1, source_target_pairs={{0,128},{128,0},{1,129},{129,1},{2,130},{130,2},{3,131},{131,3},{4... | collective-permute-start | bytes 1572872 | tf_op jit(solution)/shard_map/ppermute | solution.py:25
  115.7 6.1 %collective-permute-start.40 = (bf16[512,256]{1,0:T(8,128)(2,1)S(1)}, bf16[512,256]{1,0:T(8,128)(2,1)S(1)}, u32[]{:S(2)}, u32[]{:S(2)}) collective-permute-start(bf16[512,256]{1,0:T(8,128)(2,1)S(1)} %slice.28), channel_id=1, source_target_pairs={{0,1},{1,2},{2,3},{3,0},{128,131},{129,128},{130,129},{131,130},{4... | collective-permute-start | bytes 786440 | tf_op jit(solution)/shard_map/ppermute | solution.py:40
  117.2 6.2 %collective-permute-start.42 = (bf16[1024,256]{1,0:T(8,128)(2,1)S(1)}, bf16[1024,256]{1,0:T(8,128)(2,1)S(1)}, u32[]{:S(2)}, u32[]{:S(2)}) collective-permute-start(bf16[1024,256]{1,0:T(8,128)(2,1)S(1)} %collective-permute-done.38.side), channel_id=1, source_target_pairs={{0,128},{128,0},{1,129},{129,1},{2,130},{130,2},{3,131},{131,3},{4... | collective-permute-start | bytes 1572872 | tf_op jit(solution)/shard_map/ppermute | solution.py:25
  127.2 14.9 %all-to-all-start = ((f32[32,8,128]{2,1,0:T(8,128)}), f32[32,8,128]{2,1,0:T(8,128)S(1)}, u32[]{:S(2)}, u32[]{:S(2)}) async-start(f32[32,8,128]{2,1,0:T(8,128)} %shard_map.114), calls=%async_computation | async-start | bytes 262144 | tf_op jit(solution)/shard_map/all_to_all | solution.py:483
  (32 other events, 318.7 us)

commit v2 on v1

--- a/solution.py
+++ b/solution.py
@@ -154,7 +154,7 @@
 
 
 def project_small_body(
-    where, own, s1, a1, a2, a3, got, ws, ws_g, yz, yz_g, far, far_g, order, query, pairs, rows
+    where, own, s1, z1, z2, z3, got, ws, ws_g, yz, yz_g, far, far_g, order, query, pairs, rows
 ):
     core, z = where[0], where[1]
     way = 2 * core - 1
@@ -165,8 +165,8 @@
         rows[at, KS:] = ref[row + 16 : row + 32, col:]
 
     put(0, own, 0, 0)
-    put(4, a3, 0, DL)
-    for i, ref, col in ((1, s1, 0), (2, a1, DL), (3, a2, DL)):
+    put(4, z3, 0, DL)
+    for i, ref, col in ((1, s1, 0), (2, z1, DL), (3, z2, DL)):
         put(way * i, ref, 0, col)
         put(-way * i, got, 32 * i - 32, 0)
 
@@ -192,30 +192,41 @@
 
 
 def project_body(
-    where, near, a1, a2, a3, a4, b1, b2, b3, w0, y1, y1_g, pr, y2, y2_g, far, far_g,
-    order, kept, sent,
+    where, near, z1, z2, z3, z4, w0, y1, y1_g, yz, pr, y2, y2_g, own, other
 ):
-    core, x = where[0], where[2]
     blocks = (
-        (w0, 0, 0), (y1, 0, 0), (far, 0, 0), (y1_g, 48, 0),
-        (pr, 0, 0), (y2, 0, 0), (far, 0, DL), (y2_g, 48, 0),
-        (w0, 48, 0), (y1, 48, 0), (far_g, 0, 0), (y1_g, 0, 0),
-        (pr, 48, 0), (y2, 48, 0), (far_g, 0, DL), (y2_g, 0, 0),
-    )
+        (w0, 0, 0), (y1, 0, 0), (yz, 0, 0), (y1_g, 48, 0),
+        (pr, 0, 0), (y2, 0, 0), (yz, 0, DL), (y2_g, 48, 0),
+        (w0, 48, 0), (y1, 48, 0), (y1_g, 0, 0), (pr, 48, 0), (y2, 48, 0), (y2_g, 0, 0),
+    )
+    total = product(blocks, (near, z1, z2, z3, z4))
+    own[...] = total[:384, :]
+    other[...] = total[384:, :]
+
+
+def product(blocks, rows):
+    near, z1, z2, z3, z4 = rows
     total = None
     for k in range(0, DL, 1024):
         at = slice(k, k + 1024)
         cols = jnp.concatenate(
             [ref[row : row + 48, col + k : col + k + 1024] for ref, row, col in blocks], 0
         )
-        rows = jnp.concatenate([ref[:, at] for ref in (near, a1, b1, a2, b2, a3, b3, a4)], 0)
-        term = dot_t(cols, rows)
+        parts = [near[:, at], z1[:, at], z2[32:, at], z2[:32, at], z3[32:, at]]
+        parts += [z3[:32, at], z4[32:, at], z4[:32, at]]
+        term = dot_t(cols, jnp.concatenate(parts, 0))
         total = term if total is None else total + term
-    total = total.astype(BF)
-    own, other = total[:384, :], total[384:, :]
+    return total.astype(BF)
+
+
+def finish_body(where, near, z1, z2, z3, z4, yz_g, own, other, order, kept, sent):
+    core, x = where[0], where[2]
+    far = product(((yz_g, 0, 0), (yz_g, 0, DL)), (near, z1, z2, z3, z4))
+    parts = [other[0:96, :], far[:48, :], other[96:240, :], far[48:, :], other[240:, :]]
+    first, second = own[...], jnp.concatenate(parts, 0)
     mine = core == x % 2
-    sent[...] = ordered(jnp.where(mine, other, own), order)
-    kept[...] = ordered(jnp.where(mine, own, other), order)
+    sent[...] = ordered(jnp.where(mine, second, first), order)
+    kept[...] = ordered(jnp.where(mine, first, second), order)
 
 
 def attend(query, pairs, scores):
@@ -331,45 +342,42 @@
     xw = flip(w, "x", 1)
     across = cross(mine)
     s1 = spread(s0, "z")
-    ws, mix_l, mix_s, _ = tie(ws, mix_large.T, mix_small.T, mine)
+    w_g, ws, mix_l, mix_s, _ = tie(w_g, ws, mix_large.T, mix_small.T, mine)
     top, low, left, right = slice(0, 48), slice(48, 96), slice(0, DL), slice(DL, None)
     near, pair, every = slice(0, 16), slice(16, 32), slice(None)
+    ws = jnp.concatenate([ws, jnp.zeros((4, DS), BF)], 0)
+    ws = jnp.concatenate([ws[:, :PART], ws[:, PART : 2 * PART], ws[:, 2 * PART :]], 0)
+    trade = [(g * 8 + i, (1 - g) * 8 + (i ^ 1)) for g in range(2) for i in range(8) if i % 2 != g]
+    ws_other = lax.ppermute(ws, ("grp", "z"), trade)
+    w0 = pack((96, DL), [(w, None, top), (w_g, None, low)])
+    y1 = spread(w0, "y")
     order_l, order_s, maps = call(
         setup_body,
         [((384, 384), BF), ((512, 384), BF), ((HD, HD), BF)],
         (where, mix_l, mix_s),
     )
-    w_g, _ = tie(w_g, mine)
-    w0 = pack((96, DL), [(w, None, top), (w_g, None, low)])
-    y1 = spread(w0, "y")
-    ws = jnp.concatenate([ws, jnp.zeros((4, DS), BF)], 0)
-    ws = jnp.concatenate([ws[:, :PART], ws[:, PART : 2 * PART], ws[:, 2 * PART :]], 0)
-    trade = [(g * 8 + i, (1 - g) * 8 + (i ^ 1)) for g in range(2) for i in range(8) if i % 2 != g]
-    ws_other = lax.ppermute(ws, ("grp", "z"), trade)
 
     across, s1, w0, ws_other = tie(across, s1, w0, ws_other)
     ws = jnp.where(core == z_low, ws, ws_other)
     ws_cross = cross(ws)
 
-    def block(own, facing, small):
-        return pack(
-            (32, DL + KS),
-            [
-                (own, None, (near, left)),
-                (facing, None, (pair, left)),
-                (s1, small, (every, right)),
-            ],
-        )
-
-    a0 = block(mine, across, slice(0, 32))
-    a1 = spread(a0, "z")
+    def block(at, own, facing, small):
+        return [
+            (own, None, (slice(at, at + 16), left)),
+            (facing, None, (slice(at + 16, at + 32), left)),
+            (s1, small, (slice(at, at + 32), right)),
+        ]
+
+    a0 = pack((32, DL + KS), block(0, mine, across, slice(0, 32)))
+    z1 = spread(a0, "z")
     across, xw, _ = tie(across, xw, a0)
-    b0 = block(other, swap(across), slice(32, 64))
+    got = swap(across)
     pr = pack((96, DL), [(xw, None, top), (swap(xw), None, low)])
 
-    a1, b0, y1, pr, ws_cross, maps = tie(a1, b0, y1, pr, ws_cross, maps)
-    a2 = spread(a1, "z")
-    b1 = spread(b0, "z")
+    z1, y1, got, pr, ws_cross, maps = tie(z1, y1, got, pr, ws_cross, maps)
+    z2 = spread(
+        pack((64, DL + KS), [(z1, None, slice(0, 32))] + block(32, other, got, slice(32, 64))), "z"
+    )
     y2 = spread(pr, "y")
     ws2 = jnp.concatenate([ws, ws_cross], 1)
     ws4 = jnp.concatenate([ws2, flip(ws2, "x", 1)], 1)
@@ -377,9 +385,8 @@
     y1_g = swap(y1)
     maps_g = swap(maps)
 
-    a2, b1, y1, y1_g, y2, ws4, ws4_g, maps_g = tie(a2, b1, y1, y1_g, y2, ws4, ws4_g, maps_g)
-    a3 = spread(a2, "z")
-    b2 = spread(b1, "z")
+    z2, y1, y1_g, y2, ws4, ws4_g, maps_g = tie(z2, y1, y1_g, y2, ws4, ws4_g, maps_g)
+    z3 = spread(z2, "z")
     ends = [slice(DL, 2 * DL), slice(2 * DL, 2 * DL + 4 * PART), slice(2 * DL + 4 * PART, None)]
     yz = spread(
         pack(
@@ -391,30 +398,35 @@
     )
     y2_g = swap(y2)
 
-    a3, b2, y2_g = tie(a3, b2, y2_g)
-    a4 = spread(a3, "z")
-    b3 = spread(b2, "z")
+    z3, y2_g = tie(z3, y2_g)
+    z4 = spread(z3, "z")
     s_got = swap(
         pack(
             (96, KS),
             [
                 (s1, slice(32, 64), slice(0, 32)),
-                (b1, (every, right), slice(32, 64)),
-                (b2, (every, right), slice(64, 96)),
+                (z2, (slice(32, 64), right), slice(32, 64)),
+                (z3, (slice(32, 64), right), slice(64, 96)),
             ],
         )
     )
 
-    a4, b3, yz, s_got = tie(a4, b3, yz, s_got)
+    z4, yz, s_got = tie(z4, yz, s_got)
     far_s = spread(pack((48, 4 * PART), [(yz, (every, ends[1]), every)]), "y")
     yz_g = swap(yz)
-    kept, sent = call(
+    own, another = call(
         project_body,
-        [((256, 384), BF)] * 2,
-        (where, a0, a1, a2, a3, a4, b1, b2, b3)
-        + (w0, y1, y1_g, pr, y2, y2_g, yz, yz_g, order_l),
+        [((384, 256), BF), ((288, 256), BF)],
+        (where, a0, z1, z2, z3, z4, w0, y1, y1_g, yz, pr, y2, y2_g),
         limit=12,
         flops=2**32,
+    )
+    kept, sent = call(
+        finish_body,
+        [((256, 384), BF)] * 2,
+        (where, a0, z1, z2, z3, z4, yz_g, own, another, order_l),
+        limit=12,
+        flops=2**29,
     )
 
     taken = flip(sent, "x", 1)
@@ -424,7 +436,7 @@
     query_s, own_s = call(
         project_small_body,
         [((128, HD), BF), ((128, 2 * HD), BF)],
-        (where, s0, s1, a1, a2, a3, s_got, ws4, ws4_g, yz, yz_g, far_s, far_s_g, order_s),
+        (where, s0, s1, z1, z2, z3, s_got, ws4, ws4_g, yz, yz_g, far_s, far_s_g, order_s),
         [pltpu.VMEM((128, DS), BF)],
         limit=6,
         flops=2**29,

time: 146 us -> 143 us (0.979)
  waiting for transfers between devices: 63.2 us -> 61.1 us
    ppermute x25, starting transfers between devices: 22 us -> 26.9 us  [flip(): return lax.ppermute(block, axis, [(i, i ^ mask) for i in range(count)])]
    ppermute x17 -> x14, starting transfers between devices: 24.3 us -> 19.4 us  [spread(): return lax.ppermute(block, ('grp', axis), pairs)]
    ppermute x25, waiting for transfers between devices: 16.3 us -> 14.8 us  [flip(): return lax.ppermute(block, axis, [(i, i ^ mask) for i in range(count)])]
    ppermute x17 -> x14, waiting for transfers between devices: 34.2 us -> 33.5 us  [spread(): return lax.ppermute(block, ('grp', axis), pairs)]
    pallas_call x6 -> x7, Pallas kernels: 16.6 us -> 16.7 us  [call(): pl.pallas_call(body, out_shape=[jax.ShapeDtypeStruct(shape, dtype) for sh...]
  transfers between devices with their start and end apart: 46 -> 43, of which waited for: 26 -> 22; matrix products, arithmetic and copies ran while one was open for 1% -> 1% of each run, Pallas kernels for 12% -> 13%
where the time goes in v2:
time: 143 us
  waiting for transfers between devices  61.1 us (43%)
  starting transfers between devices  56 us (39%)
  Pallas kernels  20.4 us (14%)
  local copies, waits for them, and re-layouts  2.16 us (2%)
  other arithmetic  2.16 us (2%)
    ppermute x14, waiting for transfers between devices, spread(): return lax.ppermute(block, ('grp', axis), pairs)  33.5 us
    ppermute x25, starting transfers between devices, flip(): return lax.ppermute(block, axis, [(i, i ^ mask) for i in range(count)])  26.9 us
    ppermute x14, starting transfers between devices, spread(): return lax.ppermute(block, ('grp', axis), pairs)  19.4 us
    pallas_call x7, Pallas kernels, call(): pl.pallas_call(body, out_shape=[jax.ShapeDtypeStruct(shape, dtype) for sh...  16.7 us
    ppermute x25, waiting for transfers between devices, flip(): return lax.ppermute(block, axis, [(i, i ^ mask) for i in range(count)])  14.8 us
    all_to_all x1, waiting for transfers between devices, shards(): lax.all_to_all(total, ('z', 'x'), split_axis=0, concat_axis=0, tiled=True)  9.05 us
    all_to_all x1, starting transfers between devices, shards(): lax.all_to_all(total, ('z', 'x'), split_axis=0, concat_axis=0, tiled=True)  4.6 us
    pallas_call x9, Pallas kernels, pack(): pl.pallas_call(body, out_shape=jax.ShapeDtypeStruct(shape, BF), in_specs=...  3.72 us
  transfers between devices with their start and end apart: 43, of which 22 were waited for; matrix products, arithmetic and copies ran while one was open for 1% of the time, Pallas kernels for 13%

profile of v2, /device:TPU:1, one launch (start us, length us, event | category | flops | bytes accessed | tf_op | source)
XLA Modules:
  0.0 142.6 jit_solution(4371960456361982768)
XLA Ops:
  0.0 3.2 %collective-permute-start.2 = (bf16[48,5120]{1,0:T(8,128)(2,1)}, bf16[48,5120]{1,0:T(8,128)(2,1)S(1)}, u32[]{:S(2)}, u32[]{:S(2)}) collective-permute-start(bf16[48,5120]{1,0:T(8,128)(2,1)} %bitcast.10), channel_id=1, source_target_pairs={{0,128},{128,0},{1,129},{129,1},{2,130},{130,2},{3,131},{131,3},{4... | collective-permute-start | bytes 1474568 | tf_op jit(solution)/shard_map/ppermute | solution.py:25
  3.9 2.6 %shard_map.100 = (bf16[16,5120]{1,0:T(8,128)(2,1)}, bf16[16,5120]{1,0:T(8,128)(2,1)}, bf16[64,768]{1,0:T(8,128)(2,1)}) custom-call(s32[4]{0:T(128)} %pad_add_fusion.where, bf16[32,5120]{1,0:T(8,128)(2,1)} %large.1, bf16[32,1536]{1,0:T(8,128)(2,1)} %small.1, f32[5120]{0:T(1024)} %gain_l.1, f32[1536]{0:T(1024)} %gain_s.1), custom_call_target="tpu_custom_call" | custom-call | bytes 1048576 | tf_op jit(solution)/shard_map/pallas_call | solution.py:54
  8.3 2.3 %collective-permute-start.5 = (bf16[96,5120]{1,0:T(8,128)(2,1)S(1)}, bf16[96,5120]{1,0:T(8,128)(2,1)S(1)}, u32[]{:S(2)}, u32[]{:S(2)}) collective-permute-start(bf16[96,5120]{1,0:T(8,128)(2,1)S(1)} %shard_map.101.w0), channel_id=1, source_target_pairs={{0,1},{1,2},{2,3},{3,0},{128,131},{129,128},{130,129},{131,130},{4... | collective-permute-start | bytes 2949128 | tf_op jit(solution)/shard_map/ppermute | solution.py:40
  10.6 1.8 %collective-permute-start = (bf16[16,5120]{1,0:T(8,128)(2,1)S(1)}, bf16[16,5120]{1,0:T(8,128)(2,1)S(1)}, u32[]{:S(2)}, u32[]{:S(2)}) collective-permute-start(bf16[16,5120]{1,0:T(8,128)(2,1)S(1)} %copy-done.5), channel_id=1, source_target_pairs={{0,12},{12,0},{4,8},{8,4},{1,13},{13,1},{5,9},{9,5},{2,14},{14,2},... | collective-permute-start | bytes 491528 | tf_op jit(solution)/shard_map/ppermute | solution.py:33
  12.4 5.6 %collective-permute-start.1 = (bf16[64,768]{1,0:T(8,128)(2,1)S(1)}, bf16[64,768]{1,0:T(8,128)(2,1)S(1)}, u32[]{:S(2)}, u32[]{:S(2)}) collective-permute-start(bf16[64,768]{1,0:T(8,128)(2,1)S(1)} %copy-done.6), channel_id=1, source_target_pairs={{0,16},{16,32},{32,48},{48,64},{64,80},{80,96},{96,112},{112,0},{1... | collective-permute-start | bytes 294920 | tf_op jit(solution)/shard_map/ppermute | solution.py:40
  18.0 1.9 %collective-permute-start.3 = (bf16[48,512]{1,0:T(8,128)(2,1)S(1)}, bf16[48,512]{1,0:T(8,128)(2,1)}, u32[]{:S(2)}, u32[]{:S(2)}) collective-permute-start(bf16[48,512]{1,0:T(8,128)(2,1)S(1)} %pad_maximum_fusion.3), channel_id=1, source_target_pairs={{16,128},{48,160},{80,192},{112,224},{128,16},{160,48},{192,80},{2... | collective-permute-start | bytes 147464 | tf_op jit(solution)/shard_map/ppermute | solution.py:351
  20.0 3.6 %collective-permute-done.3 = bf16[48,512]{1,0:T(8,128)(2,1)} collective-permute-done((bf16[48,512]{1,0:T(8,128)(2,1)S(1)}, bf16[48,512]{1,0:T(8,128)(2,1)}, u32[]{:S(2)}, u32[]{:S(2)}) %collective-permute-start.3) | collective-permute-done | bytes 49184 | tf_op jit(solution)/shard_map/ppermute | solution.py:351
  30.8 2.5 %collective-permute-start.11 = (bf16[96,5120]{1,0:T(8,128)(2,1)S(1)}, bf16[96,5120]{1,0:T(8,128)(2,1)S(1)}, u32[]{:S(2)}, u32[]{:S(2)}) collective-permute-start(bf16[96,5120]{1,0:T(8,128)(2,1)S(1)} %collective-permute-done.5.refs_0_.y1), channel_id=1, source_target_pairs={{0,128},{128,0},{1,129},{129,1},{2,130},{130,2},{3,131},{131,3},{4... | collective-permute-start | bytes 2949128 | tf_op jit(solution)/shard_map/ppermute | solution.py:25
  35.0 4.2 %collective-permute-done.13 = bf16[48,1024]{1,0:T(8,128)(2,1)S(1)} collective-permute-done((bf16[48,1024]{1,0:T(8,128)(2,1)S(1)}, bf16[48,1024]{1,0:T(8,128)(2,1)S(1)}, u32[]{:S(2)}, u32[]{:S(2)}) %collective-permute-start.13) | collective-permute-done | bytes 98336 | tf_op jit(solution)/shard_map/ppermute | solution.py:25
  40.8 4.4 %collective-permute-done.10.refs_1_.z2 = bf16[64,5888]{1,0:T(8,128)(2,1)S(1)} collective-permute-done((bf16[64,5888]{1,0:T(8,128)(2,1)S(1)}, bf16[64,5888]{1,0:T(8,128)(2,1)S(1)}, u32[]{:S(2)}, u32[]{:S(2)}) %collective-permute-start.10) | collective-permute-done | bytes 753696 | tf_op jit(solution)/shard_map/ppermute | solution.py:40
  46.5 2.1 %collective-permute-start.17 = (bf16[96,5120]{1,0:T(8,128)(2,1)S(1)}, bf16[96,5120]{1,0:T(8,128)(2,1)S(1)}, u32[]{:S(2)}, u32[]{:S(2)}) collective-permute-start(bf16[96,5120]{1,0:T(8,128)(2,1)S(1)} %collective-permute-done.12.refs_1_.y2), channel_id=1, source_target_pairs={{0,128},{128,0},{1,129},{129,1},{2,130},{130,2},{3,131},{131,3},{4... | collective-permute-start | bytes 2949128 | tf_op jit(solution)/shard_map/ppermute | solution.py:25
  50.1 9.2 %collective-permute-done.16.refs_2_.z3 = bf16[64,5888]{1,0:T(8,128)(2,1)S(1)} collective-permute-done((bf16[64,5888]{1,0:T(8,128)(2,1)S(1)}, bf16[64,5888]{1,0:T(8,128)(2,1)S(1)}, u32[]{:S(2)}, u32[]{:S(2)}) %collective-permute-start.16) | collective-permute-done | bytes 753696 | tf_op jit(solution)/shard_map/ppermute | solution.py:40
  59.4 1.8 %collective-permute-start.18 = (bf16[64,5888]{1,0:T(8,128)(2,1)S(1)}, bf16[64,5888]{1,0:T(8,128)(2,1)S(1)}, u32[]{:S(2)}, u32[]{:S(2)}) collective-permute-start(bf16[64,5888]{1,0:T(8,128)(2,1)S(1)} %collective-permute-done.16.refs_2_.z3), channel_id=1, source_target_pairs={{0,16},{16,32},{32,48},{48,64},{64,80},{80,96},{96,112},{112,0},{1... | collective-permute-start | bytes 2261000 | tf_op jit(solution)/shard_map/ppermute | solution.py:40
  62.7 4.4 %collective-permute-done.19.refs_0_.yz = bf16[48,14336]{1,0:T(8,128)(2,1)S(1)} collective-permute-done((bf16[48,14336]{1,0:T(8,128)(2,1)S(1)}, bf16[48,14336]{1,0:T(8,128)(2,1)S(1)}, u32[]{:S(2)}, u32[]{:S(2)}) %collective-permute-start.19) | collective-permute-done | bytes 1376288 | tf_op jit(solution)/shard_map/ppermute | solution.py:40
  67.1 3.1 %collective-permute-done.18.z4 = bf16[64,5888]{1,0:T(8,128)(2,1)S(1)} collective-permute-done((bf16[64,5888]{1,0:T(8,128)(2,1)S(1)}, bf16[64,5888]{1,0:T(8,128)(2,1)S(1)}, u32[]{:S(2)}, u32[]{:S(2)}) %collective-permute-start.18) | collective-permute-done | bytes 753696 | tf_op jit(solution)/shard_map/ppermute | solution.py:40
  70.1 4.1 %collective-permute-start.21 = (bf16[48,14336]{1,0:T(8,128)(2,1)S(1)}, bf16[48,14336]{1,0:T(8,128)(2,1)S(1)}, u32[]{:S(2)}, u32[]{:S(2)}) collective-permute-start(bf16[48,14336]{1,0:T(8,128)(2,1)S(1)} %collective-permute-done.19.refs_0_.yz), channel_id=1, source_target_pairs={{0,128},{128,0},{1,129},{129,1},{2,130},{130,2},{3,131},{131,3},{4... | collective-permute-start | bytes 4128776 | tf_op jit(solution)/shard_map/ppermute | solution.py:25
  75.5 2.5 %shard_map.109 = (bf16[384,256]{1,0:T(8,128)(2,1)S(1)}, bf16[288,256]{1,0:T(8,128)(2,1)S(1)}) custom-call(s32[4]{0:T(128)S(1)} %copy-done.9, bf16[32,5888]{1,0:T(8,128)(2,1)S(1)} %shard_map.102.near, bf16[32,5888]{1,0:T(8,128)(2,1)S(1)} %collective-permute-done.4.refs_0_.z1, bf16[64,5888]{1,0:T(8,128)(2,1)S(1)} %collective-permute-done.10.refs_1_.z2, ...), custom_call_target="tpu_custom_call" | custom-call | flops 4294967296 | bytes 1048576 | tf_op jit(solution)/shard_map/pallas_call | solution.py:54
  78.0 2.3 %shard_map.110 = (bf16[256,384]{1,0:T(8,128)(2,1)S(1)}, bf16[256,384]{1,0:T(8,128)(2,1)S(1)}) custom-call(s32[4]{0:T(128)S(1)} %copy-done.9, bf16[32,5888]{1,0:T(8,128)(2,1)S(1)} %shard_map.102.near, bf16[32,5888]{1,0:T(8,128)(2,1)S(1)} %collective-permute-done.4.refs_0_.z1, bf16[64,5888]{1,0:T(8,128)(2,1)S(1)} %collective-permute-done.10.refs_1_.z2, ...), custom_call_target="tpu_custom_call" | custom-call | flops 536870912 | bytes 1048576 | tf_op jit(solution)/shard_map/pallas_call | solution.py:54
  82.4 1.5 %shard_map.111 = (bf16[128,128]{1,0:T(8,128)(2,1)S(1)}, bf16[128,256]{1,0:T(8,128)(2,1)S(1)}) custom-call(s32[4]{0:T(128)S(1)} %copy-done.9, bf16[64,768]{1,0:T(8,128)(2,1)S(1)} %copy-done.7, bf16[64,768]{1,0:T(8,128)(2,1)S(1)} %collective-permute-done.1.refs_2_.refs_3_.refs_0_.s1, bf16[32,5888]{1,0:T(8,128)(2,1)S(1)} %collective-permute-done.4.refs_0_.z1, ...), custom_call_target="tpu_custom_call" | custom-call | flops 536870912 | bytes 1048576 | tf_op jit(solution)/shard_map/pallas_call | solution.py:54
  84.4 3.4 %collective-permute-done.24.refs_1_.taken = bf16[256,384]{1,0:T(8,128)(2,1)S(1)} collective-permute-done((bf16[256,384]{1,0:T(8,128)(2,1)S(1)}, bf16[256,384]{1,0:T(8,128)(2,1)S(1)}, u32[]{:S(2)}, u32[]{:S(2)}) %collective-permute-start.24) | collective-permute-done | bytes 196640 | tf_op jit(solution)/shard_map/ppermute | solution.py:25
  93.2 1.8 %collective-permute-done.29.refs_1_.refs_5_ = bf16[256,256]{1,0:T(8,128)(2,1)S(1)} collective-permute-done((bf16[256,256]{1,0:T(8,128)(2,1)S(1)}, bf16[256,256]{1,0:T(8,128)(2,1)S(1)}, u32[]{:S(2)}, u32[]{:S(2)}) %collective-permute-start.29) | collective-permute-done | bytes 131104 | tf_op jit(solution)/shard_map/ppermute | solution.py:40
  95.0 2.9 %collective-permute-start.30 = (bf16[256,256]{1,0:T(8,128)(2,1)S(1)}, bf16[256,256]{1,0:T(8,128)(2,1)S(1)}, u32[]{:S(2)}, u32[]{:S(2)}) collective-permute-start(bf16[256,256]{1,0:T(8,128)(2,1)S(1)} %collective-permute-done.29.refs_1_.refs_5_), channel_id=1, source_target_pairs={{0,128},{128,0},{1,129},{129,1},{2,130},{130,2},{3,131},{131,3},{4... | collective-permute-start | bytes 393224 | tf_op jit(solution)/shard_map/ppermute | solution.py:25
  99.9 2.2 %collective-permute-start.35 = (bf16[1024,256]{1,0:T(8,128)(2,1)S(1)}, bf16[1024,256]{1,0:T(8,128)(2,1)S(1)}, u32[]{:S(2)}, u32[]{:S(2)}) collective-permute-start(bf16[1024,256]{1,0:T(8,128)(2,1)S(1)} %shard_map.113.own), channel_id=1, source_target_pairs={{0,1},{1,2},{2,3},{3,0},{128,131},{129,128},{130,129},{131,130},{4... | collective-permute-start | bytes 1572872 | tf_op jit(solution)/shard_map/ppermute | solution.py:40
  102.8 5.5 %collective-permute-done.35.side = bf16[1024,256]{1,0:T(8,128)(2,1)S(1)} collective-permute-done((bf16[1024,256]{1,0:T(8,128)(2,1)S(1)}, bf16[1024,256]{1,0:T(8,128)(2,1)S(1)}, u32[]{:S(2)}, u32[]{:S(2)}) %collective-permute-start.35) | collective-permute-done | bytes 524320 | tf_op jit(solution)/shard_map/ppermute | solution.py:40
  108.3 2.8 %collective-permute-done.34.far = bf16[512,256]{1,0:T(8,128)(2,1)S(1)} collective-permute-done((bf16[512,256]{1,0:T(8,128)(2,1)S(1)}, bf16[512,256]{1,0:T(8,128)(2,1)S(1)}, u32[]{:S(2)}, u32[]{:S(2)}) %collective-permute-start.34) | collective-permute-done | bytes 262176 | tf_op jit(solution)/shard_map/ppermute | solution.py:40
  111.1 2.2 %collective-permute-start.36 = (bf16[512,256]{1,0:T(8,128)(2,1)S(1)}, bf16[512,256]{1,0:T(8,128)(2,1)S(1)}, u32[]{:S(2)}, u32[]{:S(2)}) collective-permute-start(bf16[512,256]{1,0:T(8,128)(2,1)S(1)} %collective-permute-done.34.far), channel_id=1, source_target_pairs={{0,128},{128,0},{1,129},{129,1},{2,130},{130,2},{3,131},{131,3},{4... | collective-permute-start | bytes 786440 | tf_op jit(solution)/shard_map/ppermute | solution.py:25
  114.5 4.6 %shard_map.114 = (f32[32,8,128]{2,1,0:T(8,128)S(1)}, f32[32,8,128]{2,1,0:T(8,128)S(1)}) custom-call(s32[4]{0:T(128)S(1)} %copy-done.9, bf16[256,384]{1,0:T(8,128)(2,1)S(1)} %get-tuple-element.94.refs_0_.kept, bf16[256,384]{1,0:T(8,128)(2,1)S(1)} %collective-permute-done.24.refs_1_.taken, bf16[128,128]{1,0:T(8,128)(2,1)S(1)} %get-tuple-element.73.maps, ...), custom_call_target="tpu_custom_call" | custom-call | flops 4294967296 | bytes 1048576 | tf_op jit(solution)/shard_map/pallas_call | solution.py:54
  119.1 1.9 %collective-permute-start.40 = (bf16[512,256]{1,0:T(8,128)(2,1)S(1)}, bf16[512,256]{1,0:T(8,128)(2,1)S(1)}, u32[]{:S(2)}, u32[]{:S(2)}) collective-permute-start(bf16[512,256]{1,0:T(8,128)(2,1)S(1)} %collective-permute-done.37.far), channel_id=1, source_target_pairs={{0,128},{128,0},{1,129},{129,1},{2,130},{130,2},{3,131},{131,3},{4... | collective-permute-start | bytes 786440 | tf_op jit(solution)/shard_map/ppermute | solution.py:25
  122.4 2.4 %shard_map.115 = f32[32,8,128]{2,1,0:T(8,128)} custom-call(s32[4]{0:T(128)S(1)} %copy-done.9, bf16[128,128]{1,0:T(8,128)(2,1)S(1)} %get-tuple-element.92.query, bf16[128,128]{1,0:T(8,128)(2,1)S(1)} %get-tuple-element.73.maps, bf16[128,128]{1,0:T(8,128)(2,1)S(1)} %collective-permute-done.15.maps_g, f32[32,8,128]{2,1,0:T(8,128)S(1)} %get-tuple-element.102.keep, ...), custom_call_target="tpu_custom_call" | custom-call | flops 1073741824 | bytes 1048576 | tf_op jit(solution)/shard_map/pallas_call | solution.py:54
  124.9 4.6 %all-to-all-start = ((f32[32,8,128]{2,1,0:T(8,128)}), f32[32,8,128]{2,1,0:T(8,128)S(1)}, u32[]{:S(2)}, u32[]{:S(2)}) async-start(f32[32,8,128]{2,1,0:T(8,128)} %shard_map.115), calls=%async_computation | async-start | bytes 262144 | tf_op jit(solution)/shard_map/all_to_all | solution.py:495
  129.8 9.1 %all-to-all-done = f32[32,8,128]{2,1,0:T(8,128)S(1)} async-done(((f32[32,8,128]{2,1,0:T(8,128)}), f32[32,8,128]{2,1,0:T(8,128)S(1)}, u32[]{:S(2)}, u32[]{:S(2)}) %all-to-all-start) | async-done | bytes 131104 | tf_op jit(solution)/shard_map/all_to_all | solution.py:495
  139.1 2.1 %collective-permute-start.41 = (f32[16,64]{1,0:T(8,128)S(1)}, f32[16,64]{1,0:T(8,128)S(1)}, u32[]{:S(2)}, u32[]{:S(2)}) collective-permute-start(f32[16,64]{1,0:T(8,128)S(1)} %fusion.1), channel_id=1, source_target_pairs={{0,128},{128,0},{1,129},{129,1},{2,130},{130,2},{3,131},{131,3},{4... | collective-permute-start | bytes 12296 | tf_op jit(solution)/shard_map/ppermute | solution.py:25
  (118 shorter events, 33.5 us)
Async XLA Ops:
  0.0 6.6 %collective-permute-start.2 = (bf16[48,5120]{1,0:T(8,128)(2,1)}, bf16[48,5120]{1,0:T(8,128)(2,1)S(1)}, u32[]{:S(2)}, u32[]{:S(2)}) collective-permute-start(bf16[48,5120]{1,0:T(8,128)(2,1)} %bitcast.10), channel_id=1, source_target_pairs={{0,128},{128,0},{1,129},{129,1},{2,130},{130,2},{3,131},{131,3},{4... | collective-permute-start | bytes 1474568 | tf_op jit(solution)/shard_map/ppermute | solution.py:25
  3.2 20.5 %collective-permute-start.6 = (bf16[48,5120]{1,0:T(8,128)(2,1)}, bf16[48,5120]{1,0:T(8,128)(2,1)}, u32[]{:S(2)}, u32[]{:S(2)}) collective-permute-start(bf16[48,5120]{1,0:T(8,128)(2,1)} %bitcast.11), channel_id=1, source_target_pairs={{0,4},{4,0},{8,12},{12,8},{1,5},{5,1},{9,13},{13,9},{2,6},{6,2},{1... | collective-permute-start | bytes 1474568 | tf_op jit(solution)/shard_map/ppermute | solution.py:25
  8.3 22.5 %collective-permute-start.5 = (bf16[96,5120]{1,0:T(8,128)(2,1)S(1)}, bf16[96,5120]{1,0:T(8,128)(2,1)S(1)}, u32[]{:S(2)}, u32[]{:S(2)}) collective-permute-start(bf16[96,5120]{1,0:T(8,128)(2,1)S(1)} %shard_map.101.w0), channel_id=1, source_target_pairs={{0,1},{1,2},{2,3},{3,0},{128,131},{129,128},{130,129},{131,130},{4... | collective-permute-start | bytes 2949128 | tf_op jit(solution)/shard_map/ppermute | solution.py:40
  10.6 9.4 %collective-permute-start = (bf16[16,5120]{1,0:T(8,128)(2,1)S(1)}, bf16[16,5120]{1,0:T(8,128)(2,1)S(1)}, u32[]{:S(2)}, u32[]{:S(2)}) collective-permute-start(bf16[16,5120]{1,0:T(8,128)(2,1)S(1)} %copy-done.5), channel_id=1, source_target_pairs={{0,12},{12,0},{4,8},{8,4},{1,13},{13,1},{5,9},{9,5},{2,14},{14,2},... | collective-permute-start | bytes 491528 | tf_op jit(solution)/shard_map/ppermute | solution.py:33
  12.4 7.6 %collective-permute-start.1 = (bf16[64,768]{1,0:T(8,128)(2,1)S(1)}, bf16[64,768]{1,0:T(8,128)(2,1)S(1)}, u32[]{:S(2)}, u32[]{:S(2)}) collective-permute-start(bf16[64,768]{1,0:T(8,128)(2,1)S(1)} %copy-done.6), channel_id=1, source_target_pairs={{0,16},{16,32},{32,48},{48,64},{64,80},{80,96},{96,112},{112,0},{1... | collective-permute-start | bytes 294920 | tf_op jit(solution)/shard_map/ppermute | solution.py:40
  18.0 5.5 %collective-permute-start.3 = (bf16[48,512]{1,0:T(8,128)(2,1)S(1)}, bf16[48,512]{1,0:T(8,128)(2,1)}, u32[]{:S(2)}, u32[]{:S(2)}) collective-permute-start(bf16[48,512]{1,0:T(8,128)(2,1)S(1)} %pad_maximum_fusion.3), channel_id=1, source_target_pairs={{16,128},{48,160},{80,192},{112,224},{128,16},{160,48},{192,80},{2... | collective-permute-start | bytes 147464 | tf_op jit(solution)/shard_map/ppermute | solution.py:351
  23.8 4.5 %collective-permute-start.8 = (bf16[48,5120]{1,0:T(8,128)(2,1)}, bf16[48,5120]{1,0:T(8,128)(2,1)}, u32[]{:S(2)}, u32[]{:S(2)}) collective-permute-start(bf16[48,5120]{1,0:T(8,128)(2,1)} %collective-permute-done.6.refs_0_), channel_id=1, source_target_pairs={{0,128},{128,0},{1,129},{129,1},{2,130},{130,2},{3,131},{131,3},{4... | collective-permute-start | bytes 1474568 | tf_op jit(solution)/shard_map/ppermute | solution.py:25
  23.9 6.8 %collective-permute-start.4 = (bf16[32,5888]{1,0:T(8,128)(2,1)S(1)}, bf16[32,5888]{1,0:T(8,128)(2,1)S(1)}, u32[]{:S(2)}, u32[]{:S(2)}) collective-permute-start(bf16[32,5888]{1,0:T(8,128)(2,1)S(1)} %shard_map.102.near), channel_id=1, source_target_pairs={{0,16},{16,32},{32,48},{48,64},{64,80},{80,96},{96,112},{112,0},{1... | collective-permute-start | bytes 1130504 | tf_op jit(solution)/shard_map/ppermute | solution.py:40
  24.0 5.8 %collective-permute-start.7 = (bf16[16,5120]{1,0:T(8,128)(2,1)}, bf16[16,5120]{1,0:T(8,128)(2,1)S(1)}, u32[]{:S(2)}, u32[]{:S(2)}) collective-permute-start(bf16[16,5120]{1,0:T(8,128)(2,1)} %copy-done.4), channel_id=1, source_target_pairs={{0,128},{128,0},{1,129},{129,1},{2,130},{130,2},{3,131},{131,3},{4... | collective-permute-start | bytes 491528 | tf_op jit(solution)/shard_map/ppermute | solution.py:25
  25.3 4.5 %collective-permute-start.9 = (bf16[48,512]{1,0:T(8,128)(2,1)S(1)}, bf16[48,512]{1,0:T(8,128)(2,1)S(1)}, u32[]{:S(2)}, u32[]{:S(2)}) collective-permute-start(bf16[48,512]{1,0:T(8,128)(2,1)S(1)} %broadcast_select_fusion), channel_id=1, source_target_pairs={{0,12},{12,0},{4,8},{8,4},{1,13},{13,1},{5,9},{9,5},{2,14},{14,2},... | collective-permute-start | bytes 147464 | tf_op jit(solution)/shard_map/ppermute | solution.py:33
  30.8 14.4 %collective-permute-start.11 = (bf16[96,5120]{1,0:T(8,128)(2,1)S(1)}, bf16[96,5120]{1,0:T(8,128)(2,1)S(1)}, u32[]{:S(2)}, u32[]{:S(2)}) collective-permute-start(bf16[96,5120]{1,0:T(8,128)(2,1)S(1)} %collective-permute-done.5.refs_0_.y1), channel_id=1, source_target_pairs={{0,128},{128,0},{1,129},{129,1},{2,130},{130,2},{3,131},{131,3},{4... | collective-permute-start | bytes 2949128 | tf_op jit(solution)/shard_map/ppermute | solution.py:25
  33.3 13.2 %collective-permute-start.12 = (bf16[96,5120]{1,0:T(8,128)(2,1)S(1)}, bf16[96,5120]{1,0:T(8,128)(2,1)S(1)}, u32[]{:S(2)}, u32[]{:S(2)}) collective-permute-start(bf16[96,5120]{1,0:T(8,128)(2,1)S(1)} %shard_map.103.pr), channel_id=1, source_target_pairs={{0,1},{1,2},{2,3},{3,0},{128,131},{129,128},{130,129},{131,130},{4... | collective-permute-start | bytes 2949128 | tf_op jit(solution)/shard_map/ppermute | solution.py:40
  34.4 10.9 %collective-permute-start.10 = (bf16[64,5888]{1,0:T(8,128)(2,1)S(1)}, bf16[64,5888]{1,0:T(8,128)(2,1)S(1)}, u32[]{:S(2)}, u32[]{:S(2)}) collective-permute-start(bf16[64,5888]{1,0:T(8,128)(2,1)S(1)} %shard_map.105), channel_id=1, source_target_pairs={{0,16},{16,32},{32,48},{48,64},{64,80},{80,96},{96,112},{112,0},{1... | collective-permute-start | bytes 2261000 | tf_op jit(solution)/shard_map/ppermute | solution.py:40
  34.9 4.3 %collective-permute-start.13 = (bf16[48,1024]{1,0:T(8,128)(2,1)S(1)}, bf16[48,1024]{1,0:T(8,128)(2,1)S(1)}, u32[]{:S(2)}, u32[]{:S(2)}) collective-permute-start(bf16[48,1024]{1,0:T(8,128)(2,1)S(1)} %pad_maximum_fusion.2), channel_id=1, source_target_pairs={{0,4},{4,0},{8,12},{12,8},{1,5},{5,1},{9,13},{13,9},{2,6},{6,2},{1... | collective-permute-start | bytes 294920 | tf_op jit(solution)/shard_map/ppermute | solution.py:25
  46.5 12.9 %collective-permute-start.17 = (bf16[96,5120]{1,0:T(8,128)(2,1)S(1)}, bf16[96,5120]{1,0:T(8,128)(2,1)S(1)}, u32[]{:S(2)}, u32[]{:S(2)}) collective-permute-start(bf16[96,5120]{1,0:T(8,128)(2,1)S(1)} %collective-permute-done.12.refs_1_.y2), channel_id=1, source_target_pairs={{0,128},{128,0},{1,129},{129,1},{2,130},{130,2},{3,131},{131,3},{4... | collective-permute-start | bytes 2949128 | tf_op jit(solution)/shard_map/ppermute | solution.py:25
  48.6 10.8 %collective-permute-start.16 = (bf16[64,5888]{1,0:T(8,128)(2,1)S(1)}, bf16[64,5888]{1,0:T(8,128)(2,1)S(1)}, u32[]{:S(2)}, u32[]{:S(2)}) collective-permute-start(bf16[64,5888]{1,0:T(8,128)(2,1)S(1)} %collective-permute-done.10.refs_1_.z2), channel_id=1, source_target_pairs={{0,16},{16,32},{32,48},{48,64},{64,80},{80,96},{96,112},{112,0},{1... | collective-permute-start | bytes 2261000 | tf_op jit(solution)/shard_map/ppermute | solution.py:40
  49.4 17.7 %collective-permute-start.19 = (bf16[48,14336]{1,0:T(8,128)(2,1)S(1)}, bf16[48,14336]{1,0:T(8,128)(2,1)S(1)}, u32[]{:S(2)}, u32[]{:S(2)}) collective-permute-start(bf16[48,14336]{1,0:T(8,128)(2,1)S(1)} %shard_map.106), channel_id=1, source_target_pairs={{0,1},{1,2},{2,3},{3,0},{128,131},{129,128},{130,129},{131,130},{4... | collective-permute-start | bytes 4128776 | tf_op jit(solution)/shard_map/ppermute | solution.py:40
  59.4 10.8 %collective-permute-start.18 = (bf16[64,5888]{1,0:T(8,128)(2,1)S(1)}, bf16[64,5888]{1,0:T(8,128)(2,1)S(1)}, u32[]{:S(2)}, u32[]{:S(2)}) collective-permute-start(bf16[64,5888]{1,0:T(8,128)(2,1)S(1)} %collective-permute-done.16.refs_2_.z3), channel_id=1, source_target_pairs={{0,16},{16,32},{32,48},{48,64},{64,80},{80,96},{96,112},{112,0},{1... | collective-permute-start | bytes 2261000 | tf_op jit(solution)/shard_map/ppermute | solution.py:40
  70.1 7.9 %collective-permute-start.21 = (bf16[48,14336]{1,0:T(8,128)(2,1)S(1)}, bf16[48,14336]{1,0:T(8,128)(2,1)S(1)}, u32[]{:S(2)}, u32[]{:S(2)}) collective-permute-start(bf16[48,14336]{1,0:T(8,128)(2,1)S(1)} %collective-permute-done.19.refs_0_.yz), channel_id=1, source_target_pairs={{0,128},{128,0},{1,129},{129,1},{2,130},{130,2},{3,131},{131,3},{4... | collective-permute-start | bytes 4128776 | tf_op jit(solution)/shard_map/ppermute | solution.py:25
  74.3 6.1 %collective-permute-start.22 = (bf16[48,2048]{1,0:T(8,128)(2,1)S(1)}, bf16[48,2048]{1,0:T(8,128)(2,1)S(1)}, u32[]{:S(2)}, u32[]{:S(2)}) collective-permute-start(bf16[48,2048]{1,0:T(8,128)(2,1)S(1)} %shard_map.108), channel_id=1, source_target_pairs={{0,1},{1,2},{2,3},{3,0},{128,131},{129,128},{130,129},{131,130},{4... | collective-permute-start | bytes 589832 | tf_op jit(solution)/shard_map/ppermute | solution.py:40
  81.3 6.5 %collective-permute-start.24 = (bf16[256,384]{1,0:T(8,128)(2,1)S(1)}, bf16[256,384]{1,0:T(8,128)(2,1)S(1)}, u32[]{:S(2)}, u32[]{:S(2)}) collective-permute-start(bf16[256,384]{1,0:T(8,128)(2,1)S(1)} %get-tuple-element.89), channel_id=1, source_target_pairs={{0,4},{4,0},{8,12},{12,8},{1,5},{5,1},{9,13},{13,9},{2,6},{6,2},{1... | collective-permute-start | bytes 589832 | tf_op jit(solution)/shard_map/ppermute | solution.py:25
  84.3 4.3 %collective-permute-start.26 = (bf16[256,384]{1,0:T(8,128)(2,1)S(1)}, bf16[256,384]{1,0:T(8,128)(2,1)S(1)}, u32[]{:S(2)}, u32[]{:S(2)}) collective-permute-start(bf16[256,384]{1,0:T(8,128)(2,1)S(1)} %get-tuple-element.94.refs_0_.kept), channel_id=1, source_target_pairs={{0,128},{128,0},{1,129},{129,1},{2,130},{130,2},{3,131},{131,3},{4... | collective-permute-start | bytes 589832 | tf_op jit(solution)/shard_map/ppermute | solution.py:25
  89.8 12.4 %collective-permute-start.28 = (bf16[1024,256]{1,0:T(8,128)(2,1)S(1)}, bf16[1024,256]{1,0:T(8,128)(2,1)S(1)}, u32[]{:S(2)}, u32[]{:S(2)}) collective-permute-start(bf16[1024,256]{1,0:T(8,128)(2,1)S(1)} %shard_map.112.own), channel_id=1, source_target_pairs={{0,1},{1,2},{2,3},{3,0},{128,131},{129,128},{130,129},{131,130},{4... | collective-permute-start | bytes 1572872 | tf_op jit(solution)/shard_map/ppermute | solution.py:40
  90.9 4.1 %collective-permute-start.29 = (bf16[256,256]{1,0:T(8,128)(2,1)S(1)}, bf16[256,256]{1,0:T(8,128)(2,1)S(1)}, u32[]{:S(2)}, u32[]{:S(2)}) collective-permute-start(bf16[256,256]{1,0:T(8,128)(2,1)S(1)} %pad_maximum_fusion.1), channel_id=1, source_target_pairs={{0,4},{4,8},{8,12},{12,0},{128,140},{132,128},{136,132},{140,136},... | collective-permute-start | bytes 393224 | tf_op jit(solution)/shard_map/ppermute | solution.py:40
  92.0 5.9 %collective-permute-start.31 = (bf16[128,256]{1,0:T(8,128)(2,1)S(1)}, bf16[128,256]{1,0:T(8,128)(2,1)S(1)}, u32[]{:S(2)}, u32[]{:S(2)}) collective-permute-start(bf16[128,256]{1,0:T(8,128)(2,1)S(1)} %get-tuple-element.95.refs_0_), channel_id=1, source_target_pairs={{0,8},{4,12},{8,0},{12,4},{1,9},{5,13},{9,1},{13,5},{2,10},{6,14},... | collective-permute-start | bytes 196616 | tf_op jit(solution)/shard_map/ppermute | solution.py:25
  95.0 4.1 %collective-permute-start.30 = (bf16[256,256]{1,0:T(8,128)(2,1)S(1)}, bf16[256,256]{1,0:T(8,128)(2,1)S(1)}, u32[]{:S(2)}, u32[]{:S(2)}) collective-permute-start(bf16[256,256]{1,0:T(8,128)(2,1)S(1)} %collective-permute-done.29.refs_1_.refs_5_), channel_id=1, source_target_pairs={{0,128},{128,0},{1,129},{129,1},{2,130},{130,2},{3,131},{131,3},{4... | collective-permute-start | bytes 393224 | tf_op jit(solution)/shard_map/ppermute | solution.py:25
  99.9 8.4 %collective-permute-start.35 = (bf16[1024,256]{1,0:T(8,128)(2,1)S(1)}, bf16[1024,256]{1,0:T(8,128)(2,1)S(1)}, u32[]{:S(2)}, u32[]{:S(2)}) collective-permute-start(bf16[1024,256]{1,0:T(8,128)(2,1)S(1)} %shard_map.113.own), channel_id=1, source_target_pairs={{0,1},{1,2},{2,3},{3,0},{128,131},{129,128},{130,129},{131,130},{4... | collective-permute-start | bytes 1572872 | tf_op jit(solution)/shard_map/ppermute | solution.py:40
  102.2 8.9 %collective-permute-start.34 = (bf16[512,256]{1,0:T(8,128)(2,1)S(1)}, bf16[512,256]{1,0:T(8,128)(2,1)S(1)}, u32[]{:S(2)}, u32[]{:S(2)}) collective-permute-start(bf16[512,256]{1,0:T(8,128)(2,1)S(1)} %slice.24), channel_id=1, source_target_pairs={{0,1},{1,2},{2,3},{3,0},{128,131},{129,128},{130,129},{131,130},{4... | collective-permute-start | bytes 786440 | tf_op jit(solution)/shard_map/ppermute | solution.py:40
  102.7 11.9 %collective-permute-start.33 = (bf16[1024,256]{1,0:T(8,128)(2,1)S(1)}, bf16[1024,256]{1,0:T(8,128)(2,1)S(1)}, u32[]{:S(2)}, u32[]{:S(2)}) collective-permute-start(bf16[1024,256]{1,0:T(8,128)(2,1)S(1)} %collective-permute-done.28.side), channel_id=1, source_target_pairs={{0,128},{128,0},{1,129},{129,1},{2,130},{130,2},{3,131},{131,3},{4... | collective-permute-start | bytes 1572872 | tf_op jit(solution)/shard_map/ppermute | solution.py:25
  113.4 5.7 %collective-permute-start.37 = (bf16[512,256]{1,0:T(8,128)(2,1)S(1)}, bf16[512,256]{1,0:T(8,128)(2,1)S(1)}, u32[]{:S(2)}, u32[]{:S(2)}) collective-permute-start(bf16[512,256]{1,0:T(8,128)(2,1)S(1)} %slice.28), channel_id=1, source_target_pairs={{0,1},{1,2},{2,3},{3,0},{128,131},{129,128},{130,129},{131,130},{4... | collective-permute-start | bytes 786440 | tf_op jit(solution)/shard_map/ppermute | solution.py:40
  114.4 6.6 %collective-permute-start.39 = (bf16[1024,256]{1,0:T(8,128)(2,1)S(1)}, bf16[1024,256]{1,0:T(8,128)(2,1)S(1)}, u32[]{:S(2)}, u32[]{:S(2)}) collective-permute-start(bf16[1024,256]{1,0:T(8,128)(2,1)S(1)} %collective-permute-done.35.side), channel_id=1, source_target_pairs={{0,128},{128,0},{1,129},{129,1},{2,130},{130,2},{3,131},{131,3},{4... | collective-permute-start | bytes 1572872 | tf_op jit(solution)/shard_map/ppermute | solution.py:25
  124.9 14.0 %all-to-all-start = ((f32[32,8,128]{2,1,0:T(8,128)}), f32[32,8,128]{2,1,0:T(8,128)S(1)}, u32[]{:S(2)}, u32[]{:S(2)}) async-start(f32[32,8,128]{2,1,0:T(8,128)} %shard_map.115), calls=%async_computation | async-start | bytes 262144 | tf_op jit(solution)/shard_map/all_to_all | solution.py:495
  (28 other events, 291.9 us)

commit v3 on v2

--- a/solution.py
+++ b/solution.py
@@ -85,9 +85,9 @@
 
 
 def norm_body(
-    where, large, small, gain_l, gain_s, mine, other, out_s, hold_l, hold_s, g_l, g_s, sems
+    large, small, gain_l, gain_s, mine, other, out_s, hold_l, hold_s, g_l, g_s, sems
 ):
-    core = where[0]
+    core = lax.axis_index("grp")
     tasks = [
         pltpu.make_async_copy(source, target, sems.at[i])
         for i, (source, target) in enumerate(
@@ -326,7 +326,7 @@
     mine, other, s0 = call(
         norm_body,
         [((16, DL), BF), ((16, DL), BF), ((64, KS), BF)],
-        (where, latent_large, latent_small, gain_large, gain_small),
+        (latent_large, latent_small, gain_large, gain_small),
         [
             pltpu.VMEM((32, DL), BF),
             pltpu.VMEM((32, DS), BF),
@@ -335,7 +335,7 @@
             pltpu.SemaphoreType.DMA((4,)),
         ],
         limit=60,
-        placed=[SMEM] + [ANY] * 4,
+        placed=[ANY] * 4,
     )
     w, ws = qkv_large.T, qkv_small.T
     w_g = swap(w)

time: 143 us -> 142 us (level)
  transfers between devices with their start and end apart: 43 -> 43, of which waited for: 22 -> 22; matrix products, arithmetic and copies ran while one was open for 1% -> 1% of each run, Pallas kernels for 13% -> 12%
where the time goes in v3:
time: 142 us; the launch traced here: 141 us
  waiting for transfers between devices  61 us (43%)
  starting transfers between devices  56 us (39%)
  Pallas kernels  19.7 us (14%)
  local copies, waits for them, and re-layouts  2.15 us (2%)
  other arithmetic  1.57 us (1%)
    ppermute x14, waiting for transfers between devices, spread(): return lax.ppermute(block, ('grp', axis), pairs)  33.5 us
    ppermute x25, starting transfers between devices, flip(): return lax.ppermute(block, axis, [(i, i ^ mask) for i in range(count)])  26.9 us
    ppermute x14, starting transfers between devices, spread(): return lax.ppermute(block, ('grp', axis), pairs)  19.3 us
    pallas_call x7, Pallas kernels, call(): pl.pallas_call(body, out_shape=[jax.ShapeDtypeStruct(shape, dtype) for sh...  16 us
    ppermute x25, waiting for transfers between devices, flip(): return lax.ppermute(block, axis, [(i, i ^ mask) for i in range(count)])  14.8 us
    all_to_all x1, waiting for transfers between devices, shards(): lax.all_to_all(total, ('z', 'x'), split_axis=0, concat_axis=0, tiled=True)  9.06 us
    all_to_all x1, starting transfers between devices, shards(): lax.all_to_all(total, ('z', 'x'), split_axis=0, concat_axis=0, tiled=True)  4.62 us
    pallas_call x9, Pallas kernels, pack(): pl.pallas_call(body, out_shape=jax.ShapeDtypeStruct(shape, BF), in_specs=...  3.71 us
  transfers between devices with their start and end apart: 43, of which 22 were waited for; matrix products, arithmetic and copies ran while one was open for 1% of the time, Pallas kernels for 12%

profile of v3, /device:TPU:1, one launch (start us, length us, event | category | flops | bytes accessed | tf_op | source)
XLA Modules:
  0.0 141.3 jit_solution(2236091432891904723)
XLA Ops:
  0.0 3.2 %collective-permute-start.2 = (bf16[48,5120]{1,0:T(8,128)(2,1)}, bf16[48,5120]{1,0:T(8,128)(2,1)S(1)}, u32[]{:S(2)}, u32[]{:S(2)}) collective-permute-start(bf16[48,5120]{1,0:T(8,128)(2,1)} %bitcast.10), channel_id=1, source_target_pairs={{0,128},{128,0},{1,129},{129,1},{2,130},{130,2},{3,131},{131,3},{4... | collective-permute-start | bytes 1474568 | tf_op jit(solution)/shard_map/ppermute | solution.py:25
  3.2 2.0 %shard_map.100 = (bf16[16,5120]{1,0:T(8,128)(2,1)}, bf16[16,5120]{1,0:T(8,128)(2,1)}, bf16[64,768]{1,0:T(8,128)(2,1)}) custom-call(bf16[32,5120]{1,0:T(8,128)(2,1)} %large.1, bf16[32,1536]{1,0:T(8,128)(2,1)} %small.1, f32[5120]{0:T(1024)} %gain_l.1, f32[1536]{0:T(1024)} %gain_s.1), custom_call_target="tpu_custom_call" | custom-call | bytes 1048576 | tf_op jit(solution)/shard_map/pallas_call | solution.py:54
  6.9 2.3 %collective-permute-start.5 = (bf16[96,5120]{1,0:T(8,128)(2,1)S(1)}, bf16[96,5120]{1,0:T(8,128)(2,1)S(1)}, u32[]{:S(2)}, u32[]{:S(2)}) collective-permute-start(bf16[96,5120]{1,0:T(8,128)(2,1)S(1)} %shard_map.101.w0), channel_id=1, source_target_pairs={{0,1},{1,2},{2,3},{3,0},{128,131},{129,128},{130,129},{131,130},{4... | collective-permute-start | bytes 2949128 | tf_op jit(solution)/shard_map/ppermute | solution.py:40
  9.2 1.8 %collective-permute-start = (bf16[16,5120]{1,0:T(8,128)(2,1)S(1)}, bf16[16,5120]{1,0:T(8,128)(2,1)S(1)}, u32[]{:S(2)}, u32[]{:S(2)}) collective-permute-start(bf16[16,5120]{1,0:T(8,128)(2,1)S(1)} %copy-done.5), channel_id=1, source_target_pairs={{0,12},{12,0},{4,8},{8,4},{1,13},{13,1},{5,9},{9,5},{2,14},{14,2},... | collective-permute-start | bytes 491528 | tf_op jit(solution)/shard_map/ppermute | solution.py:33
  11.0 5.6 %collective-permute-start.1 = (bf16[64,768]{1,0:T(8,128)(2,1)S(1)}, bf16[64,768]{1,0:T(8,128)(2,1)S(1)}, u32[]{:S(2)}, u32[]{:S(2)}) collective-permute-start(bf16[64,768]{1,0:T(8,128)(2,1)S(1)} %copy-done.6), channel_id=1, source_target_pairs={{0,16},{16,32},{32,48},{48,64},{64,80},{80,96},{96,112},{112,0},{1... | collective-permute-start | bytes 294920 | tf_op jit(solution)/shard_map/ppermute | solution.py:40
  16.7 1.9 %collective-permute-start.3 = (bf16[48,512]{1,0:T(8,128)(2,1)S(1)}, bf16[48,512]{1,0:T(8,128)(2,1)}, u32[]{:S(2)}, u32[]{:S(2)}) collective-permute-start(bf16[48,512]{1,0:T(8,128)(2,1)S(1)} %pad_maximum_fusion.3), channel_id=1, source_target_pairs={{16,128},{48,160},{80,192},{112,224},{128,16},{160,48},{192,80},{2... | collective-permute-start | bytes 147464 | tf_op jit(solution)/shard_map/ppermute | solution.py:351
  18.6 3.6 %collective-permute-done.3 = bf16[48,512]{1,0:T(8,128)(2,1)} collective-permute-done((bf16[48,512]{1,0:T(8,128)(2,1)S(1)}, bf16[48,512]{1,0:T(8,128)(2,1)}, u32[]{:S(2)}, u32[]{:S(2)}) %collective-permute-start.3) | collective-permute-done | bytes 49184 | tf_op jit(solution)/shard_map/ppermute | solution.py:351
  29.4 2.5 %collective-permute-start.11 = (bf16[96,5120]{1,0:T(8,128)(2,1)S(1)}, bf16[96,5120]{1,0:T(8,128)(2,1)S(1)}, u32[]{:S(2)}, u32[]{:S(2)}) collective-permute-start(bf16[96,5120]{1,0:T(8,128)(2,1)S(1)} %collective-permute-done.5.refs_0_.y1), channel_id=1, source_target_pairs={{0,128},{128,0},{1,129},{129,1},{2,130},{130,2},{3,131},{131,3},{4... | collective-permute-start | bytes 2949128 | tf_op jit(solution)/shard_map/ppermute | solution.py:25
  33.6 4.2 %collective-permute-done.13 = bf16[48,1024]{1,0:T(8,128)(2,1)S(1)} collective-permute-done((bf16[48,1024]{1,0:T(8,128)(2,1)S(1)}, bf16[48,1024]{1,0:T(8,128)(2,1)S(1)}, u32[]{:S(2)}, u32[]{:S(2)}) %collective-permute-start.13) | collective-permute-done | bytes 98336 | tf_op jit(solution)/shard_map/ppermute | solution.py:25
  39.4 4.4 %collective-permute-done.10.refs_1_.z2 = bf16[64,5888]{1,0:T(8,128)(2,1)S(1)} collective-permute-done((bf16[64,5888]{1,0:T(8,128)(2,1)S(1)}, bf16[64,5888]{1,0:T(8,128)(2,1)S(1)}, u32[]{:S(2)}, u32[]{:S(2)}) %collective-permute-start.10) | collective-permute-done | bytes 753696 | tf_op jit(solution)/shard_map/ppermute | solution.py:40
  45.1 2.1 %collective-permute-start.17 = (bf16[96,5120]{1,0:T(8,128)(2,1)S(1)}, bf16[96,5120]{1,0:T(8,128)(2,1)S(1)}, u32[]{:S(2)}, u32[]{:S(2)}) collective-permute-start(bf16[96,5120]{1,0:T(8,128)(2,1)S(1)} %collective-permute-done.12.refs_1_.y2), channel_id=1, source_target_pairs={{0,128},{128,0},{1,129},{129,1},{2,130},{130,2},{3,131},{131,3},{4... | collective-permute-start | bytes 2949128 | tf_op jit(solution)/shard_map/ppermute | solution.py:25
  48.7 9.2 %collective-permute-done.16.refs_2_.z3 = bf16[64,5888]{1,0:T(8,128)(2,1)S(1)} collective-permute-done((bf16[64,5888]{1,0:T(8,128)(2,1)S(1)}, bf16[64,5888]{1,0:T(8,128)(2,1)S(1)}, u32[]{:S(2)}, u32[]{:S(2)}) %collective-permute-start.16) | collective-permute-done | bytes 753696 | tf_op jit(solution)/shard_map/ppermute | solution.py:40
  58.0 1.7 %collective-permute-start.18 = (bf16[64,5888]{1,0:T(8,128)(2,1)S(1)}, bf16[64,5888]{1,0:T(8,128)(2,1)S(1)}, u32[]{:S(2)}, u32[]{:S(2)}) collective-permute-start(bf16[64,5888]{1,0:T(8,128)(2,1)S(1)} %collective-permute-done.16.refs_2_.z3), channel_id=1, source_target_pairs={{0,16},{16,32},{32,48},{48,64},{64,80},{80,96},{96,112},{112,0},{1... | collective-permute-start | bytes 2261000 | tf_op jit(solution)/shard_map/ppermute | solution.py:40
  61.3 4.4 %collective-permute-done.19.refs_0_.yz = bf16[48,14336]{1,0:T(8,128)(2,1)S(1)} collective-permute-done((bf16[48,14336]{1,0:T(8,128)(2,1)S(1)}, bf16[48,14336]{1,0:T(8,128)(2,1)S(1)}, u32[]{:S(2)}, u32[]{:S(2)}) %collective-permute-start.19) | collective-permute-done | bytes 1376288 | tf_op jit(solution)/shard_map/ppermute | solution.py:40
  65.7 3.1 %collective-permute-done.18.z4 = bf16[64,5888]{1,0:T(8,128)(2,1)S(1)} collective-permute-done((bf16[64,5888]{1,0:T(8,128)(2,1)S(1)}, bf16[64,5888]{1,0:T(8,128)(2,1)S(1)}, u32[]{:S(2)}, u32[]{:S(2)}) %collective-permute-start.18) | collective-permute-done | bytes 753696 | tf_op jit(solution)/shard_map/ppermute | solution.py:40
  68.8 4.1 %collective-permute-start.21 = (bf16[48,14336]{1,0:T(8,128)(2,1)S(1)}, bf16[48,14336]{1,0:T(8,128)(2,1)S(1)}, u32[]{:S(2)}, u32[]{:S(2)}) collective-permute-start(bf16[48,14336]{1,0:T(8,128)(2,1)S(1)} %collective-permute-done.19.refs_0_.yz), channel_id=1, source_target_pairs={{0,128},{128,0},{1,129},{129,1},{2,130},{130,2},{3,131},{131,3},{4... | collective-permute-start | bytes 4128776 | tf_op jit(solution)/shard_map/ppermute | solution.py:25
  74.1 2.5 %shard_map.109 = (bf16[384,256]{1,0:T(8,128)(2,1)S(1)}, bf16[288,256]{1,0:T(8,128)(2,1)S(1)}) custom-call(s32[4]{0:T(128)S(1)} %pad_add_fusion.where, bf16[32,5888]{1,0:T(8,128)(2,1)S(1)} %shard_map.102.near, bf16[32,5888]{1,0:T(8,128)(2,1)S(1)} %collective-permute-done.4.refs_0_.z1, bf16[64,5888]{1,0:T(8,128)(2,1)S(1)} %collective-permute-done.10.refs_1_.z2, ...), custom_call_target="tpu_custom_call" | custom-call | flops 4294967296 | bytes 1048576 | tf_op jit(solution)/shard_map/pallas_call | solution.py:54
  76.7 2.3 %shard_map.110 = (bf16[256,384]{1,0:T(8,128)(2,1)S(1)}, bf16[256,384]{1,0:T(8,128)(2,1)S(1)}) custom-call(s32[4]{0:T(128)S(1)} %pad_add_fusion.where, bf16[32,5888]{1,0:T(8,128)(2,1)S(1)} %shard_map.102.near, bf16[32,5888]{1,0:T(8,128)(2,1)S(1)} %collective-permute-done.4.refs_0_.z1, bf16[64,5888]{1,0:T(8,128)(2,1)S(1)} %collective-permute-done.10.refs_1_.z2, ...), custom_call_target="tpu_custom_call" | custom-call | flops 536870912 | bytes 1048576 | tf_op jit(solution)/shard_map/pallas_call | solution.py:54
  81.0 1.5 %shard_map.111 = (bf16[128,128]{1,0:T(8,128)(2,1)S(1)}, bf16[128,256]{1,0:T(8,128)(2,1)S(1)}) custom-call(s32[4]{0:T(128)S(1)} %pad_add_fusion.where, bf16[64,768]{1,0:T(8,128)(2,1)S(1)} %copy-done.7, bf16[64,768]{1,0:T(8,128)(2,1)S(1)} %collective-permute-done.1.refs_2_.refs_3_.refs_0_.s1, bf16[32,5888]{1,0:T(8,128)(2,1)S(1)} %collective-permute-done.4.refs_0_.z1, ...), custom_call_target="tpu_custom_call" | custom-call | flops 536870912 | bytes 1048576 | tf_op jit(solution)/shard_map/pallas_call | solution.py:54
  83.1 3.4 %collective-permute-done.24.refs_1_.taken = bf16[256,384]{1,0:T(8,128)(2,1)S(1)} collective-permute-done((bf16[256,384]{1,0:T(8,128)(2,1)S(1)}, bf16[256,384]{1,0:T(8,128)(2,1)S(1)}, u32[]{:S(2)}, u32[]{:S(2)}) %collective-permute-start.24) | collective-permute-done | bytes 196640 | tf_op jit(solution)/shard_map/ppermute | solution.py:25
  91.8 1.8 %collective-permute-done.29.refs_1_.refs_5_ = bf16[256,256]{1,0:T(8,128)(2,1)S(1)} collective-permute-done((bf16[256,256]{1,0:T(8,128)(2,1)S(1)}, bf16[256,256]{1,0:T(8,128)(2,1)S(1)}, u32[]{:S(2)}, u32[]{:S(2)}) %collective-permute-start.29) | collective-permute-done | bytes 131104 | tf_op jit(solution)/shard_map/ppermute | solution.py:40
  93.7 2.9 %collective-permute-start.30 = (bf16[256,256]{1,0:T(8,128)(2,1)S(1)}, bf16[256,256]{1,0:T(8,128)(2,1)S(1)}, u32[]{:S(2)}, u32[]{:S(2)}) collective-permute-start(bf16[256,256]{1,0:T(8,128)(2,1)S(1)} %collective-permute-done.29.refs_1_.refs_5_), channel_id=1, source_target_pairs={{0,128},{128,0},{1,129},{129,1},{2,130},{130,2},{3,131},{131,3},{4... | collective-permute-start | bytes 393224 | tf_op jit(solution)/shard_map/ppermute | solution.py:25
  98.5 2.2 %collective-permute-start.35 = (bf16[1024,256]{1,0:T(8,128)(2,1)S(1)}, bf16[1024,256]{1,0:T(8,128)(2,1)S(1)}, u32[]{:S(2)}, u32[]{:S(2)}) collective-permute-start(bf16[1024,256]{1,0:T(8,128)(2,1)S(1)} %shard_map.113.own), channel_id=1, source_target_pairs={{0,1},{1,2},{2,3},{3,0},{128,131},{129,128},{130,129},{131,130},{4... | collective-permute-start | bytes 1572872 | tf_op jit(solution)/shard_map/ppermute | solution.py:40
  101.4 5.5 %collective-permute-done.35.side = bf16[1024,256]{1,0:T(8,128)(2,1)S(1)} collective-permute-done((bf16[1024,256]{1,0:T(8,128)(2,1)S(1)}, bf16[1024,256]{1,0:T(8,128)(2,1)S(1)}, u32[]{:S(2)}, u32[]{:S(2)}) %collective-permute-start.35) | collective-permute-done | bytes 524320 | tf_op jit(solution)/shard_map/ppermute | solution.py:40
  106.9 2.8 %collective-permute-done.34.far = bf16[512,256]{1,0:T(8,128)(2,1)S(1)} collective-permute-done((bf16[512,256]{1,0:T(8,128)(2,1)S(1)}, bf16[512,256]{1,0:T(8,128)(2,1)S(1)}, u32[]{:S(2)}, u32[]{:S(2)}) %collective-permute-start.34) | collective-permute-done | bytes 262176 | tf_op jit(solution)/shard_map/ppermute | solution.py:40
  109.7 2.2 %collective-permute-start.36 = (bf16[512,256]{1,0:T(8,128)(2,1)S(1)}, bf16[512,256]{1,0:T(8,128)(2,1)S(1)}, u32[]{:S(2)}, u32[]{:S(2)}) collective-permute-start(bf16[512,256]{1,0:T(8,128)(2,1)S(1)} %collective-permute-done.34.far), channel_id=1, source_target_pairs={{0,128},{128,0},{1,129},{129,1},{2,130},{130,2},{3,131},{131,3},{4... | collective-permute-start | bytes 786440 | tf_op jit(solution)/shard_map/ppermute | solution.py:25
  113.2 4.6 %shard_map.114 = (f32[32,8,128]{2,1,0:T(8,128)S(1)}, f32[32,8,128]{2,1,0:T(8,128)S(1)}) custom-call(s32[4]{0:T(128)S(1)} %pad_add_fusion.where, bf16[256,384]{1,0:T(8,128)(2,1)S(1)} %get-tuple-element.94.refs_0_.kept, bf16[256,384]{1,0:T(8,128)(2,1)S(1)} %collective-permute-done.24.refs_1_.taken, bf16[128,128]{1,0:T(8,128)(2,1)S(1)} %get-tuple-element.73.maps, ...), custom_call_target="tpu_custom_call" | custom-call | flops 4294967296 | bytes 1048576 | tf_op jit(solution)/shard_map/pallas_call | solution.py:54
  117.7 1.9 %collective-permute-start.40 = (bf16[512,256]{1,0:T(8,128)(2,1)S(1)}, bf16[512,256]{1,0:T(8,128)(2,1)S(1)}, u32[]{:S(2)}, u32[]{:S(2)}) collective-permute-start(bf16[512,256]{1,0:T(8,128)(2,1)S(1)} %collective-permute-done.37.far), channel_id=1, source_target_pairs={{0,128},{128,0},{1,129},{129,1},{2,130},{130,2},{3,131},{131,3},{4... | collective-permute-start | bytes 786440 | tf_op jit(solution)/shard_map/ppermute | solution.py:25
  121.0 2.4 %shard_map.115 = f32[32,8,128]{2,1,0:T(8,128)} custom-call(s32[4]{0:T(128)S(1)} %pad_add_fusion.where, bf16[128,128]{1,0:T(8,128)(2,1)S(1)} %get-tuple-element.92.query, bf16[128,128]{1,0:T(8,128)(2,1)S(1)} %get-tuple-element.73.maps, bf16[128,128]{1,0:T(8,128)(2,1)S(1)} %collective-permute-done.15.maps_g, f32[32,8,128]{2,1,0:T(8,128)S(1)} %get-tuple-element.102.keep, ...), custom_call_target="tpu_custom_call" | custom-call | flops 1073741824 | bytes 1048576 | tf_op jit(solution)/shard_map/pallas_call | solution.py:54
  123.5 4.6 %all-to-all-start = ((f32[32,8,128]{2,1,0:T(8,128)}), f32[32,8,128]{2,1,0:T(8,128)S(1)}, u32[]{:S(2)}, u32[]{:S(2)}) async-start(f32[32,8,128]{2,1,0:T(8,128)} %shard_map.115), calls=%async_computation | async-start | bytes 262144 | tf_op jit(solution)/shard_map/all_to_all | solution.py:495
  128.4 9.1 %all-to-all-done = f32[32,8,128]{2,1,0:T(8,128)S(1)} async-done(((f32[32,8,128]{2,1,0:T(8,128)}), f32[32,8,128]{2,1,0:T(8,128)S(1)}, u32[]{:S(2)}, u32[]{:S(2)}) %all-to-all-start) | async-done | bytes 131104 | tf_op jit(solution)/shard_map/all_to_all | solution.py:495
  137.7 2.1 %collective-permute-start.41 = (f32[16,64]{1,0:T(8,128)S(1)}, f32[16,64]{1,0:T(8,128)S(1)}, u32[]{:S(2)}, u32[]{:S(2)}) collective-permute-start(f32[16,64]{1,0:T(8,128)S(1)} %fusion.1), channel_id=1, source_target_pairs={{0,128},{128,0},{1,129},{129,1},{2,130},{130,2},{3,131},{131,3},{4... | collective-permute-start | bytes 12296 | tf_op jit(solution)/shard_map/ppermute | solution.py:25
  (114 shorter events, 32.8 us)
Async XLA Ops:
  0.0 5.2 %collective-permute-start.2 = (bf16[48,5120]{1,0:T(8,128)(2,1)}, bf16[48,5120]{1,0:T(8,128)(2,1)S(1)}, u32[]{:S(2)}, u32[]{:S(2)}) collective-permute-start(bf16[48,5120]{1,0:T(8,128)(2,1)} %bitcast.10), channel_id=1, source_target_pairs={{0,128},{128,0},{1,129},{129,1},{2,130},{130,2},{3,131},{131,3},{4... | collective-permute-start | bytes 1474568 | tf_op jit(solution)/shard_map/ppermute | solution.py:25
  3.2 19.2 %collective-permute-start.6 = (bf16[48,5120]{1,0:T(8,128)(2,1)}, bf16[48,5120]{1,0:T(8,128)(2,1)}, u32[]{:S(2)}, u32[]{:S(2)}) collective-permute-start(bf16[48,5120]{1,0:T(8,128)(2,1)} %bitcast.11), channel_id=1, source_target_pairs={{0,4},{4,0},{8,12},{12,8},{1,5},{5,1},{9,13},{13,9},{2,6},{6,2},{1... | collective-permute-start | bytes 1474568 | tf_op jit(solution)/shard_map/ppermute | solution.py:25
  6.9 22.5 %collective-permute-start.5 = (bf16[96,5120]{1,0:T(8,128)(2,1)S(1)}, bf16[96,5120]{1,0:T(8,128)(2,1)S(1)}, u32[]{:S(2)}, u32[]{:S(2)}) collective-permute-start(bf16[96,5120]{1,0:T(8,128)(2,1)S(1)} %shard_map.101.w0), channel_id=1, source_target_pairs={{0,1},{1,2},{2,3},{3,0},{128,131},{129,128},{130,129},{131,130},{4... | collective-permute-start | bytes 2949128 | tf_op jit(solution)/shard_map/ppermute | solution.py:40
  9.2 9.4 %collective-permute-start = (bf16[16,5120]{1,0:T(8,128)(2,1)S(1)}, bf16[16,5120]{1,0:T(8,128)(2,1)S(1)}, u32[]{:S(2)}, u32[]{:S(2)}) collective-permute-start(bf16[16,5120]{1,0:T(8,128)(2,1)S(1)} %copy-done.5), channel_id=1, source_target_pairs={{0,12},{12,0},{4,8},{8,4},{1,13},{13,1},{5,9},{9,5},{2,14},{14,2},... | collective-permute-start | bytes 491528 | tf_op jit(solution)/shard_map/ppermute | solution.py:33
  11.0 7.6 %collective-permute-start.1 = (bf16[64,768]{1,0:T(8,128)(2,1)S(1)}, bf16[64,768]{1,0:T(8,128)(2,1)S(1)}, u32[]{:S(2)}, u32[]{:S(2)}) collective-permute-start(bf16[64,768]{1,0:T(8,128)(2,1)S(1)} %copy-done.6), channel_id=1, source_target_pairs={{0,16},{16,32},{32,48},{48,64},{64,80},{80,96},{96,112},{112,0},{1... | collective-permute-start | bytes 294920 | tf_op jit(solution)/shard_map/ppermute | solution.py:40
  16.7 5.5 %collective-permute-start.3 = (bf16[48,512]{1,0:T(8,128)(2,1)S(1)}, bf16[48,512]{1,0:T(8,128)(2,1)}, u32[]{:S(2)}, u32[]{:S(2)}) collective-permute-start(bf16[48,512]{1,0:T(8,128)(2,1)S(1)} %pad_maximum_fusion.3), channel_id=1, source_target_pairs={{16,128},{48,160},{80,192},{112,224},{128,16},{160,48},{192,80},{2... | collective-permute-start | bytes 147464 | tf_op jit(solution)/shard_map/ppermute | solution.py:351
  22.5 4.6 %collective-permute-start.8 = (bf16[48,5120]{1,0:T(8,128)(2,1)}, bf16[48,5120]{1,0:T(8,128)(2,1)}, u32[]{:S(2)}, u32[]{:S(2)}) collective-permute-start(bf16[48,5120]{1,0:T(8,128)(2,1)} %collective-permute-done.6.refs_0_), channel_id=1, source_target_pairs={{0,128},{128,0},{1,129},{129,1},{2,130},{130,2},{3,131},{131,3},{4... | collective-permute-start | bytes 1474568 | tf_op jit(solution)/shard_map/ppermute | solution.py:25
  22.6 6.8 %collective-permute-start.4 = (bf16[32,5888]{1,0:T(8,128)(2,1)S(1)}, bf16[32,5888]{1,0:T(8,128)(2,1)S(1)}, u32[]{:S(2)}, u32[]{:S(2)}) collective-permute-start(bf16[32,5888]{1,0:T(8,128)(2,1)S(1)} %shard_map.102.near), channel_id=1, source_target_pairs={{0,16},{16,32},{32,48},{48,64},{64,80},{80,96},{96,112},{112,0},{1... | collective-permute-start | bytes 1130504 | tf_op jit(solution)/shard_map/ppermute | solution.py:40
  22.7 5.8 %collective-permute-start.7 = (bf16[16,5120]{1,0:T(8,128)(2,1)}, bf16[16,5120]{1,0:T(8,128)(2,1)S(1)}, u32[]{:S(2)}, u32[]{:S(2)}) collective-permute-start(bf16[16,5120]{1,0:T(8,128)(2,1)} %copy-done.4), channel_id=1, source_target_pairs={{0,128},{128,0},{1,129},{129,1},{2,130},{130,2},{3,131},{131,3},{4... | collective-permute-start | bytes 491528 | tf_op jit(solution)/shard_map/ppermute | solution.py:25
  23.9 4.5 %collective-permute-start.9 = (bf16[48,512]{1,0:T(8,128)(2,1)S(1)}, bf16[48,512]{1,0:T(8,128)(2,1)S(1)}, u32[]{:S(2)}, u32[]{:S(2)}) collective-permute-start(bf16[48,512]{1,0:T(8,128)(2,1)S(1)} %broadcast_select_fusion), channel_id=1, source_target_pairs={{0,12},{12,0},{4,8},{8,4},{1,13},{13,1},{5,9},{9,5},{2,14},{14,2},... | collective-permute-start | bytes 147464 | tf_op jit(solution)/shard_map/ppermute | solution.py:33
  29.4 14.4 %collective-permute-start.11 = (bf16[96,5120]{1,0:T(8,128)(2,1)S(1)}, bf16[96,5120]{1,0:T(8,128)(2,1)S(1)}, u32[]{:S(2)}, u32[]{:S(2)}) collective-permute-start(bf16[96,5120]{1,0:T(8,128)(2,1)S(1)} %collective-permute-done.5.refs_0_.y1), channel_id=1, source_target_pairs={{0,128},{128,0},{1,129},{129,1},{2,130},{130,2},{3,131},{131,3},{4... | collective-permute-start | bytes 2949128 | tf_op jit(solution)/shard_map/ppermute | solution.py:25
  31.9 13.2 %collective-permute-start.12 = (bf16[96,5120]{1,0:T(8,128)(2,1)S(1)}, bf16[96,5120]{1,0:T(8,128)(2,1)S(1)}, u32[]{:S(2)}, u32[]{:S(2)}) collective-permute-start(bf16[96,5120]{1,0:T(8,128)(2,1)S(1)} %shard_map.103.pr), channel_id=1, source_target_pairs={{0,1},{1,2},{2,3},{3,0},{128,131},{129,128},{130,129},{131,130},{4... | collective-permute-start | bytes 2949128 | tf_op jit(solution)/shard_map/ppermute | solution.py:40
  33.0 10.9 %collective-permute-start.10 = (bf16[64,5888]{1,0:T(8,128)(2,1)S(1)}, bf16[64,5888]{1,0:T(8,128)(2,1)S(1)}, u32[]{:S(2)}, u32[]{:S(2)}) collective-permute-start(bf16[64,5888]{1,0:T(8,128)(2,1)S(1)} %shard_map.105), channel_id=1, source_target_pairs={{0,16},{16,32},{32,48},{48,64},{64,80},{80,96},{96,112},{112,0},{1... | collective-permute-start | bytes 2261000 | tf_op jit(solution)/shard_map/ppermute | solution.py:40
  33.5 4.3 %collective-permute-start.13 = (bf16[48,1024]{1,0:T(8,128)(2,1)S(1)}, bf16[48,1024]{1,0:T(8,128)(2,1)S(1)}, u32[]{:S(2)}, u32[]{:S(2)}) collective-permute-start(bf16[48,1024]{1,0:T(8,128)(2,1)S(1)} %pad_maximum_fusion.2), channel_id=1, source_target_pairs={{0,4},{4,0},{8,12},{12,8},{1,5},{5,1},{9,13},{13,9},{2,6},{6,2},{1... | collective-permute-start | bytes 294920 | tf_op jit(solution)/shard_map/ppermute | solution.py:25
  45.1 12.9 %collective-permute-start.17 = (bf16[96,5120]{1,0:T(8,128)(2,1)S(1)}, bf16[96,5120]{1,0:T(8,128)(2,1)S(1)}, u32[]{:S(2)}, u32[]{:S(2)}) collective-permute-start(bf16[96,5120]{1,0:T(8,128)(2,1)S(1)} %collective-permute-done.12.refs_1_.y2), channel_id=1, source_target_pairs={{0,128},{128,0},{1,129},{129,1},{2,130},{130,2},{3,131},{131,3},{4... | collective-permute-start | bytes 2949128 | tf_op jit(solution)/shard_map/ppermute | solution.py:25
  47.2 10.8 %collective-permute-start.16 = (bf16[64,5888]{1,0:T(8,128)(2,1)S(1)}, bf16[64,5888]{1,0:T(8,128)(2,1)S(1)}, u32[]{:S(2)}, u32[]{:S(2)}) collective-permute-start(bf16[64,5888]{1,0:T(8,128)(2,1)S(1)} %collective-permute-done.10.refs_1_.z2), channel_id=1, source_target_pairs={{0,16},{16,32},{32,48},{48,64},{64,80},{80,96},{96,112},{112,0},{1... | collective-permute-start | bytes 2261000 | tf_op jit(solution)/shard_map/ppermute | solution.py:40
  48.0 17.7 %collective-permute-start.19 = (bf16[48,14336]{1,0:T(8,128)(2,1)S(1)}, bf16[48,14336]{1,0:T(8,128)(2,1)S(1)}, u32[]{:S(2)}, u32[]{:S(2)}) collective-permute-start(bf16[48,14336]{1,0:T(8,128)(2,1)S(1)} %shard_map.106), channel_id=1, source_target_pairs={{0,1},{1,2},{2,3},{3,0},{128,131},{129,128},{130,129},{131,130},{4... | collective-permute-start | bytes 4128776 | tf_op jit(solution)/shard_map/ppermute | solution.py:40
  58.0 10.8 %collective-permute-start.18 = (bf16[64,5888]{1,0:T(8,128)(2,1)S(1)}, bf16[64,5888]{1,0:T(8,128)(2,1)S(1)}, u32[]{:S(2)}, u32[]{:S(2)}) collective-permute-start(bf16[64,5888]{1,0:T(8,128)(2,1)S(1)} %collective-permute-done.16.refs_2_.z3), channel_id=1, source_target_pairs={{0,16},{16,32},{32,48},{48,64},{64,80},{80,96},{96,112},{112,0},{1... | collective-permute-start | bytes 2261000 | tf_op jit(solution)/shard_map/ppermute | solution.py:40
  68.8 7.9 %collective-permute-start.21 = (bf16[48,14336]{1,0:T(8,128)(2,1)S(1)}, bf16[48,14336]{1,0:T(8,128)(2,1)S(1)}, u32[]{:S(2)}, u32[]{:S(2)}) collective-permute-start(bf16[48,14336]{1,0:T(8,128)(2,1)S(1)} %collective-permute-done.19.refs_0_.yz), channel_id=1, source_target_pairs={{0,128},{128,0},{1,129},{129,1},{2,130},{130,2},{3,131},{131,3},{4... | collective-permute-start | bytes 4128776 | tf_op jit(solution)/shard_map/ppermute | solution.py:25
  72.9 6.1 %collective-permute-start.22 = (bf16[48,2048]{1,0:T(8,128)(2,1)S(1)}, bf16[48,2048]{1,0:T(8,128)(2,1)S(1)}, u32[]{:S(2)}, u32[]{:S(2)}) collective-permute-start(bf16[48,2048]{1,0:T(8,128)(2,1)S(1)} %shard_map.108), channel_id=1, source_target_pairs={{0,1},{1,2},{2,3},{3,0},{128,131},{129,128},{130,129},{131,130},{4... | collective-permute-start | bytes 589832 | tf_op jit(solution)/shard_map/ppermute | solution.py:40
  79.9 6.5 %collective-permute-start.24 = (bf16[256,384]{1,0:T(8,128)(2,1)S(1)}, bf16[256,384]{1,0:T(8,128)(2,1)S(1)}, u32[]{:S(2)}, u32[]{:S(2)}) collective-permute-start(bf16[256,384]{1,0:T(8,128)(2,1)S(1)} %get-tuple-element.89), channel_id=1, source_target_pairs={{0,4},{4,0},{8,12},{12,8},{1,5},{5,1},{9,13},{13,9},{2,6},{6,2},{1... | collective-permute-start | bytes 589832 | tf_op jit(solution)/shard_map/ppermute | solution.py:25
  82.9 4.3 %collective-permute-start.26 = (bf16[256,384]{1,0:T(8,128)(2,1)S(1)}, bf16[256,384]{1,0:T(8,128)(2,1)S(1)}, u32[]{:S(2)}, u32[]{:S(2)}) collective-permute-start(bf16[256,384]{1,0:T(8,128)(2,1)S(1)} %get-tuple-element.94.refs_0_.kept), channel_id=1, source_target_pairs={{0,128},{128,0},{1,129},{129,1},{2,130},{130,2},{3,131},{131,3},{4... | collective-permute-start | bytes 589832 | tf_op jit(solution)/shard_map/ppermute | solution.py:25
  88.4 12.4 %collective-permute-start.28 = (bf16[1024,256]{1,0:T(8,128)(2,1)S(1)}, bf16[1024,256]{1,0:T(8,128)(2,1)S(1)}, u32[]{:S(2)}, u32[]{:S(2)}) collective-permute-start(bf16[1024,256]{1,0:T(8,128)(2,1)S(1)} %shard_map.112.own), channel_id=1, source_target_pairs={{0,1},{1,2},{2,3},{3,0},{128,131},{129,128},{130,129},{131,130},{4... | collective-permute-start | bytes 1572872 | tf_op jit(solution)/shard_map/ppermute | solution.py:40
  89.5 4.1 %collective-permute-start.29 = (bf16[256,256]{1,0:T(8,128)(2,1)S(1)}, bf16[256,256]{1,0:T(8,128)(2,1)S(1)}, u32[]{:S(2)}, u32[]{:S(2)}) collective-permute-start(bf16[256,256]{1,0:T(8,128)(2,1)S(1)} %pad_maximum_fusion.1), channel_id=1, source_target_pairs={{0,4},{4,8},{8,12},{12,0},{128,140},{132,128},{136,132},{140,136},... | collective-permute-start | bytes 393224 | tf_op jit(solution)/shard_map/ppermute | solution.py:40
  90.6 5.9 %collective-permute-start.31 = (bf16[128,256]{1,0:T(8,128)(2,1)S(1)}, bf16[128,256]{1,0:T(8,128)(2,1)S(1)}, u32[]{:S(2)}, u32[]{:S(2)}) collective-permute-start(bf16[128,256]{1,0:T(8,128)(2,1)S(1)} %get-tuple-element.95.refs_0_), channel_id=1, source_target_pairs={{0,8},{4,12},{8,0},{12,4},{1,9},{5,13},{9,1},{13,5},{2,10},{6,14},... | collective-permute-start | bytes 196616 | tf_op jit(solution)/shard_map/ppermute | solution.py:25
  93.7 4.1 %collective-permute-start.30 = (bf16[256,256]{1,0:T(8,128)(2,1)S(1)}, bf16[256,256]{1,0:T(8,128)(2,1)S(1)}, u32[]{:S(2)}, u32[]{:S(2)}) collective-permute-start(bf16[256,256]{1,0:T(8,128)(2,1)S(1)} %collective-permute-done.29.refs_1_.refs_5_), channel_id=1, source_target_pairs={{0,128},{128,0},{1,129},{129,1},{2,130},{130,2},{3,131},{131,3},{4... | collective-permute-start | bytes 393224 | tf_op jit(solution)/shard_map/ppermute | solution.py:25
  98.5 8.4 %collective-permute-start.35 = (bf16[1024,256]{1,0:T(8,128)(2,1)S(1)}, bf16[1024,256]{1,0:T(8,128)(2,1)S(1)}, u32[]{:S(2)}, u32[]{:S(2)}) collective-permute-start(bf16[1024,256]{1,0:T(8,128)(2,1)S(1)} %shard_map.113.own), channel_id=1, source_target_pairs={{0,1},{1,2},{2,3},{3,0},{128,131},{129,128},{130,129},{131,130},{4... | collective-permute-start | bytes 1572872 | tf_op jit(solution)/shard_map/ppermute | solution.py:40
  100.8 8.9 %collective-permute-start.34 = (bf16[512,256]{1,0:T(8,128)(2,1)S(1)}, bf16[512,256]{1,0:T(8,128)(2,1)S(1)}, u32[]{:S(2)}, u32[]{:S(2)}) collective-permute-start(bf16[512,256]{1,0:T(8,128)(2,1)S(1)} %slice.24), channel_id=1, source_target_pairs={{0,1},{1,2},{2,3},{3,0},{128,131},{129,128},{130,129},{131,130},{4... | collective-permute-start | bytes 786440 | tf_op jit(solution)/shard_map/ppermute | solution.py:40
  101.3 11.9 %collective-permute-start.33 = (bf16[1024,256]{1,0:T(8,128)(2,1)S(1)}, bf16[1024,256]{1,0:T(8,128)(2,1)S(1)}, u32[]{:S(2)}, u32[]{:S(2)}) collective-permute-start(bf16[1024,256]{1,0:T(8,128)(2,1)S(1)} %collective-permute-done.28.side), channel_id=1, source_target_pairs={{0,128},{128,0},{1,129},{129,1},{2,130},{130,2},{3,131},{131,3},{4... | collective-permute-start | bytes 1572872 | tf_op jit(solution)/shard_map/ppermute | solution.py:25
  112.0 5.7 %collective-permute-start.37 = (bf16[512,256]{1,0:T(8,128)(2,1)S(1)}, bf16[512,256]{1,0:T(8,128)(2,1)S(1)}, u32[]{:S(2)}, u32[]{:S(2)}) collective-permute-start(bf16[512,256]{1,0:T(8,128)(2,1)S(1)} %slice.28), channel_id=1, source_target_pairs={{0,1},{1,2},{2,3},{3,0},{128,131},{129,128},{130,129},{131,130},{4... | collective-permute-start | bytes 786440 | tf_op jit(solution)/shard_map/ppermute | solution.py:40
  113.0 6.6 %collective-permute-start.39 = (bf16[1024,256]{1,0:T(8,128)(2,1)S(1)}, bf16[1024,256]{1,0:T(8,128)(2,1)S(1)}, u32[]{:S(2)}, u32[]{:S(2)}) collective-permute-start(bf16[1024,256]{1,0:T(8,128)(2,1)S(1)} %collective-permute-done.35.side), channel_id=1, source_target_pairs={{0,128},{128,0},{1,129},{129,1},{2,130},{130,2},{3,131},{131,3},{4... | collective-permute-start | bytes 1572872 | tf_op jit(solution)/shard_map/ppermute | solution.py:25
  123.5 14.0 %all-to-all-start = ((f32[32,8,128]{2,1,0:T(8,128)}), f32[32,8,128]{2,1,0:T(8,128)S(1)}, u32[]{:S(2)}, u32[]{:S(2)}) async-start(f32[32,8,128]{2,1,0:T(8,128)} %shard_map.115), calls=%async_computation | async-start | bytes 262144 | tf_op jit(solution)/shard_map/all_to_all | solution.py:495
  (26 other events, 264.3 us)

commit v4 on v3

--- a/solution.py
+++ b/solution.py
@@ -229,58 +229,68 @@
     kept[...] = ordered(jnp.where(mine, first, second), order)
 
 
-def attend(query, pairs, scores):
-    top = None
-    start = 0
-    for ref, first, last in pairs:
-        for lo in range(first, last, 512):
-            count = 512
-            block = dot_t(query, ref[lo : lo + count, :HD])
-            scores[:, start : start + count] = block
-            for at in range(0, count, 128):
-                part = block[:, at : at + 128]
-                top = part if top is None else jnp.maximum(top, part)
-            start += count
-    biggest = jnp.max(top, axis=1, keepdims=True)
-    total, mixed = None, None
-    start = 0
-    for ref, first, last in pairs:
-        for lo in range(first, last, 512):
-            count = 512
-            block = scores[:, start : start + count]
-            weights = jnp.exp2((block - biggest) * (HD**-0.5 * LOG2E))
-            for at in range(0, count, 128):
-                part = weights[:, at : at + 128]
-                total = part if total is None else total + part
-            values = ref[lo : lo + count, HD:]
-            term = jnp.dot(weights.astype(BF), values, preferred_element_type=F32)
-            mixed = term if mixed is None else mixed + term
-            start += count
-    return (mixed / jnp.sum(total, axis=1, keepdims=True)).astype(BF)
+def spots(pairs):
+    return [(ref, lo) for ref, first, last in pairs for lo in range(first, last, 512)]
+
+
+def score(query, spot, scores, start, top):
+    ref, lo = spot
+    block = dot_t(query, ref[lo : lo + 512, :HD])
+    scores[:, start : start + 512] = block
+    for at in range(0, 512, 128):
+        part = block[:, at : at + 128]
+        top = part if top is None else jnp.maximum(top, part)
+    return top
+
+
+def weigh(spot, scores, start, biggest, total, mixed):
+    ref, lo = spot
+    block = scores[:, start : start + 512]
+    weights = jnp.exp2((block - biggest) * (HD**-0.5 * LOG2E))
+    for at in range(0, 512, 128):
+        part = weights[:, at : at + 128]
+        total = part if total is None else total + part
+    term = jnp.dot(weights.astype(BF), ref[lo : lo + 512, HD:], preferred_element_type=F32)
+    return total, term if mixed is None else mixed + term
+
+
+def attend(tiles, pairs, scores):
+    places = spots(pairs)
+    tops = [None] * len(tiles)
+    for i, spot in enumerate(places):
+        tops[0] = score(tiles[0], spot, scores[0], 512 * i, tops[0])
+    done = []
+    for t in range(len(tiles)):
+        biggest = jnp.max(tops[t], axis=1, keepdims=True)
+        total, mixed = None, None
+        for i, spot in enumerate(places):
+            total, mixed = weigh(spot, scores[t], 512 * i, biggest, total, mixed)
+            if t + 1 < len(tiles):
+                tops[t + 1] = score(tiles[t + 1], spot, scores[t + 1], 512 * i, tops[t + 1])
+        done.append((mixed / jnp.sum(total, axis=1, keepdims=True)).astype(BF))
+    return done
 
 
 def large_body(
     where, kept, taken, maps, maps_g, own, side, side_g, far, far_g,
-    keep, send, scores, query,
+    keep, send, scores_0, scores_1,
 ):
     pairs = ((own, 0, 1024), (side, 0, 1024), (side_g, 0, 1024), (far, 0, 512), (far_g, 0, 512))
     core, z, x = where[0], where[1], where[2]
     way = 2 * core - 1
     keep[...] = jnp.zeros_like(keep)
     send[...] = jnp.zeros_like(send)
-    query[:256, :] = kept[:, :HD]
-    query[256:, :] = taken[:, :HD]
     map_left, map_right = sides(core == x % 2, maps[:64, :], maps_g[:64, :])
 
-    @pl.loop(0, 2)
-    def _(s):
-        done = attend(query[pl.ds(pl.multiple_of(s * 256, 256), 256), :], pairs, scores)
+    tiles = attend((kept[:, :HD], taken[:, :HD]), pairs, (scores_0, scores_1))
+
+    def chip(step, x_at):
+        return (z + 8 + step) % 8 * 4 + x_at
+
+    for s, done in enumerate(tiles):
         left = GUIDANCE * dot_t(done, map_left)
         right = GUIDANCE * dot_t(done, map_right)
         x_own = x ^ s
-
-        def chip(step, x_at):
-            return (z + 8 + step) % 8 * 4 + x_at
 
         def folded(row):
             return left[row : row + 8] + right[row + 8 : row + 16]
@@ -299,7 +309,7 @@
     pairs = ((own, 0, 1024), (side, 0, 1024), (side_g, 0, 1024), (far, 0, 512), (far_g, 0, 512))
     core, z_at, x = where[0], where[1], where[2]
     map_left, map_right = sides(core == z_at % 2, maps[64:, :], maps_g[64:, :])
-    done = attend(query[...], pairs, scores)
+    (done,) = attend((query[...],), pairs, (scores,))
     left = (1.0 - GUIDANCE) * dot_t(done, map_left)
     right = (1.0 - GUIDANCE) * dot_t(done, map_right)
     out[...] = keep[...] + got[...]
@@ -478,7 +488,7 @@
         large_body,
         [((32, 8, 128), F32)] * 2,
         (where, kept, taken, maps, maps_g, all_l, k_side, k_side_g, k_far, k_far_g),
-        [pltpu.VMEM((256, 4096), F32), pltpu.VMEM((512, HD), BF)],
+        [pltpu.VMEM((256, 4096), F32)] * 2,
         flops=2**32,
     )
     keep, send, s_far = tie(keep, send, s_far)

time: 142 us -> 142 us (level)
  transfers between devices with their start and end apart: 43 -> 43, of which waited for: 22 -> 23; matrix products, arithmetic and copies ran while one was open for 1% -> 1% of each run, Pallas kernels for 12% -> 12%
where the time goes in v4:
time: 142 us; the launch traced here: 141 us
  waiting for transfers between devices  61.6 us (43%)
  starting transfers between devices  56.1 us (40%)
  Pallas kernels  19 us (13%)
  local copies, waits for them, and re-layouts  2.15 us (2%)
  other arithmetic  1.57 us (1%)
    ppermute x14, waiting for transfers between devices, spread(): return lax.ppermute(block, ('grp', axis), pairs)  34.1 us
    ppermute x25, starting transfers between devices, flip(): return lax.ppermute(block, axis, [(i, i ^ mask) for i in range(count)])  27 us
    ppermute x14, starting transfers between devices, spread(): return lax.ppermute(block, ('grp', axis), pairs)  19.3 us
    pallas_call x7, Pallas kernels, call(): pl.pallas_call(body, out_shape=[jax.ShapeDtypeStruct(shape, dtype) for sh...  15.3 us
    ppermute x25, waiting for transfers between devices, flip(): return lax.ppermute(block, axis, [(i, i ^ mask) for i in range(count)])  14.8 us
    all_to_all x1, waiting for transfers between devices, shards(): lax.all_to_all(total, ('z', 'x'), split_axis=0, concat_axis=0, tiled=True)  9.06 us
    all_to_all x1, starting transfers between devices, shards(): lax.all_to_all(total, ('z', 'x'), split_axis=0, concat_axis=0, tiled=True)  4.62 us
    pallas_call x9, Pallas kernels, pack(): pl.pallas_call(body, out_shape=jax.ShapeDtypeStruct(shape, BF), in_specs=...  3.71 us
  transfers between devices with their start and end apart: 43, of which 23 were waited for; matrix products, arithmetic and copies ran while one was open for 1% of the time, Pallas kernels for 12%

profile of v4, /device:TPU:1, one launch (start us, length us, event | category | flops | bytes accessed | tf_op | source)
XLA Modules:
  0.0 141.3 jit_solution(17336145862105623433)
XLA Ops:
  0.0 3.2 %collective-permute-start.2 = (bf16[48,5120]{1,0:T(8,128)(2,1)}, bf16[48,5120]{1,0:T(8,128)(2,1)S(1)}, u32[]{:S(2)}, u32[]{:S(2)}) collective-permute-start(bf16[48,5120]{1,0:T(8,128)(2,1)} %bitcast.10), channel_id=1, source_target_pairs={{0,128},{128,0},{1,129},{129,1},{2,130},{130,2},{3,131},{131,3},{4... | collective-permute-start | bytes 1474568 | tf_op jit(solution)/shard_map/ppermute | solution.py:25
  3.2 2.0 %shard_map.100 = (bf16[16,5120]{1,0:T(8,128)(2,1)}, bf16[16,5120]{1,0:T(8,128)(2,1)}, bf16[64,768]{1,0:T(8,128)(2,1)}) custom-call(bf16[32,5120]{1,0:T(8,128)(2,1)} %large.1, bf16[32,1536]{1,0:T(8,128)(2,1)} %small.1, f32[5120]{0:T(1024)} %gain_l.1, f32[1536]{0:T(1024)} %gain_s.1), custom_call_target="tpu_custom_call" | custom-call | bytes 1048576 | tf_op jit(solution)/shard_map/pallas_call | solution.py:54
  6.9 2.3 %collective-permute-start.5 = (bf16[96,5120]{1,0:T(8,128)(2,1)S(1)}, bf16[96,5120]{1,0:T(8,128)(2,1)S(1)}, u32[]{:S(2)}, u32[]{:S(2)}) collective-permute-start(bf16[96,5120]{1,0:T(8,128)(2,1)S(1)} %shard_map.101.w0), channel_id=1, source_target_pairs={{0,1},{1,2},{2,3},{3,0},{128,131},{129,128},{130,129},{131,130},{4... | collective-permute-start | bytes 2949128 | tf_op jit(solution)/shard_map/ppermute | solution.py:40
  9.2 1.8 %collective-permute-start = (bf16[16,5120]{1,0:T(8,128)(2,1)S(1)}, bf16[16,5120]{1,0:T(8,128)(2,1)S(1)}, u32[]{:S(2)}, u32[]{:S(2)}) collective-permute-start(bf16[16,5120]{1,0:T(8,128)(2,1)S(1)} %copy-done.5), channel_id=1, source_target_pairs={{0,12},{12,0},{4,8},{8,4},{1,13},{13,1},{5,9},{9,5},{2,14},{14,2},... | collective-permute-start | bytes 491528 | tf_op jit(solution)/shard_map/ppermute | solution.py:33
  11.0 5.6 %collective-permute-start.1 = (bf16[64,768]{1,0:T(8,128)(2,1)S(1)}, bf16[64,768]{1,0:T(8,128)(2,1)S(1)}, u32[]{:S(2)}, u32[]{:S(2)}) collective-permute-start(bf16[64,768]{1,0:T(8,128)(2,1)S(1)} %copy-done.6), channel_id=1, source_target_pairs={{0,16},{16,32},{32,48},{48,64},{64,80},{80,96},{96,112},{112,0},{1... | collective-permute-start | bytes 294920 | tf_op jit(solution)/shard_map/ppermute | solution.py:40
  16.7 1.9 %collective-permute-start.3 = (bf16[48,512]{1,0:T(8,128)(2,1)S(1)}, bf16[48,512]{1,0:T(8,128)(2,1)}, u32[]{:S(2)}, u32[]{:S(2)}) collective-permute-start(bf16[48,512]{1,0:T(8,128)(2,1)S(1)} %pad_maximum_fusion.3), channel_id=1, source_target_pairs={{16,128},{48,160},{80,192},{112,224},{128,16},{160,48},{192,80},{2... | collective-permute-start | bytes 147464 | tf_op jit(solution)/shard_map/ppermute | solution.py:361
  18.6 3.6 %collective-permute-done.3 = bf16[48,512]{1,0:T(8,128)(2,1)} collective-permute-done((bf16[48,512]{1,0:T(8,128)(2,1)S(1)}, bf16[48,512]{1,0:T(8,128)(2,1)}, u32[]{:S(2)}, u32[]{:S(2)}) %collective-permute-start.3) | collective-permute-done | bytes 49184 | tf_op jit(solution)/shard_map/ppermute | solution.py:361
  29.4 2.5 %collective-permute-start.11 = (bf16[96,5120]{1,0:T(8,128)(2,1)S(1)}, bf16[96,5120]{1,0:T(8,128)(2,1)S(1)}, u32[]{:S(2)}, u32[]{:S(2)}) collective-permute-start(bf16[96,5120]{1,0:T(8,128)(2,1)S(1)} %collective-permute-done.5.refs_0_.y1), channel_id=1, source_target_pairs={{0,128},{128,0},{1,129},{129,1},{2,130},{130,2},{3,131},{131,3},{4... | collective-permute-start | bytes 2949128 | tf_op jit(solution)/shard_map/ppermute | solution.py:25
  33.6 4.2 %collective-permute-done.13 = bf16[48,1024]{1,0:T(8,128)(2,1)S(1)} collective-permute-done((bf16[48,1024]{1,0:T(8,128)(2,1)S(1)}, bf16[48,1024]{1,0:T(8,128)(2,1)S(1)}, u32[]{:S(2)}, u32[]{:S(2)}) %collective-permute-start.13) | collective-permute-done | bytes 98336 | tf_op jit(solution)/shard_map/ppermute | solution.py:25
  39.4 4.4 %collective-permute-done.10.refs_1_.z2 = bf16[64,5888]{1,0:T(8,128)(2,1)S(1)} collective-permute-done((bf16[64,5888]{1,0:T(8,128)(2,1)S(1)}, bf16[64,5888]{1,0:T(8,128)(2,1)S(1)}, u32[]{:S(2)}, u32[]{:S(2)}) %collective-permute-start.10) | collective-permute-done | bytes 753696 | tf_op jit(solution)/shard_map/ppermute | solution.py:40
  45.1 2.1 %collective-permute-start.17 = (bf16[96,5120]{1,0:T(8,128)(2,1)S(1)}, bf16[96,5120]{1,0:T(8,128)(2,1)S(1)}, u32[]{:S(2)}, u32[]{:S(2)}) collective-permute-start(bf16[96,5120]{1,0:T(8,128)(2,1)S(1)} %collective-permute-done.12.refs_1_.y2), channel_id=1, source_target_pairs={{0,128},{128,0},{1,129},{129,1},{2,130},{130,2},{3,131},{131,3},{4... | collective-permute-start | bytes 2949128 | tf_op jit(solution)/shard_map/ppermute | solution.py:25
  48.7 9.2 %collective-permute-done.16.refs_2_.z3 = bf16[64,5888]{1,0:T(8,128)(2,1)S(1)} collective-permute-done((bf16[64,5888]{1,0:T(8,128)(2,1)S(1)}, bf16[64,5888]{1,0:T(8,128)(2,1)S(1)}, u32[]{:S(2)}, u32[]{:S(2)}) %collective-permute-start.16) | collective-permute-done | bytes 753696 | tf_op jit(solution)/shard_map/ppermute | solution.py:40
  58.0 1.7 %collective-permute-start.18 = (bf16[64,5888]{1,0:T(8,128)(2,1)S(1)}, bf16[64,5888]{1,0:T(8,128)(2,1)S(1)}, u32[]{:S(2)}, u32[]{:S(2)}) collective-permute-start(bf16[64,5888]{1,0:T(8,128)(2,1)S(1)} %collective-permute-done.16.refs_2_.z3), channel_id=1, source_target_pairs={{0,16},{16,32},{32,48},{48,64},{64,80},{80,96},{96,112},{112,0},{1... | collective-permute-start | bytes 2261000 | tf_op jit(solution)/shard_map/ppermute | solution.py:40
  61.3 4.4 %collective-permute-done.19.refs_0_.yz = bf16[48,14336]{1,0:T(8,128)(2,1)S(1)} collective-permute-done((bf16[48,14336]{1,0:T(8,128)(2,1)S(1)}, bf16[48,14336]{1,0:T(8,128)(2,1)S(1)}, u32[]{:S(2)}, u32[]{:S(2)}) %collective-permute-start.19) | collective-permute-done | bytes 1376288 | tf_op jit(solution)/shard_map/ppermute | solution.py:40
  65.7 3.1 %collective-permute-done.18.z4 = bf16[64,5888]{1,0:T(8,128)(2,1)S(1)} collective-permute-done((bf16[64,5888]{1,0:T(8,128)(2,1)S(1)}, bf16[64,5888]{1,0:T(8,128)(2,1)S(1)}, u32[]{:S(2)}, u32[]{:S(2)}) %collective-permute-start.18) | collective-permute-done | bytes 753696 | tf_op jit(solution)/shard_map/ppermute | solution.py:40
  68.8 4.1 %collective-permute-start.21 = (bf16[48,14336]{1,0:T(8,128)(2,1)S(1)}, bf16[48,14336]{1,0:T(8,128)(2,1)S(1)}, u32[]{:S(2)}, u32[]{:S(2)}) collective-permute-start(bf16[48,14336]{1,0:T(8,128)(2,1)S(1)} %collective-permute-done.19.refs_0_.yz), channel_id=1, source_target_pairs={{0,128},{128,0},{1,129},{129,1},{2,130},{130,2},{3,131},{131,3},{4... | collective-permute-start | bytes 4128776 | tf_op jit(solution)/shard_map/ppermute | solution.py:25
  74.1 2.5 %shard_map.109 = (bf16[384,256]{1,0:T(8,128)(2,1)S(1)}, bf16[288,256]{1,0:T(8,128)(2,1)S(1)}) custom-call(s32[4]{0:T(128)S(1)} %pad_add_fusion.where, bf16[32,5888]{1,0:T(8,128)(2,1)S(1)} %shard_map.102.near, bf16[32,5888]{1,0:T(8,128)(2,1)S(1)} %collective-permute-done.4.refs_0_.z1, bf16[64,5888]{1,0:T(8,128)(2,1)S(1)} %collective-permute-done.10.refs_1_.z2, ...), custom_call_target="tpu_custom_call" | custom-call | flops 4294967296 | bytes 1048576 | tf_op jit(solution)/shard_map/pallas_call | solution.py:54
  76.7 2.3 %shard_map.110 = (bf16[256,384]{1,0:T(8,128)(2,1)S(1)}, bf16[256,384]{1,0:T(8,128)(2,1)S(1)}) custom-call(s32[4]{0:T(128)S(1)} %pad_add_fusion.where, bf16[32,5888]{1,0:T(8,128)(2,1)S(1)} %shard_map.102.near, bf16[32,5888]{1,0:T(8,128)(2,1)S(1)} %collective-permute-done.4.refs_0_.z1, bf16[64,5888]{1,0:T(8,128)(2,1)S(1)} %collective-permute-done.10.refs_1_.z2, ...), custom_call_target="tpu_custom_call" | custom-call | flops 536870912 | bytes 1048576 | tf_op jit(solution)/shard_map/pallas_call | solution.py:54
  81.0 1.5 %shard_map.111 = (bf16[128,128]{1,0:T(8,128)(2,1)S(1)}, bf16[128,256]{1,0:T(8,128)(2,1)S(1)}) custom-call(s32[4]{0:T(128)S(1)} %pad_add_fusion.where, bf16[64,768]{1,0:T(8,128)(2,1)S(1)} %copy-done.7, bf16[64,768]{1,0:T(8,128)(2,1)S(1)} %collective-permute-done.1.refs_2_.refs_3_.refs_0_.s1, bf16[32,5888]{1,0:T(8,128)(2,1)S(1)} %collective-permute-done.4.refs_0_.z1, ...), custom_call_target="tpu_custom_call" | custom-call | flops 536870912 | bytes 1048576 | tf_op jit(solution)/shard_map/pallas_call | solution.py:54
  83.1 3.4 %collective-permute-done.24.refs_1_.taken = bf16[256,384]{1,0:T(8,128)(2,1)S(1)} collective-permute-done((bf16[256,384]{1,0:T(8,128)(2,1)S(1)}, bf16[256,384]{1,0:T(8,128)(2,1)S(1)}, u32[]{:S(2)}, u32[]{:S(2)}) %collective-permute-start.24) | collective-permute-done | bytes 196640 | tf_op jit(solution)/shard_map/ppermute | solution.py:25
  91.8 1.8 %collective-permute-done.29.refs_1_.refs_5_ = bf16[256,256]{1,0:T(8,128)(2,1)S(1)} collective-permute-done((bf16[256,256]{1,0:T(8,128)(2,1)S(1)}, bf16[256,256]{1,0:T(8,128)(2,1)S(1)}, u32[]{:S(2)}, u32[]{:S(2)}) %collective-permute-start.29) | collective-permute-done | bytes 131104 | tf_op jit(solution)/shard_map/ppermute | solution.py:40
  93.7 2.9 %collective-permute-start.30 = (bf16[256,256]{1,0:T(8,128)(2,1)S(1)}, bf16[256,256]{1,0:T(8,128)(2,1)S(1)}, u32[]{:S(2)}, u32[]{:S(2)}) collective-permute-start(bf16[256,256]{1,0:T(8,128)(2,1)S(1)} %collective-permute-done.29.refs_1_.refs_5_), channel_id=1, source_target_pairs={{0,128},{128,0},{1,129},{129,1},{2,130},{130,2},{3,131},{131,3},{4... | collective-permute-start | bytes 393224 | tf_op jit(solution)/shard_map/ppermute | solution.py:25
  98.5 2.2 %collective-permute-start.35 = (bf16[1024,256]{1,0:T(8,128)(2,1)S(1)}, bf16[1024,256]{1,0:T(8,128)(2,1)S(1)}, u32[]{:S(2)}, u32[]{:S(2)}) collective-permute-start(bf16[1024,256]{1,0:T(8,128)(2,1)S(1)} %shard_map.113.own), channel_id=1, source_target_pairs={{0,1},{1,2},{2,3},{3,0},{128,131},{129,128},{130,129},{131,130},{4... | collective-permute-start | bytes 1572872 | tf_op jit(solution)/shard_map/ppermute | solution.py:40
  101.4 5.5 %collective-permute-done.35.side = bf16[1024,256]{1,0:T(8,128)(2,1)S(1)} collective-permute-done((bf16[1024,256]{1,0:T(8,128)(2,1)S(1)}, bf16[1024,256]{1,0:T(8,128)(2,1)S(1)}, u32[]{:S(2)}, u32[]{:S(2)}) %collective-permute-start.35) | collective-permute-done | bytes 524320 | tf_op jit(solution)/shard_map/ppermute | solution.py:40
  106.9 2.8 %collective-permute-done.34.far = bf16[512,256]{1,0:T(8,128)(2,1)S(1)} collective-permute-done((bf16[512,256]{1,0:T(8,128)(2,1)S(1)}, bf16[512,256]{1,0:T(8,128)(2,1)S(1)}, u32[]{:S(2)}, u32[]{:S(2)}) %collective-permute-start.34) | collective-permute-done | bytes 262176 | tf_op jit(solution)/shard_map/ppermute | solution.py:40
  109.7 2.2 %collective-permute-start.36 = (bf16[512,256]{1,0:T(8,128)(2,1)S(1)}, bf16[512,256]{1,0:T(8,128)(2,1)S(1)}, u32[]{:S(2)}, u32[]{:S(2)}) collective-permute-start(bf16[512,256]{1,0:T(8,128)(2,1)S(1)} %collective-permute-done.34.far), channel_id=1, source_target_pairs={{0,128},{128,0},{1,129},{129,1},{2,130},{130,2},{3,131},{131,3},{4... | collective-permute-start | bytes 786440 | tf_op jit(solution)/shard_map/ppermute | solution.py:25
  113.2 3.8 %shard_map.114 = (f32[32,8,128]{2,1,0:T(8,128)S(1)}, f32[32,8,128]{2,1,0:T(8,128)S(1)}) custom-call(s32[4]{0:T(128)S(1)} %pad_add_fusion.where, bf16[256,384]{1,0:T(8,128)(2,1)S(1)} %get-tuple-element.94.refs_0_.kept, bf16[256,384]{1,0:T(8,128)(2,1)S(1)} %collective-permute-done.24.refs_1_.taken, bf16[128,128]{1,0:T(8,128)(2,1)S(1)} %get-tuple-element.73.maps, ...), custom_call_target="tpu_custom_call" | custom-call | flops 4294967296 | bytes 1048576 | tf_op jit(solution)/shard_map/pallas_call | solution.py:54
  117.6 2.1 %collective-permute-start.40 = (bf16[512,256]{1,0:T(8,128)(2,1)S(1)}, bf16[512,256]{1,0:T(8,128)(2,1)S(1)}, u32[]{:S(2)}, u32[]{:S(2)}) collective-permute-start(bf16[512,256]{1,0:T(8,128)(2,1)S(1)} %collective-permute-done.37.far), channel_id=1, source_target_pairs={{0,128},{128,0},{1,129},{129,1},{2,130},{130,2},{3,131},{131,3},{4... | collective-permute-start | bytes 786440 | tf_op jit(solution)/shard_map/ppermute | solution.py:25
  121.0 2.4 %shard_map.115 = f32[32,8,128]{2,1,0:T(8,128)} custom-call(s32[4]{0:T(128)S(1)} %pad_add_fusion.where, bf16[128,128]{1,0:T(8,128)(2,1)S(1)} %get-tuple-element.92.query, bf16[128,128]{1,0:T(8,128)(2,1)S(1)} %get-tuple-element.73.maps, bf16[128,128]{1,0:T(8,128)(2,1)S(1)} %collective-permute-done.15.maps_g, f32[32,8,128]{2,1,0:T(8,128)S(1)} %get-tuple-element.102.keep, ...), custom_call_target="tpu_custom_call" | custom-call | flops 1073741824 | bytes 1048576 | tf_op jit(solution)/shard_map/pallas_call | solution.py:54
  123.5 4.6 %all-to-all-start = ((f32[32,8,128]{2,1,0:T(8,128)}), f32[32,8,128]{2,1,0:T(8,128)S(1)}, u32[]{:S(2)}, u32[]{:S(2)}) async-start(f32[32,8,128]{2,1,0:T(8,128)} %shard_map.115), calls=%async_computation | async-start | bytes 262144 | tf_op jit(solution)/shard_map/all_to_all | solution.py:505
  128.4 9.1 %all-to-all-done = f32[32,8,128]{2,1,0:T(8,128)S(1)} async-done(((f32[32,8,128]{2,1,0:T(8,128)}), f32[32,8,128]{2,1,0:T(8,128)S(1)}, u32[]{:S(2)}, u32[]{:S(2)}) %all-to-all-start) | async-done | bytes 131104 | tf_op jit(solution)/shard_map/all_to_all | solution.py:505
  137.7 2.1 %collective-permute-start.41 = (f32[16,64]{1,0:T(8,128)S(1)}, f32[16,64]{1,0:T(8,128)S(1)}, u32[]{:S(2)}, u32[]{:S(2)}) collective-permute-start(f32[16,64]{1,0:T(8,128)S(1)} %fusion.1), channel_id=1, source_target_pairs={{0,128},{128,0},{1,129},{129,1},{2,130},{130,2},{3,131},{131,3},{4... | collective-permute-start | bytes 12296 | tf_op jit(solution)/shard_map/ppermute | solution.py:25
  (114 shorter events, 33.4 us)
Async XLA Ops:
  0.0 5.2 %collective-permute-start.2 = (bf16[48,5120]{1,0:T(8,128)(2,1)}, bf16[48,5120]{1,0:T(8,128)(2,1)S(1)}, u32[]{:S(2)}, u32[]{:S(2)}) collective-permute-start(bf16[48,5120]{1,0:T(8,128)(2,1)} %bitcast.10), channel_id=1, source_target_pairs={{0,128},{128,0},{1,129},{129,1},{2,130},{130,2},{3,131},{131,3},{4... | collective-permute-start | bytes 1474568 | tf_op jit(solution)/shard_map/ppermute | solution.py:25
  3.2 19.2 %collective-permute-start.6 = (bf16[48,5120]{1,0:T(8,128)(2,1)}, bf16[48,5120]{1,0:T(8,128)(2,1)}, u32[]{:S(2)}, u32[]{:S(2)}) collective-permute-start(bf16[48,5120]{1,0:T(8,128)(2,1)} %bitcast.11), channel_id=1, source_target_pairs={{0,4},{4,0},{8,12},{12,8},{1,5},{5,1},{9,13},{13,9},{2,6},{6,2},{1... | collective-permute-start | bytes 1474568 | tf_op jit(solution)/shard_map/ppermute | solution.py:25
  6.9 22.5 %collective-permute-start.5 = (bf16[96,5120]{1,0:T(8,128)(2,1)S(1)}, bf16[96,5120]{1,0:T(8,128)(2,1)S(1)}, u32[]{:S(2)}, u32[]{:S(2)}) collective-permute-start(bf16[96,5120]{1,0:T(8,128)(2,1)S(1)} %shard_map.101.w0), channel_id=1, source_target_pairs={{0,1},{1,2},{2,3},{3,0},{128,131},{129,128},{130,129},{131,130},{4... | collective-permute-start | bytes 2949128 | tf_op jit(solution)/shard_map/ppermute | solution.py:40
  9.2 9.4 %collective-permute-start = (bf16[16,5120]{1,0:T(8,128)(2,1)S(1)}, bf16[16,5120]{1,0:T(8,128)(2,1)S(1)}, u32[]{:S(2)}, u32[]{:S(2)}) collective-permute-start(bf16[16,5120]{1,0:T(8,128)(2,1)S(1)} %copy-done.5), channel_id=1, source_target_pairs={{0,12},{12,0},{4,8},{8,4},{1,13},{13,1},{5,9},{9,5},{2,14},{14,2},... | collective-permute-start | bytes 491528 | tf_op jit(solution)/shard_map/ppermute | solution.py:33
  11.0 7.6 %collective-permute-start.1 = (bf16[64,768]{1,0:T(8,128)(2,1)S(1)}, bf16[64,768]{1,0:T(8,128)(2,1)S(1)}, u32[]{:S(2)}, u32[]{:S(2)}) collective-permute-start(bf16[64,768]{1,0:T(8,128)(2,1)S(1)} %copy-done.6), channel_id=1, source_target_pairs={{0,16},{16,32},{32,48},{48,64},{64,80},{80,96},{96,112},{112,0},{1... | collective-permute-start | bytes 294920 | tf_op jit(solution)/shard_map/ppermute | solution.py:40
  16.7 5.5 %collective-permute-start.3 = (bf16[48,512]{1,0:T(8,128)(2,1)S(1)}, bf16[48,512]{1,0:T(8,128)(2,1)}, u32[]{:S(2)}, u32[]{:S(2)}) collective-permute-start(bf16[48,512]{1,0:T(8,128)(2,1)S(1)} %pad_maximum_fusion.3), channel_id=1, source_target_pairs={{16,128},{48,160},{80,192},{112,224},{128,16},{160,48},{192,80},{2... | collective-permute-start | bytes 147464 | tf_op jit(solution)/shard_map/ppermute | solution.py:361
  22.5 4.6 %collective-permute-start.8 = (bf16[48,5120]{1,0:T(8,128)(2,1)}, bf16[48,5120]{1,0:T(8,128)(2,1)}, u32[]{:S(2)}, u32[]{:S(2)}) collective-permute-start(bf16[48,5120]{1,0:T(8,128)(2,1)} %collective-permute-done.6.refs_0_), channel_id=1, source_target_pairs={{0,128},{128,0},{1,129},{129,1},{2,130},{130,2},{3,131},{131,3},{4... | collective-permute-start | bytes 1474568 | tf_op jit(solution)/shard_map/ppermute | solution.py:25
  22.6 6.8 %collective-permute-start.4 = (bf16[32,5888]{1,0:T(8,128)(2,1)S(1)}, bf16[32,5888]{1,0:T(8,128)(2,1)S(1)}, u32[]{:S(2)}, u32[]{:S(2)}) collective-permute-start(bf16[32,5888]{1,0:T(8,128)(2,1)S(1)} %shard_map.102.near), channel_id=1, source_target_pairs={{0,16},{16,32},{32,48},{48,64},{64,80},{80,96},{96,112},{112,0},{1... | collective-permute-start | bytes 1130504 | tf_op jit(solution)/shard_map/ppermute | solution.py:40
  22.7 5.8 %collective-permute-start.7 = (bf16[16,5120]{1,0:T(8,128)(2,1)}, bf16[16,5120]{1,0:T(8,128)(2,1)S(1)}, u32[]{:S(2)}, u32[]{:S(2)}) collective-permute-start(bf16[16,5120]{1,0:T(8,128)(2,1)} %copy-done.4), channel_id=1, source_target_pairs={{0,128},{128,0},{1,129},{129,1},{2,130},{130,2},{3,131},{131,3},{4... | collective-permute-start | bytes 491528 | tf_op jit(solution)/shard_map/ppermute | solution.py:25
  23.9 4.5 %collective-permute-start.9 = (bf16[48,512]{1,0:T(8,128)(2,1)S(1)}, bf16[48,512]{1,0:T(8,128)(2,1)S(1)}, u32[]{:S(2)}, u32[]{:S(2)}) collective-permute-start(bf16[48,512]{1,0:T(8,128)(2,1)S(1)} %broadcast_select_fusion), channel_id=1, source_target_pairs={{0,12},{12,0},{4,8},{8,4},{1,13},{13,1},{5,9},{9,5},{2,14},{14,2},... | collective-permute-start | bytes 147464 | tf_op jit(solution)/shard_map/ppermute | solution.py:33
  29.4 14.4 %collective-permute-start.11 = (bf16[96,5120]{1,0:T(8,128)(2,1)S(1)}, bf16[96,5120]{1,0:T(8,128)(2,1)S(1)}, u32[]{:S(2)}, u32[]{:S(2)}) collective-permute-start(bf16[96,5120]{1,0:T(8,128)(2,1)S(1)} %collective-permute-done.5.refs_0_.y1), channel_id=1, source_target_pairs={{0,128},{128,0},{1,129},{129,1},{2,130},{130,2},{3,131},{131,3},{4... | collective-permute-start | bytes 2949128 | tf_op jit(solution)/shard_map/ppermute | solution.py:25
  31.9 13.2 %collective-permute-start.12 = (bf16[96,5120]{1,0:T(8,128)(2,1)S(1)}, bf16[96,5120]{1,0:T(8,128)(2,1)S(1)}, u32[]{:S(2)}, u32[]{:S(2)}) collective-permute-start(bf16[96,5120]{1,0:T(8,128)(2,1)S(1)} %shard_map.103.pr), channel_id=1, source_target_pairs={{0,1},{1,2},{2,3},{3,0},{128,131},{129,128},{130,129},{131,130},{4... | collective-permute-start | bytes 2949128 | tf_op jit(solution)/shard_map/ppermute | solution.py:40
  33.0 10.9 %collective-permute-start.10 = (bf16[64,5888]{1,0:T(8,128)(2,1)S(1)}, bf16[64,5888]{1,0:T(8,128)(2,1)S(1)}, u32[]{:S(2)}, u32[]{:S(2)}) collective-permute-start(bf16[64,5888]{1,0:T(8,128)(2,1)S(1)} %shard_map.105), channel_id=1, source_target_pairs={{0,16},{16,32},{32,48},{48,64},{64,80},{80,96},{96,112},{112,0},{1... | collective-permute-start | bytes 2261000 | tf_op jit(solution)/shard_map/ppermute | solution.py:40
  33.5 4.3 %collective-permute-start.13 = (bf16[48,1024]{1,0:T(8,128)(2,1)S(1)}, bf16[48,1024]{1,0:T(8,128)(2,1)S(1)}, u32[]{:S(2)}, u32[]{:S(2)}) collective-permute-start(bf16[48,1024]{1,0:T(8,128)(2,1)S(1)} %pad_maximum_fusion.2), channel_id=1, source_target_pairs={{0,4},{4,0},{8,12},{12,8},{1,5},{5,1},{9,13},{13,9},{2,6},{6,2},{1... | collective-permute-start | bytes 294920 | tf_op jit(solution)/shard_map/ppermute | solution.py:25
  45.1 12.9 %collective-permute-start.17 = (bf16[96,5120]{1,0:T(8,128)(2,1)S(1)}, bf16[96,5120]{1,0:T(8,128)(2,1)S(1)}, u32[]{:S(2)}, u32[]{:S(2)}) collective-permute-start(bf16[96,5120]{1,0:T(8,128)(2,1)S(1)} %collective-permute-done.12.refs_1_.y2), channel_id=1, source_target_pairs={{0,128},{128,0},{1,129},{129,1},{2,130},{130,2},{3,131},{131,3},{4... | collective-permute-start | bytes 2949128 | tf_op jit(solution)/shard_map/ppermute | solution.py:25
  47.2 10.8 %collective-permute-start.16 = (bf16[64,5888]{1,0:T(8,128)(2,1)S(1)}, bf16[64,5888]{1,0:T(8,128)(2,1)S(1)}, u32[]{:S(2)}, u32[]{:S(2)}) collective-permute-start(bf16[64,5888]{1,0:T(8,128)(2,1)S(1)} %collective-permute-done.10.refs_1_.z2), channel_id=1, source_target_pairs={{0,16},{16,32},{32,48},{48,64},{64,80},{80,96},{96,112},{112,0},{1... | collective-permute-start | bytes 2261000 | tf_op jit(solution)/shard_map/ppermute | solution.py:40
  48.0 17.7 %collective-permute-start.19 = (bf16[48,14336]{1,0:T(8,128)(2,1)S(1)}, bf16[48,14336]{1,0:T(8,128)(2,1)S(1)}, u32[]{:S(2)}, u32[]{:S(2)}) collective-permute-start(bf16[48,14336]{1,0:T(8,128)(2,1)S(1)} %shard_map.106), channel_id=1, source_target_pairs={{0,1},{1,2},{2,3},{3,0},{128,131},{129,128},{130,129},{131,130},{4... | collective-permute-start | bytes 4128776 | tf_op jit(solution)/shard_map/ppermute | solution.py:40
  58.0 10.8 %collective-permute-start.18 = (bf16[64,5888]{1,0:T(8,128)(2,1)S(1)}, bf16[64,5888]{1,0:T(8,128)(2,1)S(1)}, u32[]{:S(2)}, u32[]{:S(2)}) collective-permute-start(bf16[64,5888]{1,0:T(8,128)(2,1)S(1)} %collective-permute-done.16.refs_2_.z3), channel_id=1, source_target_pairs={{0,16},{16,32},{32,48},{48,64},{64,80},{80,96},{96,112},{112,0},{1... | collective-permute-start | bytes 2261000 | tf_op jit(solution)/shard_map/ppermute | solution.py:40
  68.8 7.9 %collective-permute-start.21 = (bf16[48,14336]{1,0:T(8,128)(2,1)S(1)}, bf16[48,14336]{1,0:T(8,128)(2,1)S(1)}, u32[]{:S(2)}, u32[]{:S(2)}) collective-permute-start(bf16[48,14336]{1,0:T(8,128)(2,1)S(1)} %collective-permute-done.19.refs_0_.yz), channel_id=1, source_target_pairs={{0,128},{128,0},{1,129},{129,1},{2,130},{130,2},{3,131},{131,3},{4... | collective-permute-start | bytes 4128776 | tf_op jit(solution)/shard_map/ppermute | solution.py:25
  72.9 6.1 %collective-permute-start.22 = (bf16[48,2048]{1,0:T(8,128)(2,1)S(1)}, bf16[48,2048]{1,0:T(8,128)(2,1)S(1)}, u32[]{:S(2)}, u32[]{:S(2)}) collective-permute-start(bf16[48,2048]{1,0:T(8,128)(2,1)S(1)} %shard_map.108), channel_id=1, source_target_pairs={{0,1},{1,2},{2,3},{3,0},{128,131},{129,128},{130,129},{131,130},{4... | collective-permute-start | bytes 589832 | tf_op jit(solution)/shard_map/ppermute | solution.py:40
  79.9 6.5 %collective-permute-start.24 = (bf16[256,384]{1,0:T(8,128)(2,1)S(1)}, bf16[256,384]{1,0:T(8,128)(2,1)S(1)}, u32[]{:S(2)}, u32[]{:S(2)}) collective-permute-start(bf16[256,384]{1,0:T(8,128)(2,1)S(1)} %get-tuple-element.89), channel_id=1, source_target_pairs={{0,4},{4,0},{8,12},{12,8},{1,5},{5,1},{9,13},{13,9},{2,6},{6,2},{1... | collective-permute-start | bytes 589832 | tf_op jit(solution)/shard_map/ppermute | solution.py:25
  82.9 4.3 %collective-permute-start.26 = (bf16[256,384]{1,0:T(8,128)(2,1)S(1)}, bf16[256,384]{1,0:T(8,128)(2,1)S(1)}, u32[]{:S(2)}, u32[]{:S(2)}) collective-permute-start(bf16[256,384]{1,0:T(8,128)(2,1)S(1)} %get-tuple-element.94.refs_0_.kept), channel_id=1, source_target_pairs={{0,128},{128,0},{1,129},{129,1},{2,130},{130,2},{3,131},{131,3},{4... | collective-permute-start | bytes 589832 | tf_op jit(solution)/shard_map/ppermute | solution.py:25
  88.4 12.4 %collective-permute-start.28 = (bf16[1024,256]{1,0:T(8,128)(2,1)S(1)}, bf16[1024,256]{1,0:T(8,128)(2,1)S(1)}, u32[]{:S(2)}, u32[]{:S(2)}) collective-permute-start(bf16[1024,256]{1,0:T(8,128)(2,1)S(1)} %shard_map.112.own), channel_id=1, source_target_pairs={{0,1},{1,2},{2,3},{3,0},{128,131},{129,128},{130,129},{131,130},{4... | collective-permute-start | bytes 1572872 | tf_op jit(solution)/shard_map/ppermute | solution.py:40
  89.5 4.1 %collective-permute-start.29 = (bf16[256,256]{1,0:T(8,128)(2,1)S(1)}, bf16[256,256]{1,0:T(8,128)(2,1)S(1)}, u32[]{:S(2)}, u32[]{:S(2)}) collective-permute-start(bf16[256,256]{1,0:T(8,128)(2,1)S(1)} %pad_maximum_fusion.1), channel_id=1, source_target_pairs={{0,4},{4,8},{8,12},{12,0},{128,140},{132,128},{136,132},{140,136},... | collective-permute-start | bytes 393224 | tf_op jit(solution)/shard_map/ppermute | solution.py:40
  90.6 5.9 %collective-permute-start.31 = (bf16[128,256]{1,0:T(8,128)(2,1)S(1)}, bf16[128,256]{1,0:T(8,128)(2,1)S(1)}, u32[]{:S(2)}, u32[]{:S(2)}) collective-permute-start(bf16[128,256]{1,0:T(8,128)(2,1)S(1)} %get-tuple-element.95.refs_0_), channel_id=1, source_target_pairs={{0,8},{4,12},{8,0},{12,4},{1,9},{5,13},{9,1},{13,5},{2,10},{6,14},... | collective-permute-start | bytes 196616 | tf_op jit(solution)/shard_map/ppermute | solution.py:25
  93.7 4.1 %collective-permute-start.30 = (bf16[256,256]{1,0:T(8,128)(2,1)S(1)}, bf16[256,256]{1,0:T(8,128)(2,1)S(1)}, u32[]{:S(2)}, u32[]{:S(2)}) collective-permute-start(bf16[256,256]{1,0:T(8,128)(2,1)S(1)} %collective-permute-done.29.refs_1_.refs_5_), channel_id=1, source_target_pairs={{0,128},{128,0},{1,129},{129,1},{2,130},{130,2},{3,131},{131,3},{4... | collective-permute-start | bytes 393224 | tf_op jit(solution)/shard_map/ppermute | solution.py:25
  98.5 8.4 %collective-permute-start.35 = (bf16[1024,256]{1,0:T(8,128)(2,1)S(1)}, bf16[1024,256]{1,0:T(8,128)(2,1)S(1)}, u32[]{:S(2)}, u32[]{:S(2)}) collective-permute-start(bf16[1024,256]{1,0:T(8,128)(2,1)S(1)} %shard_map.113.own), channel_id=1, source_target_pairs={{0,1},{1,2},{2,3},{3,0},{128,131},{129,128},{130,129},{131,130},{4... | collective-permute-start | bytes 1572872 | tf_op jit(solution)/shard_map/ppermute | solution.py:40
  100.8 8.9 %collective-permute-start.34 = (bf16[512,256]{1,0:T(8,128)(2,1)S(1)}, bf16[512,256]{1,0:T(8,128)(2,1)S(1)}, u32[]{:S(2)}, u32[]{:S(2)}) collective-permute-start(bf16[512,256]{1,0:T(8,128)(2,1)S(1)} %slice.24), channel_id=1, source_target_pairs={{0,1},{1,2},{2,3},{3,0},{128,131},{129,128},{130,129},{131,130},{4... | collective-permute-start | bytes 786440 | tf_op jit(solution)/shard_map/ppermute | solution.py:40
  101.3 11.9 %collective-permute-start.33 = (bf16[1024,256]{1,0:T(8,128)(2,1)S(1)}, bf16[1024,256]{1,0:T(8,128)(2,1)S(1)}, u32[]{:S(2)}, u32[]{:S(2)}) collective-permute-start(bf16[1024,256]{1,0:T(8,128)(2,1)S(1)} %collective-permute-done.28.side), channel_id=1, source_target_pairs={{0,128},{128,0},{1,129},{129,1},{2,130},{130,2},{3,131},{131,3},{4... | collective-permute-start | bytes 1572872 | tf_op jit(solution)/shard_map/ppermute | solution.py:25
  112.0 5.6 %collective-permute-start.37 = (bf16[512,256]{1,0:T(8,128)(2,1)S(1)}, bf16[512,256]{1,0:T(8,128)(2,1)S(1)}, u32[]{:S(2)}, u32[]{:S(2)}) collective-permute-start(bf16[512,256]{1,0:T(8,128)(2,1)S(1)} %slice.28), channel_id=1, source_target_pairs={{0,1},{1,2},{2,3},{3,0},{128,131},{129,128},{130,129},{131,130},{4... | collective-permute-start | bytes 786440 | tf_op jit(solution)/shard_map/ppermute | solution.py:40
  113.0 6.6 %collective-permute-start.39 = (bf16[1024,256]{1,0:T(8,128)(2,1)S(1)}, bf16[1024,256]{1,0:T(8,128)(2,1)S(1)}, u32[]{:S(2)}, u32[]{:S(2)}) collective-permute-start(bf16[1024,256]{1,0:T(8,128)(2,1)S(1)} %collective-permute-done.35.side), channel_id=1, source_target_pairs={{0,128},{128,0},{1,129},{129,1},{2,130},{130,2},{3,131},{131,3},{4... | collective-permute-start | bytes 1572872 | tf_op jit(solution)/shard_map/ppermute | solution.py:25
  123.5 14.0 %all-to-all-start = ((f32[32,8,128]{2,1,0:T(8,128)}), f32[32,8,128]{2,1,0:T(8,128)S(1)}, u32[]{:S(2)}, u32[]{:S(2)}) async-start(f32[32,8,128]{2,1,0:T(8,128)} %shard_map.115), calls=%async_computation | async-start | bytes 262144 | tf_op jit(solution)/shard_map/all_to_all | solution.py:505
  (26 other events, 264.4 us)

commit v5 on v4

--- a/solution.py
+++ b/solution.py
@@ -304,7 +304,7 @@
 
 
 def small_body(
-    where, query, maps, maps_g, keep, got, own, side, side_g, far, far_g, out, scores
+    where, query, maps, maps_g, keep, own, side, side_g, far, far_g, out, scores
 ):
     pairs = ((own, 0, 1024), (side, 0, 1024), (side_g, 0, 1024), (far, 0, 512), (far_g, 0, 512))
     core, z_at, x = where[0], where[1], where[2]
@@ -312,7 +312,7 @@
     (done,) = attend((query[...],), pairs, (scores,))
     left = (1.0 - GUIDANCE) * dot_t(done, map_left)
     right = (1.0 - GUIDANCE) * dot_t(done, map_right)
-    out[...] = keep[...] + got[...]
+    out[...] = keep[...]
     for z in range(8):
         out[z * 4 + x] += left[16 * z : 16 * z + 8] + right[16 * z + 8 : 16 * z + 16]
 
@@ -497,12 +497,12 @@
     (total,) = call(
         small_body,
         [((32, 8, 128), F32)],
-        (where, query_s, maps, maps_g, keep, got, all_s, s_side, s_side_g, s_far, s_far_g),
+        (where, query_s, maps, maps_g, keep, all_s, s_side, s_side_g, s_far, s_far_g),
         [pltpu.VMEM((128, 4096), F32)],
         flops=2**30,
     )
 
-    returned = lax.all_to_all(total, ("z", "x"), split_axis=0, concat_axis=0, tiled=True)
+    returned = lax.all_to_all(total + got, ("z", "x"), split_axis=0, concat_axis=0, tiled=True)
     returned = jnp.sum(returned, axis=0)
     latent_l = lax.dynamic_slice_in_dim(latent_large, core * 16, 16, 0)
     latent_s = lax.dynamic_slice_in_dim(latent_small, core * 16, 16, 0)

time: 142 us -> 141 us (level)
  transfers between devices with their start and end apart: 43 -> 43, of which waited for: 23 -> 23; matrix products, arithmetic and copies ran while one was open for 1% -> 1% of each run, Pallas kernels for 12% -> 13%
where the time goes in v5:
time: 141 us
  waiting for transfers between devices  61.4 us (44%)
  starting transfers between devices  56.1 us (40%)
  Pallas kernels  18.3 us (13%)
  other arithmetic  2.24 us (2%)
  local copies, waits for them, and re-layouts  2.15 us (2%)
    ppermute x14, waiting for transfers between devices, spread(): return lax.ppermute(block, ('grp', axis), pairs)  34.1 us
    ppermute x25, starting transfers between devices, flip(): return lax.ppermute(block, axis, [(i, i ^ mask) for i in range(count)])  27 us
    ppermute x14, starting transfers between devices, spread(): return lax.ppermute(block, ('grp', axis), pairs)  19.3 us
    pallas_call x7, Pallas kernels, call(): pl.pallas_call(body, out_shape=[jax.ShapeDtypeStruct(shape, dtype) for sh...  14.6 us
    ppermute x25, waiting for transfers between devices, flip(): return lax.ppermute(block, axis, [(i, i ^ mask) for i in range(count)])  14.6 us
    all_to_all x1, waiting for transfers between devices, shards(): lax.all_to_all(total + got, ('z', 'x'), split_axis=0, concat_axis=0, tile...  9.06 us
    all_to_all x1, starting transfers between devices, shards(): lax.all_to_all(total + got, ('z', 'x'), split_axis=0, concat_axis=0, tile...  4.62 us
    pallas_call x9, Pallas kernels, pack(): pl.pallas_call(body, out_shape=jax.ShapeDtypeStruct(shape, BF), in_specs=...  3.71 us
  transfers between devices with their start and end apart: 43, of which 23 were waited for; matrix products, arithmetic and copies ran while one was open for 1% of the time, Pallas kernels for 13%

profile of v5, /device:TPU:1, one launch (start us, length us, event | category | flops | bytes accessed | tf_op | source)
XLA Modules:
  0.0 141.1 jit_solution(341495740991910687)
XLA Ops:
  0.0 3.2 %collective-permute-start.2 = (bf16[48,5120]{1,0:T(8,128)(2,1)}, bf16[48,5120]{1,0:T(8,128)(2,1)S(1)}, u32[]{:S(2)}, u32[]{:S(2)}) collective-permute-start(bf16[48,5120]{1,0:T(8,128)(2,1)} %bitcast.10), channel_id=1, source_target_pairs={{0,128},{128,0},{1,129},{129,1},{2,130},{130,2},{3,131},{131,3},{4... | collective-permute-start | bytes 1474568 | tf_op jit(solution)/shard_map/ppermute | solution.py:25
  3.2 2.0 %shard_map.100 = (bf16[16,5120]{1,0:T(8,128)(2,1)}, bf16[16,5120]{1,0:T(8,128)(2,1)}, bf16[64,768]{1,0:T(8,128)(2,1)}) custom-call(bf16[32,5120]{1,0:T(8,128)(2,1)} %large.1, bf16[32,1536]{1,0:T(8,128)(2,1)} %small.1, f32[5120]{0:T(1024)} %gain_l.1, f32[1536]{0:T(1024)} %gain_s.1), custom_call_target="tpu_custom_call" | custom-call | bytes 1048576 | tf_op jit(solution)/shard_map/pallas_call | solution.py:54
  6.9 2.3 %collective-permute-start.5 = (bf16[96,5120]{1,0:T(8,128)(2,1)S(1)}, bf16[96,5120]{1,0:T(8,128)(2,1)S(1)}, u32[]{:S(2)}, u32[]{:S(2)}) collective-permute-start(bf16[96,5120]{1,0:T(8,128)(2,1)S(1)} %shard_map.101.w0), channel_id=1, source_target_pairs={{0,1},{1,2},{2,3},{3,0},{128,131},{129,128},{130,129},{131,130},{4... | collective-permute-start | bytes 2949128 | tf_op jit(solution)/shard_map/ppermute | solution.py:40
  9.2 1.8 %collective-permute-start = (bf16[16,5120]{1,0:T(8,128)(2,1)S(1)}, bf16[16,5120]{1,0:T(8,128)(2,1)S(1)}, u32[]{:S(2)}, u32[]{:S(2)}) collective-permute-start(bf16[16,5120]{1,0:T(8,128)(2,1)S(1)} %copy-done.5), channel_id=1, source_target_pairs={{0,12},{12,0},{4,8},{8,4},{1,13},{13,1},{5,9},{9,5},{2,14},{14,2},... | collective-permute-start | bytes 491528 | tf_op jit(solution)/shard_map/ppermute | solution.py:33
  11.0 5.6 %collective-permute-start.1 = (bf16[64,768]{1,0:T(8,128)(2,1)S(1)}, bf16[64,768]{1,0:T(8,128)(2,1)S(1)}, u32[]{:S(2)}, u32[]{:S(2)}) collective-permute-start(bf16[64,768]{1,0:T(8,128)(2,1)S(1)} %copy-done.6), channel_id=1, source_target_pairs={{0,16},{16,32},{32,48},{48,64},{64,80},{80,96},{96,112},{112,0},{1... | collective-permute-start | bytes 294920 | tf_op jit(solution)/shard_map/ppermute | solution.py:40
  16.7 1.9 %collective-permute-start.3 = (bf16[48,512]{1,0:T(8,128)(2,1)S(1)}, bf16[48,512]{1,0:T(8,128)(2,1)}, u32[]{:S(2)}, u32[]{:S(2)}) collective-permute-start(bf16[48,512]{1,0:T(8,128)(2,1)S(1)} %pad_maximum_fusion.3), channel_id=1, source_target_pairs={{16,128},{48,160},{80,192},{112,224},{128,16},{160,48},{192,80},{2... | collective-permute-start | bytes 147464 | tf_op jit(solution)/shard_map/ppermute | solution.py:361
  18.6 3.6 %collective-permute-done.3 = bf16[48,512]{1,0:T(8,128)(2,1)} collective-permute-done((bf16[48,512]{1,0:T(8,128)(2,1)S(1)}, bf16[48,512]{1,0:T(8,128)(2,1)}, u32[]{:S(2)}, u32[]{:S(2)}) %collective-permute-start.3) | collective-permute-done | bytes 49184 | tf_op jit(solution)/shard_map/ppermute | solution.py:361
  29.4 2.5 %collective-permute-start.11 = (bf16[96,5120]{1,0:T(8,128)(2,1)S(1)}, bf16[96,5120]{1,0:T(8,128)(2,1)S(1)}, u32[]{:S(2)}, u32[]{:S(2)}) collective-permute-start(bf16[96,5120]{1,0:T(8,128)(2,1)S(1)} %collective-permute-done.5.refs_0_.y1), channel_id=1, source_target_pairs={{0,128},{128,0},{1,129},{129,1},{2,130},{130,2},{3,131},{131,3},{4... | collective-permute-start | bytes 2949128 | tf_op jit(solution)/shard_map/ppermute | solution.py:25
  33.6 4.2 %collective-permute-done.13 = bf16[48,1024]{1,0:T(8,128)(2,1)S(1)} collective-permute-done((bf16[48,1024]{1,0:T(8,128)(2,1)S(1)}, bf16[48,1024]{1,0:T(8,128)(2,1)S(1)}, u32[]{:S(2)}, u32[]{:S(2)}) %collective-permute-start.13) | collective-permute-done | bytes 98336 | tf_op jit(solution)/shard_map/ppermute | solution.py:25
  39.4 4.4 %collective-permute-done.10.refs_1_.z2 = bf16[64,5888]{1,0:T(8,128)(2,1)S(1)} collective-permute-done((bf16[64,5888]{1,0:T(8,128)(2,1)S(1)}, bf16[64,5888]{1,0:T(8,128)(2,1)S(1)}, u32[]{:S(2)}, u32[]{:S(2)}) %collective-permute-start.10) | collective-permute-done | bytes 753696 | tf_op jit(solution)/shard_map/ppermute | solution.py:40
  45.1 2.1 %collective-permute-start.17 = (bf16[96,5120]{1,0:T(8,128)(2,1)S(1)}, bf16[96,5120]{1,0:T(8,128)(2,1)S(1)}, u32[]{:S(2)}, u32[]{:S(2)}) collective-permute-start(bf16[96,5120]{1,0:T(8,128)(2,1)S(1)} %collective-permute-done.12.refs_1_.y2), channel_id=1, source_target_pairs={{0,128},{128,0},{1,129},{129,1},{2,130},{130,2},{3,131},{131,3},{4... | collective-permute-start | bytes 2949128 | tf_op jit(solution)/shard_map/ppermute | solution.py:25
  48.7 9.2 %collective-permute-done.16.refs_2_.z3 = bf16[64,5888]{1,0:T(8,128)(2,1)S(1)} collective-permute-done((bf16[64,5888]{1,0:T(8,128)(2,1)S(1)}, bf16[64,5888]{1,0:T(8,128)(2,1)S(1)}, u32[]{:S(2)}, u32[]{:S(2)}) %collective-permute-start.16) | collective-permute-done | bytes 753696 | tf_op jit(solution)/shard_map/ppermute | solution.py:40
  58.0 1.7 %collective-permute-start.18 = (bf16[64,5888]{1,0:T(8,128)(2,1)S(1)}, bf16[64,5888]{1,0:T(8,128)(2,1)S(1)}, u32[]{:S(2)}, u32[]{:S(2)}) collective-permute-start(bf16[64,5888]{1,0:T(8,128)(2,1)S(1)} %collective-permute-done.16.refs_2_.z3), channel_id=1, source_target_pairs={{0,16},{16,32},{32,48},{48,64},{64,80},{80,96},{96,112},{112,0},{1... | collective-permute-start | bytes 2261000 | tf_op jit(solution)/shard_map/ppermute | solution.py:40
  61.3 4.4 %collective-permute-done.19.refs_0_.yz = bf16[48,14336]{1,0:T(8,128)(2,1)S(1)} collective-permute-done((bf16[48,14336]{1,0:T(8,128)(2,1)S(1)}, bf16[48,14336]{1,0:T(8,128)(2,1)S(1)}, u32[]{:S(2)}, u32[]{:S(2)}) %collective-permute-start.19) | collective-permute-done | bytes 1376288 | tf_op jit(solution)/shard_map/ppermute | solution.py:40
  65.7 3.1 %collective-permute-done.18.z4 = bf16[64,5888]{1,0:T(8,128)(2,1)S(1)} collective-permute-done((bf16[64,5888]{1,0:T(8,128)(2,1)S(1)}, bf16[64,5888]{1,0:T(8,128)(2,1)S(1)}, u32[]{:S(2)}, u32[]{:S(2)}) %collective-permute-start.18) | collective-permute-done | bytes 753696 | tf_op jit(solution)/shard_map/ppermute | solution.py:40
  68.8 4.1 %collective-permute-start.21 = (bf16[48,14336]{1,0:T(8,128)(2,1)S(1)}, bf16[48,14336]{1,0:T(8,128)(2,1)S(1)}, u32[]{:S(2)}, u32[]{:S(2)}) collective-permute-start(bf16[48,14336]{1,0:T(8,128)(2,1)S(1)} %collective-permute-done.19.refs_0_.yz), channel_id=1, source_target_pairs={{0,128},{128,0},{1,129},{129,1},{2,130},{130,2},{3,131},{131,3},{4... | collective-permute-start | bytes 4128776 | tf_op jit(solution)/shard_map/ppermute | solution.py:25
  74.1 2.5 %shard_map.109 = (bf16[384,256]{1,0:T(8,128)(2,1)S(1)}, bf16[288,256]{1,0:T(8,128)(2,1)S(1)}) custom-call(s32[4]{0:T(128)S(1)} %pad_add_fusion.where, bf16[32,5888]{1,0:T(8,128)(2,1)S(1)} %shard_map.102.near, bf16[32,5888]{1,0:T(8,128)(2,1)S(1)} %collective-permute-done.4.refs_0_.z1, bf16[64,5888]{1,0:T(8,128)(2,1)S(1)} %collective-permute-done.10.refs_1_.z2, ...), custom_call_target="tpu_custom_call" | custom-call | flops 4294967296 | bytes 1048576 | tf_op jit(solution)/shard_map/pallas_call | solution.py:54
  76.7 2.3 %shard_map.110 = (bf16[256,384]{1,0:T(8,128)(2,1)S(1)}, bf16[256,384]{1,0:T(8,128)(2,1)S(1)}) custom-call(s32[4]{0:T(128)S(1)} %pad_add_fusion.where, bf16[32,5888]{1,0:T(8,128)(2,1)S(1)} %shard_map.102.near, bf16[32,5888]{1,0:T(8,128)(2,1)S(1)} %collective-permute-done.4.refs_0_.z1, bf16[64,5888]{1,0:T(8,128)(2,1)S(1)} %collective-permute-done.10.refs_1_.z2, ...), custom_call_target="tpu_custom_call" | custom-call | flops 536870912 | bytes 1048576 | tf_op jit(solution)/shard_map/pallas_call | solution.py:54
  81.0 1.5 %shard_map.111 = (bf16[128,128]{1,0:T(8,128)(2,1)S(1)}, bf16[128,256]{1,0:T(8,128)(2,1)S(1)}) custom-call(s32[4]{0:T(128)S(1)} %pad_add_fusion.where, bf16[64,768]{1,0:T(8,128)(2,1)S(1)} %copy-done.7, bf16[64,768]{1,0:T(8,128)(2,1)S(1)} %collective-permute-done.1.refs_2_.refs_3_.refs_0_.s1, bf16[32,5888]{1,0:T(8,128)(2,1)S(1)} %collective-permute-done.4.refs_0_.z1, ...), custom_call_target="tpu_custom_call" | custom-call | flops 536870912 | bytes 1048576 | tf_op jit(solution)/shard_map/pallas_call | solution.py:54
  83.1 3.4 %collective-permute-done.24.refs_1_.taken = bf16[256,384]{1,0:T(8,128)(2,1)S(1)} collective-permute-done((bf16[256,384]{1,0:T(8,128)(2,1)S(1)}, bf16[256,384]{1,0:T(8,128)(2,1)S(1)}, u32[]{:S(2)}, u32[]{:S(2)}) %collective-permute-start.24) | collective-permute-done | bytes 196640 | tf_op jit(solution)/shard_map/ppermute | solution.py:25
  91.8 1.8 %collective-permute-done.29.refs_1_.refs_5_ = bf16[256,256]{1,0:T(8,128)(2,1)S(1)} collective-permute-done((bf16[256,256]{1,0:T(8,128)(2,1)S(1)}, bf16[256,256]{1,0:T(8,128)(2,1)S(1)}, u32[]{:S(2)}, u32[]{:S(2)}) %collective-permute-start.29) | collective-permute-done | bytes 131104 | tf_op jit(solution)/shard_map/ppermute | solution.py:40
  93.7 2.9 %collective-permute-start.30 = (bf16[256,256]{1,0:T(8,128)(2,1)S(1)}, bf16[256,256]{1,0:T(8,128)(2,1)S(1)}, u32[]{:S(2)}, u32[]{:S(2)}) collective-permute-start(bf16[256,256]{1,0:T(8,128)(2,1)S(1)} %collective-permute-done.29.refs_1_.refs_5_), channel_id=1, source_target_pairs={{0,128},{128,0},{1,129},{129,1},{2,130},{130,2},{3,131},{131,3},{4... | collective-permute-start | bytes 393224 | tf_op jit(solution)/shard_map/ppermute | solution.py:25
  98.5 2.2 %collective-permute-start.35 = (bf16[1024,256]{1,0:T(8,128)(2,1)S(1)}, bf16[1024,256]{1,0:T(8,128)(2,1)S(1)}, u32[]{:S(2)}, u32[]{:S(2)}) collective-permute-start(bf16[1024,256]{1,0:T(8,128)(2,1)S(1)} %shard_map.113.own), channel_id=1, source_target_pairs={{0,1},{1,2},{2,3},{3,0},{128,131},{129,128},{130,129},{131,130},{4... | collective-permute-start | bytes 1572872 | tf_op jit(solution)/shard_map/ppermute | solution.py:40
  101.4 5.5 %collective-permute-done.35.side = bf16[1024,256]{1,0:T(8,128)(2,1)S(1)} collective-permute-done((bf16[1024,256]{1,0:T(8,128)(2,1)S(1)}, bf16[1024,256]{1,0:T(8,128)(2,1)S(1)}, u32[]{:S(2)}, u32[]{:S(2)}) %collective-permute-start.35) | collective-permute-done | bytes 524320 | tf_op jit(solution)/shard_map/ppermute | solution.py:40
  106.9 2.8 %collective-permute-done.34.far = bf16[512,256]{1,0:T(8,128)(2,1)S(1)} collective-permute-done((bf16[512,256]{1,0:T(8,128)(2,1)S(1)}, bf16[512,256]{1,0:T(8,128)(2,1)S(1)}, u32[]{:S(2)}, u32[]{:S(2)}) %collective-permute-start.34) | collective-permute-done | bytes 262176 | tf_op jit(solution)/shard_map/ppermute | solution.py:40
  109.7 2.2 %collective-permute-start.36 = (bf16[512,256]{1,0:T(8,128)(2,1)S(1)}, bf16[512,256]{1,0:T(8,128)(2,1)S(1)}, u32[]{:S(2)}, u32[]{:S(2)}) collective-permute-start(bf16[512,256]{1,0:T(8,128)(2,1)S(1)} %collective-permute-done.34.far), channel_id=1, source_target_pairs={{0,128},{128,0},{1,129},{129,1},{2,130},{130,2},{3,131},{131,3},{4... | collective-permute-start | bytes 786440 | tf_op jit(solution)/shard_map/ppermute | solution.py:25
  113.2 3.8 %shard_map.114 = (f32[32,8,128]{2,1,0:T(8,128)S(1)}, f32[32,8,128]{2,1,0:T(8,128)S(1)}) custom-call(s32[4]{0:T(128)S(1)} %pad_add_fusion.where, bf16[256,384]{1,0:T(8,128)(2,1)S(1)} %get-tuple-element.94.refs_0_.kept, bf16[256,384]{1,0:T(8,128)(2,1)S(1)} %collective-permute-done.24.refs_1_.taken, bf16[128,128]{1,0:T(8,128)(2,1)S(1)} %get-tuple-element.73.maps, ...), custom_call_target="tpu_custom_call" | custom-call | flops 4294967296 | bytes 1048576 | tf_op jit(solution)/shard_map/pallas_call | solution.py:54
  117.6 2.1 %collective-permute-start.39 = (bf16[512,256]{1,0:T(8,128)(2,1)S(1)}, bf16[512,256]{1,0:T(8,128)(2,1)S(1)}, u32[]{:S(2)}, u32[]{:S(2)}) collective-permute-start(bf16[512,256]{1,0:T(8,128)(2,1)S(1)} %collective-permute-done.37.far), channel_id=1, source_target_pairs={{0,128},{128,0},{1,129},{129,1},{2,130},{130,2},{3,131},{131,3},{4... | collective-permute-start | bytes 786440 | tf_op jit(solution)/shard_map/ppermute | solution.py:25
  120.8 1.8 %shard_map.115 = f32[32,8,128]{2,1,0:T(8,128)S(1)} custom-call(s32[4]{0:T(128)S(1)} %pad_add_fusion.where, bf16[128,128]{1,0:T(8,128)(2,1)S(1)} %get-tuple-element.92.query, bf16[128,128]{1,0:T(8,128)(2,1)S(1)} %get-tuple-element.73.maps, bf16[128,128]{1,0:T(8,128)(2,1)S(1)} %collective-permute-done.15.maps_g, f32[32,8,128]{2,1,0:T(8,128)S(1)} %get-tuple-element.102.keep, ...), custom_call_target="tpu_custom_call" | custom-call | flops 1073741824 | bytes 1048576 | tf_op jit(solution)/shard_map/pallas_call | solution.py:54
  123.3 4.6 %all-to-all-start = ((f32[32,8,128]{2,1,0:T(8,128)}), f32[32,8,128]{2,1,0:T(8,128)S(1)}, u32[]{:S(2)}, u32[]{:S(2)}) async-start(f32[32,8,128]{2,1,0:T(8,128)} %add.17), calls=%async_computation | async-start | bytes 262144 | tf_op jit(solution)/shard_map/all_to_all | solution.py:505
  128.3 9.1 %all-to-all-done = f32[32,8,128]{2,1,0:T(8,128)S(1)} async-done(((f32[32,8,128]{2,1,0:T(8,128)}), f32[32,8,128]{2,1,0:T(8,128)S(1)}, u32[]{:S(2)}, u32[]{:S(2)}) %all-to-all-start) | async-done | bytes 131104 | tf_op jit(solution)/shard_map/all_to_all | solution.py:505
  137.6 2.1 %collective-permute-start.41 = (f32[16,64]{1,0:T(8,128)S(1)}, f32[16,64]{1,0:T(8,128)S(1)}, u32[]{:S(2)}, u32[]{:S(2)}) collective-permute-start(f32[16,64]{1,0:T(8,128)S(1)} %fusion.1), channel_id=1, source_target_pairs={{0,128},{128,0},{1,129},{129,1},{2,130},{130,2},{3,131},{131,3},{4... | collective-permute-start | bytes 12296 | tf_op jit(solution)/shard_map/ppermute | solution.py:25
  (115 shorter events, 33.9 us)
Async XLA Ops:
  0.0 5.2 %collective-permute-start.2 = (bf16[48,5120]{1,0:T(8,128)(2,1)}, bf16[48,5120]{1,0:T(8,128)(2,1)S(1)}, u32[]{:S(2)}, u32[]{:S(2)}) collective-permute-start(bf16[48,5120]{1,0:T(8,128)(2,1)} %bitcast.10), channel_id=1, source_target_pairs={{0,128},{128,0},{1,129},{129,1},{2,130},{130,2},{3,131},{131,3},{4... | collective-permute-start | bytes 1474568 | tf_op jit(solution)/shard_map/ppermute | solution.py:25
  3.2 19.2 %collective-permute-start.6 = (bf16[48,5120]{1,0:T(8,128)(2,1)}, bf16[48,5120]{1,0:T(8,128)(2,1)}, u32[]{:S(2)}, u32[]{:S(2)}) collective-permute-start(bf16[48,5120]{1,0:T(8,128)(2,1)} %bitcast.11), channel_id=1, source_target_pairs={{0,4},{4,0},{8,12},{12,8},{1,5},{5,1},{9,13},{13,9},{2,6},{6,2},{1... | collective-permute-start | bytes 1474568 | tf_op jit(solution)/shard_map/ppermute | solution.py:25
  6.9 22.5 %collective-permute-start.5 = (bf16[96,5120]{1,0:T(8,128)(2,1)S(1)}, bf16[96,5120]{1,0:T(8,128)(2,1)S(1)}, u32[]{:S(2)}, u32[]{:S(2)}) collective-permute-start(bf16[96,5120]{1,0:T(8,128)(2,1)S(1)} %shard_map.101.w0), channel_id=1, source_target_pairs={{0,1},{1,2},{2,3},{3,0},{128,131},{129,128},{130,129},{131,130},{4... | collective-permute-start | bytes 2949128 | tf_op jit(solution)/shard_map/ppermute | solution.py:40
  9.2 9.4 %collective-permute-start = (bf16[16,5120]{1,0:T(8,128)(2,1)S(1)}, bf16[16,5120]{1,0:T(8,128)(2,1)S(1)}, u32[]{:S(2)}, u32[]{:S(2)}) collective-permute-start(bf16[16,5120]{1,0:T(8,128)(2,1)S(1)} %copy-done.5), channel_id=1, source_target_pairs={{0,12},{12,0},{4,8},{8,4},{1,13},{13,1},{5,9},{9,5},{2,14},{14,2},... | collective-permute-start | bytes 491528 | tf_op jit(solution)/shard_map/ppermute | solution.py:33
  11.0 7.6 %collective-permute-start.1 = (bf16[64,768]{1,0:T(8,128)(2,1)S(1)}, bf16[64,768]{1,0:T(8,128)(2,1)S(1)}, u32[]{:S(2)}, u32[]{:S(2)}) collective-permute-start(bf16[64,768]{1,0:T(8,128)(2,1)S(1)} %copy-done.6), channel_id=1, source_target_pairs={{0,16},{16,32},{32,48},{48,64},{64,80},{80,96},{96,112},{112,0},{1... | collective-permute-start | bytes 294920 | tf_op jit(solution)/shard_map/ppermute | solution.py:40
  16.7 5.5 %collective-permute-start.3 = (bf16[48,512]{1,0:T(8,128)(2,1)S(1)}, bf16[48,512]{1,0:T(8,128)(2,1)}, u32[]{:S(2)}, u32[]{:S(2)}) collective-permute-start(bf16[48,512]{1,0:T(8,128)(2,1)S(1)} %pad_maximum_fusion.3), channel_id=1, source_target_pairs={{16,128},{48,160},{80,192},{112,224},{128,16},{160,48},{192,80},{2... | collective-permute-start | bytes 147464 | tf_op jit(solution)/shard_map/ppermute | solution.py:361
  22.5 4.6 %collective-permute-start.8 = (bf16[48,5120]{1,0:T(8,128)(2,1)}, bf16[48,5120]{1,0:T(8,128)(2,1)}, u32[]{:S(2)}, u32[]{:S(2)}) collective-permute-start(bf16[48,5120]{1,0:T(8,128)(2,1)} %collective-permute-done.6.refs_0_), channel_id=1, source_target_pairs={{0,128},{128,0},{1,129},{129,1},{2,130},{130,2},{3,131},{131,3},{4... | collective-permute-start | bytes 1474568 | tf_op jit(solution)/shard_map/ppermute | solution.py:25
  22.6 6.8 %collective-permute-start.4 = (bf16[32,5888]{1,0:T(8,128)(2,1)S(1)}, bf16[32,5888]{1,0:T(8,128)(2,1)S(1)}, u32[]{:S(2)}, u32[]{:S(2)}) collective-permute-start(bf16[32,5888]{1,0:T(8,128)(2,1)S(1)} %shard_map.102.near), channel_id=1, source_target_pairs={{0,16},{16,32},{32,48},{48,64},{64,80},{80,96},{96,112},{112,0},{1... | collective-permute-start | bytes 1130504 | tf_op jit(solution)/shard_map/ppermute | solution.py:40
  22.7 5.8 %collective-permute-start.7 = (bf16[16,5120]{1,0:T(8,128)(2,1)}, bf16[16,5120]{1,0:T(8,128)(2,1)S(1)}, u32[]{:S(2)}, u32[]{:S(2)}) collective-permute-start(bf16[16,5120]{1,0:T(8,128)(2,1)} %copy-done.4), channel_id=1, source_target_pairs={{0,128},{128,0},{1,129},{129,1},{2,130},{130,2},{3,131},{131,3},{4... | collective-permute-start | bytes 491528 | tf_op jit(solution)/shard_map/ppermute | solution.py:25
  23.9 4.5 %collective-permute-start.9 = (bf16[48,512]{1,0:T(8,128)(2,1)S(1)}, bf16[48,512]{1,0:T(8,128)(2,1)S(1)}, u32[]{:S(2)}, u32[]{:S(2)}) collective-permute-start(bf16[48,512]{1,0:T(8,128)(2,1)S(1)} %broadcast_select_fusion), channel_id=1, source_target_pairs={{0,12},{12,0},{4,8},{8,4},{1,13},{13,1},{5,9},{9,5},{2,14},{14,2},... | collective-permute-start | bytes 147464 | tf_op jit(solution)/shard_map/ppermute | solution.py:33
  29.4 14.4 %collective-permute-start.11 = (bf16[96,5120]{1,0:T(8,128)(2,1)S(1)}, bf16[96,5120]{1,0:T(8,128)(2,1)S(1)}, u32[]{:S(2)}, u32[]{:S(2)}) collective-permute-start(bf16[96,5120]{1,0:T(8,128)(2,1)S(1)} %collective-permute-done.5.refs_0_.y1), channel_id=1, source_target_pairs={{0,128},{128,0},{1,129},{129,1},{2,130},{130,2},{3,131},{131,3},{4... | collective-permute-start | bytes 2949128 | tf_op jit(solution)/shard_map/ppermute | solution.py:25
  31.9 13.2 %collective-permute-start.12 = (bf16[96,5120]{1,0:T(8,128)(2,1)S(1)}, bf16[96,5120]{1,0:T(8,128)(2,1)S(1)}, u32[]{:S(2)}, u32[]{:S(2)}) collective-permute-start(bf16[96,5120]{1,0:T(8,128)(2,1)S(1)} %shard_map.103.pr), channel_id=1, source_target_pairs={{0,1},{1,2},{2,3},{3,0},{128,131},{129,128},{130,129},{131,130},{4... | collective-permute-start | bytes 2949128 | tf_op jit(solution)/shard_map/ppermute | solution.py:40
  33.0 10.9 %collective-permute-start.10 = (bf16[64,5888]{1,0:T(8,128)(2,1)S(1)}, bf16[64,5888]{1,0:T(8,128)(2,1)S(1)}, u32[]{:S(2)}, u32[]{:S(2)}) collective-permute-start(bf16[64,5888]{1,0:T(8,128)(2,1)S(1)} %shard_map.105), channel_id=1, source_target_pairs={{0,16},{16,32},{32,48},{48,64},{64,80},{80,96},{96,112},{112,0},{1... | collective-permute-start | bytes 2261000 | tf_op jit(solution)/shard_map/ppermute | solution.py:40
  33.5 4.3 %collective-permute-start.13 = (bf16[48,1024]{1,0:T(8,128)(2,1)S(1)}, bf16[48,1024]{1,0:T(8,128)(2,1)S(1)}, u32[]{:S(2)}, u32[]{:S(2)}) collective-permute-start(bf16[48,1024]{1,0:T(8,128)(2,1)S(1)} %pad_maximum_fusion.2), channel_id=1, source_target_pairs={{0,4},{4,0},{8,12},{12,8},{1,5},{5,1},{9,13},{13,9},{2,6},{6,2},{1... | collective-permute-start | bytes 294920 | tf_op jit(solution)/shard_map/ppermute | solution.py:25
  45.1 12.9 %collective-permute-start.17 = (bf16[96,5120]{1,0:T(8,128)(2,1)S(1)}, bf16[96,5120]{1,0:T(8,128)(2,1)S(1)}, u32[]{:S(2)}, u32[]{:S(2)}) collective-permute-start(bf16[96,5120]{1,0:T(8,128)(2,1)S(1)} %collective-permute-done.12.refs_1_.y2), channel_id=1, source_target_pairs={{0,128},{128,0},{1,129},{129,1},{2,130},{130,2},{3,131},{131,3},{4... | collective-permute-start | bytes 2949128 | tf_op jit(solution)/shard_map/ppermute | solution.py:25
  47.2 10.8 %collective-permute-start.16 = (bf16[64,5888]{1,0:T(8,128)(2,1)S(1)}, bf16[64,5888]{1,0:T(8,128)(2,1)S(1)}, u32[]{:S(2)}, u32[]{:S(2)}) collective-permute-start(bf16[64,5888]{1,0:T(8,128)(2,1)S(1)} %collective-permute-done.10.refs_1_.z2), channel_id=1, source_target_pairs={{0,16},{16,32},{32,48},{48,64},{64,80},{80,96},{96,112},{112,0},{1... | collective-permute-start | bytes 2261000 | tf_op jit(solution)/shard_map/ppermute | solution.py:40
  48.0 17.7 %collective-permute-start.19 = (bf16[48,14336]{1,0:T(8,128)(2,1)S(1)}, bf16[48,14336]{1,0:T(8,128)(2,1)S(1)}, u32[]{:S(2)}, u32[]{:S(2)}) collective-permute-start(bf16[48,14336]{1,0:T(8,128)(2,1)S(1)} %shard_map.106), channel_id=1, source_target_pairs={{0,1},{1,2},{2,3},{3,0},{128,131},{129,128},{130,129},{131,130},{4... | collective-permute-start | bytes 4128776 | tf_op jit(solution)/shard_map/ppermute | solution.py:40
  58.0 10.8 %collective-permute-start.18 = (bf16[64,5888]{1,0:T(8,128)(2,1)S(1)}, bf16[64,5888]{1,0:T(8,128)(2,1)S(1)}, u32[]{:S(2)}, u32[]{:S(2)}) collective-permute-start(bf16[64,5888]{1,0:T(8,128)(2,1)S(1)} %collective-permute-done.16.refs_2_.z3), channel_id=1, source_target_pairs={{0,16},{16,32},{32,48},{48,64},{64,80},{80,96},{96,112},{112,0},{1... | collective-permute-start | bytes 2261000 | tf_op jit(solution)/shard_map/ppermute | solution.py:40
  68.8 7.9 %collective-permute-start.21 = (bf16[48,14336]{1,0:T(8,128)(2,1)S(1)}, bf16[48,14336]{1,0:T(8,128)(2,1)S(1)}, u32[]{:S(2)}, u32[]{:S(2)}) collective-permute-start(bf16[48,14336]{1,0:T(8,128)(2,1)S(1)} %collective-permute-done.19.refs_0_.yz), channel_id=1, source_target_pairs={{0,128},{128,0},{1,129},{129,1},{2,130},{130,2},{3,131},{131,3},{4... | collective-permute-start | bytes 4128776 | tf_op jit(solution)/shard_map/ppermute | solution.py:25
  72.9 6.1 %collective-permute-start.22 = (bf16[48,2048]{1,0:T(8,128)(2,1)S(1)}, bf16[48,2048]{1,0:T(8,128)(2,1)S(1)}, u32[]{:S(2)}, u32[]{:S(2)}) collective-permute-start(bf16[48,2048]{1,0:T(8,128)(2,1)S(1)} %shard_map.108), channel_id=1, source_target_pairs={{0,1},{1,2},{2,3},{3,0},{128,131},{129,128},{130,129},{131,130},{4... | collective-permute-start | bytes 589832 | tf_op jit(solution)/shard_map/ppermute | solution.py:40
  79.9 6.5 %collective-permute-start.24 = (bf16[256,384]{1,0:T(8,128)(2,1)S(1)}, bf16[256,384]{1,0:T(8,128)(2,1)S(1)}, u32[]{:S(2)}, u32[]{:S(2)}) collective-permute-start(bf16[256,384]{1,0:T(8,128)(2,1)S(1)} %get-tuple-element.89), channel_id=1, source_target_pairs={{0,4},{4,0},{8,12},{12,8},{1,5},{5,1},{9,13},{13,9},{2,6},{6,2},{1... | collective-permute-start | bytes 589832 | tf_op jit(solution)/shard_map/ppermute | solution.py:25
  82.9 4.3 %collective-permute-start.26 = (bf16[256,384]{1,0:T(8,128)(2,1)S(1)}, bf16[256,384]{1,0:T(8,128)(2,1)S(1)}, u32[]{:S(2)}, u32[]{:S(2)}) collective-permute-start(bf16[256,384]{1,0:T(8,128)(2,1)S(1)} %get-tuple-element.94.refs_0_.kept), channel_id=1, source_target_pairs={{0,128},{128,0},{1,129},{129,1},{2,130},{130,2},{3,131},{131,3},{4... | collective-permute-start | bytes 589832 | tf_op jit(solution)/shard_map/ppermute | solution.py:25
  88.4 12.4 %collective-permute-start.28 = (bf16[1024,256]{1,0:T(8,128)(2,1)S(1)}, bf16[1024,256]{1,0:T(8,128)(2,1)S(1)}, u32[]{:S(2)}, u32[]{:S(2)}) collective-permute-start(bf16[1024,256]{1,0:T(8,128)(2,1)S(1)} %shard_map.112.own), channel_id=1, source_target_pairs={{0,1},{1,2},{2,3},{3,0},{128,131},{129,128},{130,129},{131,130},{4... | collective-permute-start | bytes 1572872 | tf_op jit(solution)/shard_map/ppermute | solution.py:40
  89.5 4.1 %collective-permute-start.29 = (bf16[256,256]{1,0:T(8,128)(2,1)S(1)}, bf16[256,256]{1,0:T(8,128)(2,1)S(1)}, u32[]{:S(2)}, u32[]{:S(2)}) collective-permute-start(bf16[256,256]{1,0:T(8,128)(2,1)S(1)} %pad_maximum_fusion.1), channel_id=1, source_target_pairs={{0,4},{4,8},{8,12},{12,0},{128,140},{132,128},{136,132},{140,136},... | collective-permute-start | bytes 393224 | tf_op jit(solution)/shard_map/ppermute | solution.py:40
  90.6 5.9 %collective-permute-start.31 = (bf16[128,256]{1,0:T(8,128)(2,1)S(1)}, bf16[128,256]{1,0:T(8,128)(2,1)S(1)}, u32[]{:S(2)}, u32[]{:S(2)}) collective-permute-start(bf16[128,256]{1,0:T(8,128)(2,1)S(1)} %get-tuple-element.95.refs_0_), channel_id=1, source_target_pairs={{0,8},{4,12},{8,0},{12,4},{1,9},{5,13},{9,1},{13,5},{2,10},{6,14},... | collective-permute-start | bytes 196616 | tf_op jit(solution)/shard_map/ppermute | solution.py:25
  93.7 4.1 %collective-permute-start.30 = (bf16[256,256]{1,0:T(8,128)(2,1)S(1)}, bf16[256,256]{1,0:T(8,128)(2,1)S(1)}, u32[]{:S(2)}, u32[]{:S(2)}) collective-permute-start(bf16[256,256]{1,0:T(8,128)(2,1)S(1)} %collective-permute-done.29.refs_1_.refs_5_), channel_id=1, source_target_pairs={{0,128},{128,0},{1,129},{129,1},{2,130},{130,2},{3,131},{131,3},{4... | collective-permute-start | bytes 393224 | tf_op jit(solution)/shard_map/ppermute | solution.py:25
  98.5 8.4 %collective-permute-start.35 = (bf16[1024,256]{1,0:T(8,128)(2,1)S(1)}, bf16[1024,256]{1,0:T(8,128)(2,1)S(1)}, u32[]{:S(2)}, u32[]{:S(2)}) collective-permute-start(bf16[1024,256]{1,0:T(8,128)(2,1)S(1)} %shard_map.113.own), channel_id=1, source_target_pairs={{0,1},{1,2},{2,3},{3,0},{128,131},{129,128},{130,129},{131,130},{4... | collective-permute-start | bytes 1572872 | tf_op jit(solution)/shard_map/ppermute | solution.py:40
  100.8 8.9 %collective-permute-start.34 = (bf16[512,256]{1,0:T(8,128)(2,1)S(1)}, bf16[512,256]{1,0:T(8,128)(2,1)S(1)}, u32[]{:S(2)}, u32[]{:S(2)}) collective-permute-start(bf16[512,256]{1,0:T(8,128)(2,1)S(1)} %slice.24), channel_id=1, source_target_pairs={{0,1},{1,2},{2,3},{3,0},{128,131},{129,128},{130,129},{131,130},{4... | collective-permute-start | bytes 786440 | tf_op jit(solution)/shard_map/ppermute | solution.py:40
  101.3 11.9 %collective-permute-start.33 = (bf16[1024,256]{1,0:T(8,128)(2,1)S(1)}, bf16[1024,256]{1,0:T(8,128)(2,1)S(1)}, u32[]{:S(2)}, u32[]{:S(2)}) collective-permute-start(bf16[1024,256]{1,0:T(8,128)(2,1)S(1)} %collective-permute-done.28.side), channel_id=1, source_target_pairs={{0,128},{128,0},{1,129},{129,1},{2,130},{130,2},{3,131},{131,3},{4... | collective-permute-start | bytes 1572872 | tf_op jit(solution)/shard_map/ppermute | solution.py:25
  112.0 5.6 %collective-permute-start.37 = (bf16[512,256]{1,0:T(8,128)(2,1)S(1)}, bf16[512,256]{1,0:T(8,128)(2,1)S(1)}, u32[]{:S(2)}, u32[]{:S(2)}) collective-permute-start(bf16[512,256]{1,0:T(8,128)(2,1)S(1)} %slice.28), channel_id=1, source_target_pairs={{0,1},{1,2},{2,3},{3,0},{128,131},{129,128},{130,129},{131,130},{4... | collective-permute-start | bytes 786440 | tf_op jit(solution)/shard_map/ppermute | solution.py:40
  113.0 6.6 %collective-permute-start.38 = (bf16[1024,256]{1,0:T(8,128)(2,1)S(1)}, bf16[1024,256]{1,0:T(8,128)(2,1)S(1)}, u32[]{:S(2)}, u32[]{:S(2)}) collective-permute-start(bf16[1024,256]{1,0:T(8,128)(2,1)S(1)} %collective-permute-done.35.side), channel_id=1, source_target_pairs={{0,128},{128,0},{1,129},{129,1},{2,130},{130,2},{3,131},{131,3},{4... | collective-permute-start | bytes 1572872 | tf_op jit(solution)/shard_map/ppermute | solution.py:25
  123.3 14.0 %all-to-all-start = ((f32[32,8,128]{2,1,0:T(8,128)}), f32[32,8,128]{2,1,0:T(8,128)S(1)}, u32[]{:S(2)}, u32[]{:S(2)}) async-start(f32[32,8,128]{2,1,0:T(8,128)} %add.17), calls=%async_computation | async-start | bytes 262144 | tf_op jit(solution)/shard_map/all_to_all | solution.py:505
  (26 other events, 262.3 us)
